TPU v7x, 256 devices: a whole 4x4x8 slice. The times are simulated.
256 devices in a mesh: gx: 4 (over y), gy: 8 (over z), swath: 8 (over x, core).
Axes of the slice: x: 4, y: 4, z: 8, core: 2. Of those that a mesh axis runs over, the one named last changes fastest.
Arguments:
- direction: bfloat16 [120, 10, 128, 512], P(None, None, ('gy', 'swath'), 'gx'), may hold values from -6 to 6
- courant_x: float32 [10, 128, 512], P(None, ('gy', 'swath'), 'gx'), may hold values from -0.5 to 0.5
- courant_y: float32 [10, 128, 512], P(None, ('gy', 'swath'), 'gx'), may hold values from -0.5 to 0.5
- kernel: float32 [10, 128, 512], P(None, ('gy', 'swath'), 'gx'), may hold values from 0.1 to 1.5
- mechanism: int32 [128, 512], P(('gy', 'swath'), 'gx'), may hold values from 0 to 3
- propagator: bfloat16 [4, 120, 120], replicated, may hold values from -0.5 to 0.5
- footprint_pixel: int32 [128, 512], P(('gy', 'swath'), 'gx'), may hold values from 0 to 63
- footprint_weight: float32 [128, 512], P(('gy', 'swath'), 'gx'), may hold values from 0.1 to 1
- footprint_owner: int32 [512, 1], P(('gx', 'gy', 'swath')), may hold values from 0 to 7; in each aligned block of 2 rows (0 to 1, 2 to 3, ...) at most 2 rows name the same one
- precision: float32 [16384], P(('gx', 'gy', 'swath')), may hold values from 0.3 to 3
Outputs:
- product: bfloat16 [120, 10, 128, 512], P(None, None, ('gy', 'swath'), 'gx')
- departures: float32 [16384], P(('gx', 'gy', 'swath'))
Inputs may be any that keep to these rules, and one draw needn't show every extreme that they name: `footprint_owner`: among the 2 rows of one device's blocks, no swath index is named more than 2 times.
All inputs are finite; a program needn't handle non-finite values.
Results may differ from a plain program's by a relative error of at most 0.0053.
Values may be sent and summed in bfloat16 or wider, within the bound.
No kernel may reach another device: no remote copies, remote signals or barrier semaphores. Data moves between devices by JAX's collectives and lax.ppermute only.
A program may use at most 128 MiB of HBM per device.

v0:
```python
import functools

import jax
import jax.numpy as jnp
from jax import lax
from jax.experimental import pallas as pl
from jax.experimental.pallas import tpu as pltpu
from jax.sharding import PartitionSpec as P

KD = 0.2
ALL = ("gx", "gy", "swath")
LANES = 128
NM = 4
NK = NM * NM
BF = jnp.bfloat16
F32 = jnp.float32
VMEM = pl.BlockSpec(memory_space=pltpu.VMEM)
SMEM = pl.BlockSpec(memory_space=pltpu.SMEM)


def iota(shape, dim):
    return lax.broadcasted_iota(jnp.int32, shape, dim)


def lane_roll(v, shift):
    return pltpu.roll(v, shift % v.shape[-1], v.ndim - 1)


def split(v):
    high = v.astype(BF)
    return high, (v - high.astype(F32)).astype(BF)


class Sizes:
    def __init__(self, species, levels):
        self.species = species
        self.levels = levels
        self.rows = 2 * levels
        self.base = 8 * levels
        self.st = self.base + 8
        self.st16 = -(-self.st // 16) * 16
        self.o_st = self.rows * NK
        self.o_hg = self.o_st + 2 * self.st16
        self.o_hs = self.o_hg + NK
        self.msg = self.o_hs + 2 * 16
        self.edge = NK + 8


def project_kernel(
    z, owner_ref, dir_ref, prop_ref, cx_ref, cy_ref, kern_ref, mech_ref, pix_ref, wgt_ref,
    g_ref, msg_ref, edge_ref, st_ref, d_ref, wide,
):
    species = z.species
    wide[...] = dir_ref[...].astype(F32)
    k_of = iota((NK, species), 0)
    heads = jnp.zeros((NK, species), F32)
    for m in range(NM):
        row = prop_ref[m][0:1, :].astype(F32)
        heads = heads + jnp.where(k_of % NM == m, row, 0.0)
    total = heads + jnp.where(iota((NK, species), 1) == 0, 1.0, 0.0)
    lhs = heads.astype(BF)
    for m in range(NM):
        matrix = prop_ref[m]
        term = jnp.dot(lhs, matrix, preferred_element_type=F32)
        total = total + jnp.where(k_of // NM == m, term + matrix[0:1, :].astype(F32), 0.0)
    high, low = split(total)
    both = jnp.concatenate([high, low], axis=0)
    d_ref[...] = jnp.concatenate([high, high, low], axis=0)
    cells = jnp.concatenate(
        [wide[pl.ds(r, species, stride=z.rows), :].astype(BF) for r in range(z.rows)], axis=1
    )
    g32 = jnp.dot(both, cells, preferred_element_type=F32)
    g = g32[:NK] + g32[NK:]
    lane = iota((NK, LANES), 1)
    edge = jnp.zeros((NK, LANES), F32)
    for r in range(z.rows):
        part = g[:, r * LANES : (r + 1) * LANES]
        g_ref[r * NK : (r + 1) * NK, :] = part
        msg_ref[r * NK : (r + 1) * NK, :] = part.astype(BF)
        edge = jnp.where(lane // 4 == r, lane_roll(part, 4 * r + 2), edge)
    edge_ref[0:NK, :] = edge
    lane = iota((8, LANES), 1)
    side = jnp.zeros((8, LANES), F32)
    blank = jnp.zeros((2, LANES), F32)
    own = jnp.where(iota((2, LANES), 0) == 0, owner_ref[0], owner_ref[1])
    for l in range(z.levels + 1):
        if l < z.levels:
            parts = [cx_ref[l], cy_ref[l], kern_ref[l], blank]
        else:
            parts = [
                (mech_ref[...] + 1).astype(F32),
                pix_ref[...].astype(F32),
                wgt_ref[...],
                own.astype(F32),
            ]
        block = jnp.concatenate(parts, axis=0)
        st_ref[8 * l : 8 * l + 8, :] = block
        side = jnp.where(lane // 4 == l, lane_roll(block, 4 * l + 2), side)
    st_ref[z.st :, :] = jnp.zeros((z.st16 - z.st, LANES), F32)
    edge_ref[NK:, :] = side
    high, low = split(st_ref[...])
    msg_ref[z.o_st : z.o_st + z.st16, :] = high
    msg_ref[z.o_st + z.st16 : z.o_st + 2 * z.st16, :] = low
    msg_ref[z.o_hg :, :] = jnp.zeros((z.msg - z.o_hg, LANES), BF)


def edges_kernel(z, pos_ref, x0_ref, x1_ref, main_ref, msg_ref, side_ref, part, sem):
    gx = pos_ref[0]
    even = gx % 2 == 0
    x0 = x0_ref[...]
    x1 = x1_ref[...]
    right = jnp.where(even, x0, x1)
    left = jnp.where(even, x1, x0)
    right = jnp.where(gx < pos_ref[1] - 1, right, 0.0)
    left = jnp.where(gx > 0, left, 0.0)
    side = jnp.where(iota(x0.shape, 1) % 4 < 2, left, right)
    side_ref[...] = side
    part[0:NK, :] = side[0:NK].astype(BF)
    high, low = split(jnp.concatenate([side[NK:], jnp.zeros((8, LANES), F32)], axis=0))
    part[NK : NK + 16, :] = high
    part[NK + 16 :, :] = low
    copy = pltpu.make_async_copy(part, msg_ref.at[pl.ds(z.o_hg, z.msg - z.o_hg), :], sem)
    copy.start()
    copy.wait()


def columns_kernel(
    z, pos_ref, g_ref, st_ref, side_ref, a_ref, b_ref, prec_ref,
    part_ref, ext_ref, gx3, hg3,
):
    t = pos_ref[2]
    swath = pos_ref[3]
    odd = t % 2 == 1
    n = z.o_st
    for slot in range(3):
        if slot == 1:
            gx3[n : 2 * n, :] = g_ref[...]
            hg3[NK : 2 * NK, :] = side_ref[0:NK, :]
            stat = st_ref[...]
            side = side_ref[NK:, :]
        else:
            first, second = (a_ref, b_ref) if slot == 0 else (b_ref, a_ref)
            valid = t > 0 if slot == 0 else t < pos_ref[4] - 1

            def pick(lo, hi, first=first, second=second, valid=valid):
                chosen = jnp.where(odd, first[lo:hi, :].astype(F32), second[lo:hi, :].astype(F32))
                return jnp.where(valid, chosen, 0.0)

            gx3[slot * n : (slot + 1) * n, :] = pick(0, n)
            hg3[slot * NK : (slot + 1) * NK, :] = pick(z.o_hg, z.o_hs)
            stat = pick(z.o_st, z.o_st + z.st16) + pick(z.o_st + z.st16, z.o_hg)
            side = (pick(z.o_hs, z.o_hs + 16) + pick(z.o_hs + 16, z.msg))[0:8]
        for l in range(z.levels + 1):
            ext_ref[slot, l, :, 0:LANES] = stat[8 * l : 8 * l + 8]
            ext_ref[slot, l, :, LANES:] = lane_roll(side, LANES - (4 * l + 2))
    W = 2 * LANES
    k_of = iota((NK, W), 0) // NM
    m_of = iota((8, LANES), 0)
    place = ((0, 1), (1, 0), (1, 1), (2, 0))
    masks = [
        ext_ref[s, z.levels, y : y + 1, :] == (k_of + 1).astype(F32) for s, y in place
    ]
    final = [
        ext_ref[1, z.levels, y : y + 1, 0:LANES] == (m_of + 1).astype(F32) for y in range(2)
    ]

    def level(l, sums):
        def field(s, y):
            r = 2 * l + y
            own = gx3[pl.ds(pl.multiple_of((s * z.rows + r) * NK, NK), NK), :]
            side = pltpu.roll(hg3[s * NK : (s + 1) * NK, :], LANES - 2 - 4 * r, 1)
            return jnp.concatenate([own, side], axis=1)

        stats = [ext_ref[s, l] for s in range(3)]

        def winds(s, y):
            return 0.5 * stats[s][y : y + 1, :], 0.5 * stats[s][2 + y : 3 + y, :]

        fields = [field(s, y) for s in range(3) for y in range(2)]
        firsts = []
        for i, (s, y) in enumerate(place):
            cx, cy = winds(s, y)
            mid = fields[i + 1]
            out = (
                (1.0 - 4.0 * KD) * mid
                + (KD - cx) * pltpu.roll(mid, W - 1, 1)
                + (KD + cx) * pltpu.roll(mid, 1, 1)
                + (KD - cy) * fields[i + 2]
                + (KD + cy) * fields[i]
            )
            out = jnp.where(masks[i], out, 0.0)
            half = out[0:8] + out[8:16]
            firsts.append(half + pltpu.roll(half, 4, 0))
        new = []
        for y in range(2):
            cx, cy = winds(1, y)
            cx, cy = cx[:, 0:LANES], cy[:, 0:LANES]
            mid = firsts[y + 1]
            out = (
                (1.0 - 4.0 * KD) * mid[:, 0:LANES]
                + (KD - cx) * pltpu.roll(mid, W - 1, 1)[:, 0:LANES]
                + (KD + cx) * pltpu.roll(mid, 1, 1)[:, 0:LANES]
                + (KD - cy) * firsts[y + 2][:, 0:LANES]
                + (KD + cy) * firsts[y][:, 0:LANES]
            )
            kern = stats[1][4 + y : 5 + y, 0:LANES]
            new.append(sums[y] + kern * out)
        return tuple(new)

    zero = jnp.zeros((8, LANES), F32)
    sums = lax.fori_loop(0, z.levels, level, (zero, zero))
    pixels = prec_ref.shape[1]
    sub = iota((pixels, LANES), 0)
    lane = iota((pixels, LANES), 1)
    wide8 = iota((8, LANES), 0)
    lane8 = iota((8, LANES), 1)
    total = jnp.zeros((8, LANES), F32)
    base = z.base
    for y in range(2):
        column = jnp.sum(jnp.where(final[y], sums[y], 0.0), axis=0, keepdims=True)
        column = column * st_ref[base + 4 + y : base + 5 + y, :]
        pix = st_ref[base + 2 + y : base + 3 + y, :]
        hit = jnp.where(pix == sub.astype(F32), column, 0.0)
        tall = jnp.sum(hit, axis=1, keepdims=True)
        row = jnp.sum(jnp.where(sub == lane, tall, 0.0), axis=0, keepdims=True)
        owner = st_ref[base + 6 + y : base + 7 + y, :]
        total = total + jnp.where(owner == wide8.astype(F32), row, 0.0)
    prec = jnp.concatenate([jnp.zeros((1, LANES - pixels), F32), prec_ref[...]], axis=1)
    part_ref[...] = jnp.where(
        lane8 < pixels, total, jnp.where(wide8 == swath, prec, 0.0)
    )


def pixels_kernel(z, pos_ref, p0_ref, p1_ref, p2_ref, p3_ref, ext_ref, dep_ref, back_ref):
    total = (p0_ref[...] + p1_ref[...]) + (p2_ref[...] + p3_ref[...])
    pixels = dep_ref.shape[1]
    dep = total * pltpu.roll(total, LANES - pixels, 1)
    swath = pos_ref[3]
    sub = iota((8, LANES), 0)
    dep_ref[...] = jnp.sum(jnp.where(sub == swath, dep, 0.0), axis=0, keepdims=True)[:, 0:pixels]

    def stack(f):
        out = jnp.zeros((8, LANES), F32)
        for s in range(3):
            for y in range(2):
                row = ext_ref[s, z.levels, 2 * f + y : 2 * f + y + 1, 0:LANES]
                out = jnp.where(sub == 2 * s + y, row, out)
        return out

    owner = stack(3)
    table = jnp.zeros((8, LANES), F32)
    for o in range(8):
        table = jnp.where(owner == float(o), dep[o : o + 1, :], table)
    index = stack(1).astype(jnp.int32)
    found = jnp.take_along_axis(table, index, axis=1)
    known = (sub >= 2) & (sub < 4)
    known = known | ((sub < 2) & (swath > 0)) | ((sub >= 4) & (swath < pos_ref[5] - 1))
    back_ref[...] = jnp.where(known, stack(2) * found, 0.0)


def sides_kernel(pos_ref, own_ref, x0_ref, x1_ref, wide_ref):
    gx = pos_ref[0]
    even = gx % 2 == 0
    x0 = x0_ref[...]
    x1 = x1_ref[...]
    right = jnp.where(even, x0, x1)
    left = jnp.where(even, x1, x0)
    right = jnp.where(gx < pos_ref[1] - 1, right, 0.0)
    left = jnp.where(gx > 0, left, 0.0)
    lane = iota(x0.shape, 1)
    wide_ref[:, 0:LANES] = own_ref[...]
    wide_ref[:, LANES:] = jnp.where(lane < 2, right, jnp.where(lane >= LANES - 2, left, 0.0))


def product_kernel(z, pos_ref, back_ref, other_ref, ext_ref, d_ref, out_ref, v3, tall):
    t = pos_ref[2]
    swath = pos_ref[3]
    W = 2 * LANES
    sub = iota((8, W), 0)
    other = other_ref[...]
    back = back_ref[...]
    upper = pltpu.roll(other, 6, 0)
    lower = pltpu.roll(other, 2, 0)
    back = jnp.where((sub < 2) & (swath == 0), jnp.where(t > 0, upper, 0.0), back)
    back = jnp.where(
        (sub >= 4) & (swath == pos_ref[5] - 1), jnp.where(t < pos_ref[4] - 1, lower, 0.0), back
    )
    place = [(s, y) for s in range(3) for y in range(2)]
    k_of = iota((NK, W), 0) // NM
    m_of = iota((8, W), 0) % NM
    drive = []
    for i, (s, y) in enumerate(place):
        mech = ext_ref[s, z.levels, y : y + 1, :]
        drive.append(jnp.where(mech == (m_of + 1).astype(F32), back[i : i + 1, :], 0.0))
    masks = [
        ext_ref[s, z.levels, y : y + 1, :] == (k_of + 1).astype(F32) for s, y in place[1:5]
    ]

    def unadvect(mid, cx, up, cy_up, down, cy_down):
        return (
            (1.0 - 4.0 * KD) * mid
            + pltpu.roll((KD - cx) * mid, 1, 1)
            + pltpu.roll((KD + cx) * mid, W - 1, 1)
            + (KD - cy_up) * up
            + (KD + cy_down) * down
        )

    def level(l, carry):
        stats = [ext_ref[s, l] for s in range(3)]
        cx = [0.5 * stats[s][y : y + 1] for s, y in place]
        cy = [0.5 * stats[s][2 + y : 3 + y] for s, y in place]
        kern = [stats[s][4 + y : 5 + y] for s, y in place]
        w = [kern[i] * drive[i] for i in range(6)]
        u = []
        for i in range(1, 5):
            mid = unadvect(w[i], cx[i], w[i - 1], cy[i - 1], w[i + 1], cy[i + 1])
            twice = jnp.concatenate([mid, mid], axis=0)
            u.append(jnp.where(masks[i - 1], twice, 0.0))
        for y in range(2):
            i = 2 + y
            v = unadvect(u[i - 1], cx[i], u[i - 2], cy[i - 1], u[i], cy[i + 1])[:, 0:LANES]
            high, low = split(v)
            at = pl.ds(pl.multiple_of((2 * l + y) * LANES, LANES), LANES)
            v3[0:NK, at] = high
            v3[NK : 2 * NK, at] = low
            v3[2 * NK :, at] = high
        return carry

    lax.fori_loop(0, z.levels, level, 0)
    d = d_ref[...]
    for r in range(0, z.rows, 2):
        both = lax.dot_general(
            d, v3[:, r * LANES : (r + 2) * LANES], (((0,), (0,)), ((), ())),
            preferred_element_type=F32,
        )
        tall[pl.ds(r, z.species, stride=z.rows), :] = both[:, 0:LANES]
        tall[pl.ds(r + 1, z.species, stride=z.rows), :] = both[:, LANES:]
    out_ref[...] = tall[...].astype(BF)


def shape(*dims, dtype=F32):
    return jax.ShapeDtypeStruct(dims, dtype)


LIMIT = pltpu.CompilerParams(vmem_limit_bytes=32 * 1024 * 1024)


def swaps_of(sizes):
    ngx, ngy, nsw = sizes
    nt = ngy * nsw

    def pairs(f):
        return [(g * nt + t, f(g, t)) for g in range(ngx) for t in range(nt)]

    def other(i, n, parity):
        return (i + 1) % n if i % 2 == parity else (i - 1) % n

    x0 = pairs(lambda g, t: other(g, ngx, 0) * nt + t)
    x1 = pairs(lambda g, t: other(g, ngx, 1) * nt + t)
    ya = pairs(lambda g, t: g * nt + other(t, nt, 0))
    yb = pairs(lambda g, t: g * nt + other(t, nt, 1))
    rim = [
        (g * nt + t, g * nt + (t + (1 if t % nsw else -1)) % nt)
        for g in range(ngx)
        for t in range(nt)
        if t % nsw in (0, nsw - 1)
    ]
    return x0, x1, ya, yb, rim


def per_device(
    sizes,
    direction,
    courant_x,
    courant_y,
    kernel,
    mechanism,
    propagator,
    footprint_pixel,
    footprint_weight,
    footprint_owner,
    precision,
):
    species, levels = direction.shape[:2]
    z = Sizes(species, levels)
    ngx, ngy, nsw = sizes
    x0, x1, ya, yb, rim = swaps_of(sizes)
    gx = lax.axis_index("gx")
    swath = lax.axis_index("swath")
    t = lax.axis_index("gy") * nsw + swath
    pos = jnp.stack([gx, jnp.int32(ngx), t, swath, jnp.int32(ngy * nsw), jnp.int32(nsw)]).astype(
        jnp.int32
    )

    def move(v, perm):
        return lax.ppermute(v, ALL, perm)

    g, msg, edge, st, d = pl.pallas_call(
        functools.partial(project_kernel, z),
        out_shape=(
            shape(z.o_st, LANES),
            shape(z.msg, LANES, dtype=BF),
            shape(z.edge, LANES),
            shape(z.st16, LANES),
            shape(3 * NK, species, dtype=BF),
        ),
        in_specs=[SMEM] + [VMEM] * 8,
        out_specs=(VMEM,) * 5,
        scratch_shapes=[pltpu.VMEM((species * z.rows, LANES), F32)],
        compiler_params=LIMIT,
        name="project",
    )(
        footprint_owner[:, 0],
        direction.reshape(species * z.rows, LANES),
        propagator, courant_x, courant_y, kernel, mechanism, footprint_pixel, footprint_weight,
    )
    e0 = move(edge, x0)
    e1 = move(edge, x1)
    msg, side = pl.pallas_call(
        functools.partial(edges_kernel, z),
        out_shape=(shape(z.msg, LANES, dtype=BF), shape(z.edge, LANES)),
        in_specs=[SMEM, VMEM, VMEM, pl.BlockSpec(memory_space=pl.ANY)],
        out_specs=(pl.BlockSpec(memory_space=pl.ANY), VMEM),
        scratch_shapes=[pltpu.VMEM((z.msg - z.o_hg, LANES), BF), pltpu.SemaphoreType.DMA],
        input_output_aliases={3: 0},
        compiler_params=LIMIT,
        name="edges",
    )(pos, e0, e1, msg)
    m_b = move(msg, yb)
    m_a = move(msg, ya)
    part, ext = pl.pallas_call(
        functools.partial(columns_kernel, z),
        out_shape=(shape(8, LANES), shape(3, levels + 1, 8, 2 * LANES)),
        in_specs=[SMEM] + [VMEM] * 6,
        out_specs=(VMEM, VMEM),
        scratch_shapes=[
            pltpu.VMEM((3 * z.o_st, LANES), F32),
            pltpu.VMEM((3 * NK, LANES), F32),
        ],
        compiler_params=LIMIT,
        name="columns",
    )(pos, g, st, side, m_a, m_b, precision.reshape(1, -1))
    part = part + lax.ppermute(part, "swath", [(i, i ^ 1) for i in range(nsw)])
    turns = [
        lax.ppermute(part, "swath", [(i, (i + 2 * k) % nsw) for i in range(nsw)])
        for k in range(1, 4)
    ]
    dep, back = pl.pallas_call(
        functools.partial(pixels_kernel, z),
        out_shape=(shape(1, precision.shape[0]), shape(8, LANES)),
        in_specs=[SMEM] + [VMEM] * 5,
        out_specs=(VMEM, VMEM),
        compiler_params=LIMIT,
        name="pixels",
    )(pos, part, *turns, ext)
    b0 = move(back, x0)
    b1 = move(back, x1)
    wide = pl.pallas_call(
        sides_kernel,
        out_shape=shape(8, 2 * LANES),
        in_specs=[SMEM] + [VMEM] * 3,
        out_specs=VMEM,
        compiler_params=LIMIT,
        name="sides",
    )(pos, back, b0, b1)
    across = move(wide, rim)
    product = pl.pallas_call(
        functools.partial(product_kernel, z),
        out_shape=shape(species * z.rows, LANES, dtype=BF),
        in_specs=[SMEM] + [VMEM] * 4,
        out_specs=VMEM,
        scratch_shapes=[
            pltpu.VMEM((3 * NK, z.rows * LANES), BF),
            pltpu.VMEM((species * z.rows, LANES), F32),
        ],
        compiler_params=LIMIT,
        name="product",
    )(pos, wide, across, ext, d)
    return product.reshape(direction.shape), dep.reshape(-1)


def solution(mesh):
    placed = (
        P(None, None, ("gy", "swath"), "gx"),
        P(None, ("gy", "swath"), "gx"),
        P(None, ("gy", "swath"), "gx"),
        P(None, ("gy", "swath"), "gx"),
        P(("gy", "swath"), "gx"),
        P(),
        P(("gy", "swath"), "gx"),
        P(("gy", "swath"), "gx"),
        P(("gx", "gy", "swath"), None),
        P(("gx", "gy", "swath")),
    )
    sizes = tuple(mesh.shape[a] for a in ALL)
    return jax.shard_map(
        functools.partial(per_device, sizes),
        mesh=mesh,
        in_specs=placed,
        out_specs=(P(None, None, ("gy", "swath"), "gx"), P(("gx", "gy", "swath"))),
        check_vma=False,
    )
```

profile of v0, /device:TPU:24, one launch (start us, length us, event | category | flops | bytes accessed | tf_op | source)
XLA Modules:
  0.0 51.5 jit_solution(18053410905006660916)
XLA Ops:
  0.6 0.0 copy-start.6
  0.6 0.0 copy-start.7
  0.7 0.0 copy-start.5
  0.7 0.0 copy-start.8
  0.7 0.6 %copy-done.6 = s32[2,128]{1,0:T(2,128)S(1)} copy-done((s32[2,128]{1,0:T(2,128)S(1)}, s32[2,128]{1,0:T(2,128)}, u32[]{:S(2)}) %copy-start.6) | copy-done | bytes 1048
  1.3 0.0 copy-done.7
  1.3 0.0 copy-done.5
  1.3 0.0 copy-done.8
  1.3 0.0 copy-start
  1.3 1.1 %copy-done = bf16[120,10,2,128]{3,2,1,0:T(2,128)(2,1)S(1)} copy-done((bf16[120,10,2,128]{3,2,1,0:T(2,128)(2,1)S(1)}, bf16[120,10,2,128]{3,2,1,0:T(2,128)(2,1)}, u32[]{:S(2)}) %copy-start) | copy-done | bytes 614424
  2.4 0.0 copy-start.1
  2.4 0.9 %copy-done.1 = bf16[4,120,120]{2,1,0:T(8,128)(2,1)S(1)} copy-done((bf16[4,120,120]{2,1,0:T(8,128)(2,1)S(1)}, bf16[4,120,120]{2,1,0:T(8,128)(2,1)}, u32[]{:S(2)}) %copy-start.1) | copy-done | bytes 115224
  3.3 0.0 copy-start.2
  3.3 0.7 %copy-done.2 = f32[10,2,128]{2,1,0:T(2,128)S(1)} copy-done((f32[10,2,128]{2,1,0:T(2,128)S(1)}, f32[10,2,128]{2,1,0:T(2,128)}, u32[]{:S(2)}) %copy-start.2) | copy-done | bytes 10264
  4.0 0.0 copy-start.3
  4.0 0.7 %copy-done.3 = f32[10,2,128]{2,1,0:T(2,128)S(1)} copy-done((f32[10,2,128]{2,1,0:T(2,128)S(1)}, f32[10,2,128]{2,1,0:T(2,128)}, u32[]{:S(2)}) %copy-start.3) | copy-done | bytes 10264
  4.7 0.0 copy-start.4
  4.7 0.7 %copy-done.4 = f32[10,2,128]{2,1,0:T(2,128)S(1)} copy-done((f32[10,2,128]{2,1,0:T(2,128)S(1)}, f32[10,2,128]{2,1,0:T(2,128)}, u32[]{:S(2)}) %copy-start.4) | copy-done | bytes 10264
  5.4 1.0 %project.1 = (f32[320,128]{1,0:T(8,128)S(1)}, bf16[560,128]{1,0:T(8,128)(2,1)S(1)}, f32[24,128]{1,0:T(8,128)S(1)}, f32[96,128]{1,0:T(8,128)S(1)}, bf16[48,120]{1,0:T(8,128)(2,1)S(1)}) custom-call(s32[2]{0:T(128)S(1)} %bitcast.9, bf16[2400,128]{1,0:T(8,128)(2,1)S(1)} %bitcast.8, bf16[4,120,120]{2,1,0:T(8,128)(2,1)S(1)} %copy-done.1, ...), custom_call_target="tpu_custom_call" | custom-call | tf_op jit(solution)/shard_map/project/pallas_call | solution.py:398
  6.4 2.0 %collective-permute-start.1 = (f32[24,128]{1,0:T(8,128)S(1)}, f32[24,128]{1,0:T(8,128)S(1)}, u32[]{:S(2)}, u32[]{:S(2)}) collective-permute-start(f32[24,128]{1,0:T(8,128)S(1)} %get-tuple-element.15), channel_id=1, source_target_pairs={{0,192},{1,193},{2,194},{3,195},{4,196},{5,197},{6,198},{7,199},{8... | collective-permute-start | bytes 36872 | tf_op jit(solution)/shard_map/ppermute | solution.py:396
  8.5 0.0 collective-permute-start
  8.5 0.1 stack.15.pos_ref
  8.5 2.9 %collective-permute-done.1.x1_ref = f32[24,128]{1,0:T(8,128)S(1)} collective-permute-done((f32[24,128]{1,0:T(8,128)S(1)}, f32[24,128]{1,0:T(8,128)S(1)}, u32[]{:S(2)}, u32[]{:S(2)}) %collective-permute-start.1) | collective-permute-done | bytes 12320 | tf_op jit(solution)/shard_map/ppermute | solution.py:396
  11.4 0.7 %collective-permute-done.x0_ref = f32[24,128]{1,0:T(8,128)S(1)} collective-permute-done((f32[24,128]{1,0:T(8,128)S(1)}, f32[24,128]{1,0:T(8,128)S(1)}, u32[]{:S(2)}, u32[]{:S(2)}) %collective-permute-start) | collective-permute-done | bytes 12320 | tf_op jit(solution)/shard_map/ppermute | solution.py:396
  12.1 0.6 %edges.1 = (bf16[560,128]{1,0:T(8,128)(2,1)S(1)}, f32[24,128]{1,0:T(8,128)S(1)}) custom-call(s32[6]{0:T(128)S(1)} %stack.15.pos_ref, f32[24,128]{1,0:T(8,128)S(1)} %collective-permute-done.x0_ref, f32[24,128]{1,0:T(8,128)S(1)} %collective-permute-done.1.x1_ref, bf16[560,128]{1,0:T(8,128)(2,1)S(1)} %get-tuple-element.16.main_ref), custom_call_target="tpu_custom_call", output_to_operand_aliasing={{0}: (3, {})} | custom-call | tf_op jit(solution)/shard_map/edges/pallas_call | solution.py:419
  12.7 5.7 %collective-permute-start.3 = (bf16[560,128]{1,0:T(8,128)(2,1)S(1)}, bf16[560,128]{1,0:T(8,128)(2,1)S(1)}, u32[]{:S(2)}, u32[]{:S(2)}) collective-permute-start(bf16[560,128]{1,0:T(8,128)(2,1)S(1)} %get-tuple-element.18), channel_id=1, source_target_pairs={{0,63},{1,2},{2,1},{3,4},{4,3},{5,6},{6,5},{7,8},{8,7},{9,10},{10,... | collective-permute-start | bytes 430088 | tf_op jit(solution)/shard_map/ppermute | solution.py:396
  18.4 0.0 collective-permute-start.2
  18.4 2.8 %collective-permute-done.3.b_ref = bf16[560,128]{1,0:T(8,128)(2,1)S(1)} collective-permute-done((bf16[560,128]{1,0:T(8,128)(2,1)S(1)}, bf16[560,128]{1,0:T(8,128)(2,1)S(1)}, u32[]{:S(2)}, u32[]{:S(2)}) %collective-permute-start.3) | collective-permute-done | bytes 143392 | tf_op jit(solution)/shard_map/ppermute | solution.py:396
  21.2 0.0 collective-permute-done.2.a_ref
  21.2 0.0 copy-start.9
  21.2 0.7 %copy-done.9 = f32[64]{0:T(128)S(1)} copy-done((f32[64]{0:T(128)S(1)}, f32[64]{0:T(128)}, u32[]{:S(2)}) %copy-start.9) | copy-done | bytes 280
  21.9 3.2 %columns.1 = (f32[8,128]{1,0:T(8,128)S(1)}, f32[3,11,8,256]{3,2,1,0:T(8,128)S(1)}) custom-call(s32[6]{0:T(128)S(1)} %stack.15.pos_ref, f32[320,128]{1,0:T(8,128)S(1)} %get-tuple-element.13.g_ref, f32[96,128]{1,0:T(8,128)S(1)} %get-tuple-element.14.st_ref, f32[24,128]{1,0:T(8,128)S(1)} %get-tuple-element.17.side_ref, ...), custom_call_target="tpu_custom_call" | custom-call | tf_op jit(solution)/shard_map/columns/pallas_call | solution.py:431
  25.1 0.1 collective-permute-start.4
  25.2 1.2 %collective-permute-done.4 = f32[8,128]{1,0:T(8,128)S(1)} collective-permute-done((f32[8,128]{1,0:T(8,128)S(1)}, f32[8,128]{1,0:T(8,128)S(1)}, u32[]{:S(2)}, u32[]{:S(2)}) %collective-permute-start.4) | collective-permute-done | bytes 4128 | tf_op jit(solution)/shard_map/ppermute | solution.py:443
  26.4 0.0 collective-permute-start.7
  26.4 0.0 collective-permute-start.6
  26.4 2.0 %collective-permute-start.5 = (f32[8,128]{1,0:T(8,128)S(1)}, f32[8,128]{1,0:T(8,128)S(1)}, u32[]{:S(2)}, u32[]{:S(2)}) collective-permute-start(f32[8,128]{1,0:T(8,128)S(1)} %add.7.p0_ref), channel_id=1, source_target_pairs={{0,2},{1,3},{2,4},{3,5},{4,6},{5,7},{6,0},{7,1},{8,10},{9,11},{10,... | collective-permute-start | bytes 12296 | tf_op jit(solution)/shard_map/ppermute | solution.py:445
  28.4 1.6 %collective-permute-done.7.p3_ref = f32[8,128]{1,0:T(8,128)S(1)} collective-permute-done((f32[8,128]{1,0:T(8,128)S(1)}, f32[8,128]{1,0:T(8,128)S(1)}, u32[]{:S(2)}, u32[]{:S(2)}) %collective-permute-start.7) | collective-permute-done | bytes 4128 | tf_op jit(solution)/shard_map/ppermute | solution.py:445
  30.0 1.5 %collective-permute-done.6.p2_ref = f32[8,128]{1,0:T(8,128)S(1)} collective-permute-done((f32[8,128]{1,0:T(8,128)S(1)}, f32[8,128]{1,0:T(8,128)S(1)}, u32[]{:S(2)}, u32[]{:S(2)}) %collective-permute-start.6) | collective-permute-done | bytes 4128 | tf_op jit(solution)/shard_map/ppermute | solution.py:445
  31.5 1.2 %collective-permute-done.5.p1_ref = f32[8,128]{1,0:T(8,128)S(1)} collective-permute-done((f32[8,128]{1,0:T(8,128)S(1)}, f32[8,128]{1,0:T(8,128)S(1)}, u32[]{:S(2)}, u32[]{:S(2)}) %collective-permute-start.5) | collective-permute-done | bytes 4128 | tf_op jit(solution)/shard_map/ppermute | solution.py:445
  32.6 1.1 %pixels.1 = (f32[1,64]{1,0:T(1,128)}, f32[8,128]{1,0:T(8,128)S(1)}) custom-call(s32[6]{0:T(128)S(1)} %stack.15.pos_ref, f32[8,128]{1,0:T(8,128)S(1)} %add.7.p0_ref, f32[8,128]{1,0:T(8,128)S(1)} %collective-permute-done.5.p1_ref, f32[8,128]{1,0:T(8,128)S(1)} %collective-permute-done.6.p2_ref, f32[8,128]{1,0:T(8,128)S(1)} %collective-permute-done.7.p3_ref, ...), custom_call_target="tpu_custom_call" | custom-call | tf_op jit(solution)/shard_map/pixels/pallas_call | solution.py:448
  33.8 1.7 %collective-permute-start.9 = (f32[8,128]{1,0:T(8,128)S(1)}, f32[8,128]{1,0:T(8,128)S(1)}, u32[]{:S(2)}, u32[]{:S(2)}) collective-permute-start(f32[8,128]{1,0:T(8,128)S(1)} %get-tuple-element.21.own_ref), channel_id=1, source_target_pairs={{0,192},{1,193},{2,194},{3,195},{4,196},{5,197},{6,198},{7,199},{8... | collective-permute-start | bytes 12296 | tf_op jit(solution)/shard_map/ppermute | solution.py:396
  35.5 0.0 collective-permute-start.8
  35.5 3.1 %collective-permute-done.9.x1_ref = f32[8,128]{1,0:T(8,128)S(1)} collective-permute-done((f32[8,128]{1,0:T(8,128)S(1)}, f32[8,128]{1,0:T(8,128)S(1)}, u32[]{:S(2)}, u32[]{:S(2)}) %collective-permute-start.9) | collective-permute-done | bytes 4128 | tf_op jit(solution)/shard_map/ppermute | solution.py:396
  38.6 0.5 %collective-permute-done.8.x0_ref = f32[8,128]{1,0:T(8,128)S(1)} collective-permute-done((f32[8,128]{1,0:T(8,128)S(1)}, f32[8,128]{1,0:T(8,128)S(1)}, u32[]{:S(2)}, u32[]{:S(2)}) %collective-permute-start.8) | collective-permute-done | bytes 4128 | tf_op jit(solution)/shard_map/ppermute | solution.py:396
  39.1 0.6 %sides.1.back_ref = f32[8,256]{1,0:T(8,128)S(1)} custom-call(s32[6]{0:T(128)S(1)} %stack.15.pos_ref, f32[8,128]{1,0:T(8,128)S(1)} %get-tuple-element.21.own_ref, f32[8,128]{1,0:T(8,128)S(1)} %collective-permute-done.8.x0_ref, f32[8,128]{1,0:T(8,128)S(1)} %collective-permute-done.9.x1_ref), custom_call_target="tpu_custom_call" | custom-call | tf_op jit(solution)/shard_map/sides/pallas_call | solution.py:458
  39.7 3.9 %collective-permute-start.10 = (f32[8,256]{1,0:T(8,128)S(1)}, f32[8,256]{1,0:T(8,128)S(1)}, u32[]{:S(2)}, u32[]{:S(2)}) collective-permute-start(f32[8,256]{1,0:T(8,128)S(1)} %sides.1.back_ref), channel_id=1, source_target_pairs={{0,63},{7,8},{8,7},{15,16},{16,15},{23,24},{24,23},{31,32},{32,31}... | collective-permute-start | bytes 24584 | tf_op jit(solution)/shard_map/ppermute | solution.py:396
  43.6 4.3 %collective-permute-done.10.other_ref = f32[8,256]{1,0:T(8,128)S(1)} collective-permute-done((f32[8,256]{1,0:T(8,128)S(1)}, f32[8,256]{1,0:T(8,128)S(1)}, u32[]{:S(2)}, u32[]{:S(2)}) %collective-permute-start.10) | collective-permute-done | bytes 8224 | tf_op jit(solution)/shard_map/ppermute | solution.py:396
  48.0 3.5 %product.1 = bf16[2400,128]{1,0:T(8,128)(2,1)} custom-call(s32[6]{0:T(128)S(1)} %stack.15.pos_ref, f32[8,256]{1,0:T(8,128)S(1)} %sides.1.back_ref, f32[8,256]{1,0:T(8,128)S(1)} %collective-permute-done.10.other_ref, f32[3,11,8,256]{3,2,1,0:T(8,128)S(1)} %get-tuple-element.20.ext_ref, bf16[48,120]{1,0:T(8,128)(2,1)S(1)} %get-tuple-element.22.d_ref), custom_call_target="tpu_custom_call" | custom-call | tf_op jit(solution)/shard_map/product/pallas_call | solution.py:467
  (1 shorter events, 0.0 us)
Async XLA Ops:
  0.6 0.7 %copy-start.6 = (s32[2,128]{1,0:T(2,128)S(1)}, s32[2,128]{1,0:T(2,128)}, u32[]{:S(2)}) copy-start(s32[2,128]{1,0:T(2,128)} %pix_ref.1) | copy-start | bytes 3076
  0.6 0.7 %copy-start.7 = (f32[2,128]{1,0:T(2,128)S(1)}, f32[2,128]{1,0:T(2,128)}, u32[]{:S(2)}) copy-start(f32[2,128]{1,0:T(2,128)} %wgt_ref.1) | copy-start | bytes 3076
  0.7 0.7 %copy-start.5 = (s32[2,128]{1,0:T(2,128)S(1)}, s32[2,128]{1,0:T(2,128)}, u32[]{:S(2)}) copy-start(s32[2,128]{1,0:T(2,128)} %mech_ref.1) | copy-start | bytes 3076
  0.7 0.7 %copy-start.8 = (s32[2,1]{0,1:T(1,128)S(1)}, s32[2,1]{0,1:T(1,128)}, u32[]{:S(2)}) copy-start(s32[2,1]{0,1:T(1,128)} %param.18) | copy-start | bytes 28
  1.3 1.1 %copy-start = (bf16[120,10,2,128]{3,2,1,0:T(2,128)(2,1)S(1)}, bf16[120,10,2,128]{3,2,1,0:T(2,128)(2,1)}, u32[]{:S(2)}) copy-start(bf16[120,10,2,128]{3,2,1,0:T(2,128)(2,1)} %param.10) | copy-start | bytes 1843204
  2.4 0.9 %copy-start.1 = (bf16[4,120,120]{2,1,0:T(8,128)(2,1)S(1)}, bf16[4,120,120]{2,1,0:T(8,128)(2,1)}, u32[]{:S(2)}) copy-start(bf16[4,120,120]{2,1,0:T(8,128)(2,1)} %prop_ref.1) | copy-start | bytes 345604
  3.3 0.7 %copy-start.2 = (f32[10,2,128]{2,1,0:T(2,128)S(1)}, f32[10,2,128]{2,1,0:T(2,128)}, u32[]{:S(2)}) copy-start(f32[10,2,128]{2,1,0:T(2,128)} %cx_ref.1) | copy-start | bytes 30724
  4.0 0.7 %copy-start.3 = (f32[10,2,128]{2,1,0:T(2,128)S(1)}, f32[10,2,128]{2,1,0:T(2,128)}, u32[]{:S(2)}) copy-start(f32[10,2,128]{2,1,0:T(2,128)} %cy_ref.1) | copy-start | bytes 30724
  4.7 0.7 %copy-start.4 = (f32[10,2,128]{2,1,0:T(2,128)S(1)}, f32[10,2,128]{2,1,0:T(2,128)}, u32[]{:S(2)}) copy-start(f32[10,2,128]{2,1,0:T(2,128)} %kern_ref.1) | copy-start | bytes 30724
  6.4 5.0 %collective-permute-start.1 = (f32[24,128]{1,0:T(8,128)S(1)}, f32[24,128]{1,0:T(8,128)S(1)}, u32[]{:S(2)}, u32[]{:S(2)}) collective-permute-start(f32[24,128]{1,0:T(8,128)S(1)} %get-tuple-element.15), channel_id=1, source_target_pairs={{0,192},{1,193},{2,194},{3,195},{4,196},{5,197},{6,198},{7,199},{8... | collective-permute-start | bytes 36872 | tf_op jit(solution)/shard_map/ppermute | solution.py:396
  8.5 3.7 %collective-permute-start = (f32[24,128]{1,0:T(8,128)S(1)}, f32[24,128]{1,0:T(8,128)S(1)}, u32[]{:S(2)}, u32[]{:S(2)}) collective-permute-start(f32[24,128]{1,0:T(8,128)S(1)} %get-tuple-element.15), channel_id=1, source_target_pairs={{0,64},{1,65},{2,66},{3,67},{4,68},{5,69},{6,70},{7,71},{8,72},{9,... | collective-permute-start | bytes 36872 | tf_op jit(solution)/shard_map/ppermute | solution.py:396
  12.7 8.5 %collective-permute-start.3 = (bf16[560,128]{1,0:T(8,128)(2,1)S(1)}, bf16[560,128]{1,0:T(8,128)(2,1)S(1)}, u32[]{:S(2)}, u32[]{:S(2)}) collective-permute-start(bf16[560,128]{1,0:T(8,128)(2,1)S(1)} %get-tuple-element.18), channel_id=1, source_target_pairs={{0,63},{1,2},{2,1},{3,4},{4,3},{5,6},{6,5},{7,8},{8,7},{9,10},{10,... | collective-permute-start | bytes 430088 | tf_op jit(solution)/shard_map/ppermute | solution.py:396
  18.4 2.8 %collective-permute-start.2 = (bf16[560,128]{1,0:T(8,128)(2,1)S(1)}, bf16[560,128]{1,0:T(8,128)(2,1)S(1)}, u32[]{:S(2)}, u32[]{:S(2)}) collective-permute-start(bf16[560,128]{1,0:T(8,128)(2,1)S(1)} %get-tuple-element.18), channel_id=1, source_target_pairs={{0,1},{1,0},{2,3},{3,2},{4,5},{5,4},{6,7},{7,6},{8,9},{9,8},{10,11... | collective-permute-start | bytes 430088 | tf_op jit(solution)/shard_map/ppermute | solution.py:396
  21.2 0.7 %copy-start.9 = (f32[64]{0:T(128)S(1)}, f32[64]{0:T(128)}, u32[]{:S(2)}) copy-start(f32[64]{0:T(128)} %param.19) | copy-start | bytes 772
  25.1 1.3 %collective-permute-start.4 = (f32[8,128]{1,0:T(8,128)S(1)}, f32[8,128]{1,0:T(8,128)S(1)}, u32[]{:S(2)}, u32[]{:S(2)}) collective-permute-start(f32[8,128]{1,0:T(8,128)S(1)} %get-tuple-element.19), channel_id=1, source_target_pairs={{0,1},{1,0},{2,3},{3,2},{4,5},{5,4},{6,7},{7,6},{8,9},{9,8},{10,11... | collective-permute-start | bytes 12296 | tf_op jit(solution)/shard_map/ppermute | solution.py:443
  26.4 3.6 %collective-permute-start.7 = (f32[8,128]{1,0:T(8,128)S(1)}, f32[8,128]{1,0:T(8,128)S(1)}, u32[]{:S(2)}, u32[]{:S(2)}) collective-permute-start(f32[8,128]{1,0:T(8,128)S(1)} %add.7.p0_ref), channel_id=1, source_target_pairs={{0,6},{1,7},{2,0},{3,1},{4,2},{5,3},{6,4},{7,5},{8,14},{9,15},{10,... | collective-permute-start | bytes 12296 | tf_op jit(solution)/shard_map/ppermute | solution.py:445
  26.4 5.1 %collective-permute-start.6 = (f32[8,128]{1,0:T(8,128)S(1)}, f32[8,128]{1,0:T(8,128)S(1)}, u32[]{:S(2)}, u32[]{:S(2)}) collective-permute-start(f32[8,128]{1,0:T(8,128)S(1)} %add.7.p0_ref), channel_id=1, source_target_pairs={{0,4},{1,5},{2,6},{3,7},{4,0},{5,1},{6,2},{7,3},{8,12},{9,13},{10,... | collective-permute-start | bytes 12296 | tf_op jit(solution)/shard_map/ppermute | solution.py:445
  26.4 6.3 %collective-permute-start.5 = (f32[8,128]{1,0:T(8,128)S(1)}, f32[8,128]{1,0:T(8,128)S(1)}, u32[]{:S(2)}, u32[]{:S(2)}) collective-permute-start(f32[8,128]{1,0:T(8,128)S(1)} %add.7.p0_ref), channel_id=1, source_target_pairs={{0,2},{1,3},{2,4},{3,5},{4,6},{5,7},{6,0},{7,1},{8,10},{9,11},{10,... | collective-permute-start | bytes 12296 | tf_op jit(solution)/shard_map/ppermute | solution.py:445
  33.8 4.8 %collective-permute-start.9 = (f32[8,128]{1,0:T(8,128)S(1)}, f32[8,128]{1,0:T(8,128)S(1)}, u32[]{:S(2)}, u32[]{:S(2)}) collective-permute-start(f32[8,128]{1,0:T(8,128)S(1)} %get-tuple-element.21.own_ref), channel_id=1, source_target_pairs={{0,192},{1,193},{2,194},{3,195},{4,196},{5,197},{6,198},{7,199},{8... | collective-permute-start | bytes 12296 | tf_op jit(solution)/shard_map/ppermute | solution.py:396
  35.5 3.6 %collective-permute-start.8 = (f32[8,128]{1,0:T(8,128)S(1)}, f32[8,128]{1,0:T(8,128)S(1)}, u32[]{:S(2)}, u32[]{:S(2)}) collective-permute-start(f32[8,128]{1,0:T(8,128)S(1)} %get-tuple-element.21.own_ref), channel_id=1, source_target_pairs={{0,64},{1,65},{2,66},{3,67},{4,68},{5,69},{6,70},{7,71},{8,72},{9,... | collective-permute-start | bytes 12296 | tf_op jit(solution)/shard_map/ppermute | solution.py:396
  39.7 8.3 %collective-permute-start.10 = (f32[8,256]{1,0:T(8,128)S(1)}, f32[8,256]{1,0:T(8,128)S(1)}, u32[]{:S(2)}, u32[]{:S(2)}) collective-permute-start(f32[8,256]{1,0:T(8,128)S(1)} %sides.1.back_ref), channel_id=1, source_target_pairs={{0,63},{7,8},{8,7},{15,16},{16,15},{23,24},{24,23},{31,32},{32,31}... | collective-permute-start | bytes 24584 | tf_op jit(solution)/shard_map/ppermute | solution.py:396
where the time goes:
time: 51.8 us; the launch traced here: 51.5 us
  waiting for transfers between devices  19.7 us (38%)
  starting transfers between devices  15.5 us (30%)
  Pallas kernels  9.96 us (19%)
  local copies, waits for them, and re-layouts  5.5 us (11%)
  between operations  0.74 us (1%)
    ppermute x7, waiting for transfers between devices, move(): return lax.ppermute(v, ALL, perm)  14.3 us
    ppermute x7, starting transfers between devices, move(): return lax.ppermute(v, ALL, perm)  13.4 us
    unnamed x20, local copies, waits for them, and re-layouts  5.42 us
    ppermute x3, waiting for transfers between devices, per_device(): lax.ppermute(part, 'swath', [(i, (i + 2 * k) % nsw) for i in range(nsw)])  4.25 us
    pallas_call x1, Pallas kernels, per_device(): pl.pallas_call(functools.partial(product_kernel, z), out_shape=shape(spec...  3.49 us
    pallas_call x1, Pallas kernels, per_device(): pl.pallas_call(functools.partial(columns_kernel, z), out_shape=(shape(8,...  3.23 us
    ppermute x3, starting transfers between devices, per_device(): lax.ppermute(part, 'swath', [(i, (i + 2 * k) % nsw) for i in range(nsw)])  2.02 us
    ppermute x1, waiting for transfers between devices, per_device(): part = part + lax.ppermute(part, 'swath', [(i, i ^ 1) for i in range(nsw)])  1.15 us
  transfers between devices with their start and end apart: 11, of which 10 were waited for; matrix products, arithmetic and copies ran while one was open for 0% of the time, Pallas kernels for 0%

commit v1 on v0

v1 whole, which is shorter than its diff:
```python
import functools

import jax
import jax.numpy as jnp
from jax import lax
from jax.experimental import pallas as pl
from jax.experimental.pallas import tpu as pltpu
from jax.sharding import PartitionSpec as P

KD = 0.2
UNROLL = 10
ALL = ("gx", "gy", "swath")
LANES = 128
NM = 4
NK = NM * NM
BF = jnp.bfloat16
F32 = jnp.float32
VMEM = pl.BlockSpec(memory_space=pltpu.VMEM)
ANY = pl.BlockSpec(memory_space=pl.ANY)
HBM = pl.BlockSpec(memory_space=pltpu.HBM)


def iota(shape, dim):
    return lax.broadcasted_iota(jnp.int32, shape, dim)


def lane_roll(v, shift):
    return pltpu.roll(v, shift % v.shape[-1], v.ndim - 1)


def split(v):
    high = v.astype(BF)
    return high, (v - high.astype(F32)).astype(BF)


class Sizes:
    def __init__(self, sizes, species, levels):
        self.ngx, self.ngy, self.nsw = sizes
        self.nt = self.ngy * self.nsw
        self.species = species
        self.levels = levels
        self.rows = 2 * levels
        self.base = 8 * levels
        self.st = self.base + 8
        self.st16 = -(-(self.st + 1) // 16) * 16
        self.o_st = self.rows * NK
        self.msg = self.o_st + 2 * self.st16
        self.edge = NK + 8
        self.far = NK + 2 * 16

    def place(self):
        gx = lax.axis_index("gx")
        swath = lax.axis_index("swath")
        return gx, swath, lax.axis_index("gy") * self.nsw + swath


def project_kernel(
    z, dir_hbm, prop_hbm, cx_hbm, cy_hbm, kern_hbm, mech_hbm, pix_hbm, wgt_hbm, own_hbm, prec_hbm,
    g_ref, msg_ref, edge_ref, st_ref, d_ref,
    dir_ref, prop_ref, cx_ref, cy_ref, kern_ref, mech_ref, pix_ref, wgt_ref, own_ref, prec_ref,
    wide, sems,
):
    sources = (
        prop_hbm, dir_hbm, cx_hbm, cy_hbm, kern_hbm, mech_hbm, pix_hbm, wgt_hbm, own_hbm, prec_hbm
    )
    targets = (
        prop_ref, dir_ref, cx_ref, cy_ref, kern_ref, mech_ref, pix_ref, wgt_ref, own_ref, prec_ref
    )
    copies = [
        pltpu.make_async_copy(a, b, sems.at[i]) for i, (a, b) in enumerate(zip(sources, targets))
    ]
    for copy in copies:
        copy.start()
    species = z.species
    copies[0].wait()
    k_of = iota((NK, species), 0)
    heads = jnp.zeros((NK, species), F32)
    for m in range(NM):
        row = prop_ref[m][0:1, :].astype(F32)
        heads = heads + jnp.where(k_of % NM == m, row, 0.0)
    total = heads + jnp.where(iota((NK, species), 1) == 0, 1.0, 0.0)
    lhs = heads.astype(BF)
    for m in range(NM):
        matrix = prop_ref[m]
        term = jnp.dot(lhs, matrix, preferred_element_type=F32)
        total = total + jnp.where(k_of // NM == m, term + matrix[0:1, :].astype(F32), 0.0)
    high, low = split(total)
    both = jnp.concatenate([high, low], axis=0)
    d_ref[...] = jnp.concatenate([high, high, low], axis=0)
    copies[1].wait()
    wide[...] = dir_ref[...].astype(F32)
    cells = jnp.concatenate(
        [wide[pl.ds(r, species, stride=z.rows), :].astype(BF) for r in range(z.rows)], axis=1
    )
    g32 = jnp.dot(both, cells, preferred_element_type=F32)
    g = g32[:NK] + g32[NK:]
    lane = iota((NK, LANES), 1)
    edge = jnp.zeros((NK, LANES), F32)
    for r in range(z.rows):
        part = g[:, r * LANES : (r + 1) * LANES]
        g_ref[r * NK : (r + 1) * NK, :] = part
        msg_ref[r * NK : (r + 1) * NK, :] = part.astype(BF)
        edge = jnp.where(lane // 4 == r, lane_roll(part, 4 * r + 2), edge)
    edge_ref[0:NK, :] = edge
    for copy in copies[2:]:
        copy.wait()
    lane = iota((8, LANES), 1)
    side = jnp.zeros((8, LANES), F32)
    blank = jnp.zeros((2, LANES), F32)
    own = jnp.where(iota((2, LANES), 0) == 0, own_ref[:, 0:1], own_ref[:, 1:2])
    for l in range(z.levels + 1):
        if l < z.levels:
            parts = [cx_ref[l], cy_ref[l], kern_ref[l], blank]
        else:
            parts = [
                (mech_ref[...] + 1).astype(F32),
                pix_ref[...].astype(F32),
                wgt_ref[...],
                own.astype(F32),
            ]
        block = jnp.concatenate(parts, axis=0)
        st_ref[8 * l : 8 * l + 8, :] = block
        side = jnp.where(lane // 4 == l, lane_roll(block, 4 * l + 2), side)
    pixels = prec_ref.shape[1]
    last = jnp.concatenate([jnp.zeros((1, LANES - pixels), F32), prec_ref[...]], axis=1)
    st_ref[z.st :, :] = jnp.broadcast_to(last, (z.st16 - z.st, LANES))
    edge_ref[NK:, :] = side
    high, low = split(st_ref[...])
    msg_ref[z.o_st : z.o_st + z.st16, :] = high
    msg_ref[z.o_st + z.st16 : z.o_st + 2 * z.st16, :] = low


def sides_of(z, gx, x0, x1):
    even = gx % 2 == 0
    right = jnp.where(even, x0, x1)
    left = jnp.where(even, x1, x0)
    return jnp.where(gx > 0, left, 0.0), jnp.where(gx < z.ngx - 1, right, 0.0)


def join_kernel(z, own_ref, other_ref, msg_ref, edges_ref, out_ref):
    edges_ref[0 : z.edge, :] = own_ref[...]
    edges_ref[z.edge :, :] = other_ref[...]


def edges_kernel(z, x0_ref, x1_ref, side_ref, far_ref):
    gx, _, _ = z.place()
    left, right = sides_of(z, gx, x0_ref[...], x1_ref[...])
    side = jnp.where(iota(left.shape, 1) % 4 < 2, left, right)
    side_ref[z.edge :, :] = side[0 : z.edge]
    own = side[z.edge :]
    side_ref[0 : z.edge, :] = own
    far_ref[0:NK, :] = own[0:NK].astype(BF)
    high, low = split(jnp.concatenate([own[NK:], jnp.zeros((8, LANES), F32)], axis=0))
    far_ref[NK : NK + 16, :] = high
    far_ref[NK + 16 :, :] = low


def spread(z, side, l):
    return lane_roll(side, LANES - (4 * l + 2))


def columns_kernel(
    z, a_ref, b_ref, g_ref, st_ref, side_ref,
    part_ref, ext_ref, corner_ref, gx3, hg3,
):
    _, swath, t = z.place()
    odd = t % 2 == 1
    has_b = jnp.logical_and(t > 0, t < z.nt - 1)
    n = z.o_st
    zero = jnp.zeros((NK, LANES), F32)
    for slot in range(3):
        if slot == 1:
            gx3[n : 2 * n, :] = g_ref[...]
            hg3[NK : 2 * NK, :] = side_ref[0:NK, :]
            stat = st_ref[...]
            side = side_ref[NK : z.edge, :]
        else:
            is_a = odd if slot == 0 else jnp.logical_not(odd)

            def pick(lo, hi, is_a=is_a):
                beyond = jnp.where(has_b, b_ref[lo:hi, :].astype(F32), 0.0)
                return jnp.where(is_a, a_ref[lo:hi, :].astype(F32), beyond)

            gx3[slot * n : (slot + 1) * n, :] = pick(0, n)
            hg3[slot * NK : (slot + 1) * NK, :] = jnp.where(
                is_a, side_ref[z.edge : z.edge + NK, :], zero
            )
            stat = pick(z.o_st, z.o_st + z.st16) + pick(z.o_st + z.st16, z.msg)
            side = jnp.where(is_a, side_ref[z.edge + NK :, :], zero[0:8])
        for l in range(z.levels + 1):
            ext_ref[slot, l, :, 0:LANES] = stat[8 * l : 8 * l + 8]
            ext_ref[slot, l, :, LANES:] = spread(z, side, l)
    W = 2 * LANES
    k_of = iota((NK, W), 0) // NM
    m_of = iota((8, LANES), 0)
    place = ((0, 1), (1, 0), (1, 1), (2, 0))
    masks = [
        ext_ref[s, z.levels, y : y + 1, :] == (k_of + 1).astype(F32) for s, y in place
    ]
    final = [
        ext_ref[1, z.levels, y : y + 1, 0:LANES] == (m_of + 1).astype(F32) for y in range(2)
    ]

    def level(l, sums):
        def field(s, y):
            r = 2 * l + y
            own = gx3[pl.ds(pl.multiple_of((s * z.rows + r) * NK, NK), NK), :]
            side = pltpu.roll(hg3[s * NK : (s + 1) * NK, :], LANES - 2 - 4 * r, 1)
            return jnp.concatenate([own, side], axis=1)

        stats = [ext_ref[s, l] for s in range(3)]

        def winds(s, y):
            return 0.5 * stats[s][y : y + 1, :], 0.5 * stats[s][2 + y : 3 + y, :]

        fields = [field(s, y) for s in range(3) for y in range(2)]
        firsts = []
        for i, (s, y) in enumerate(place):
            cx, cy = winds(s, y)
            mid = fields[i + 1]
            out = (
                (1.0 - 4.0 * KD) * mid
                + (KD - cx) * pltpu.roll(mid, W - 1, 1)
                + (KD + cx) * pltpu.roll(mid, 1, 1)
                + (KD - cy) * fields[i + 2]
                + (KD + cy) * fields[i]
            )
            out = jnp.where(masks[i], out, 0.0)
            half = out[0:8] + out[8:16]
            firsts.append(half + pltpu.roll(half, 4, 0))
        new = []
        for y in range(2):
            cx, cy = winds(1, y)
            cx, cy = cx[:, 0:LANES], cy[:, 0:LANES]
            mid = firsts[y + 1]
            out = (
                (1.0 - 4.0 * KD) * mid[:, 0:LANES]
                + (KD - cx) * pltpu.roll(mid, W - 1, 1)[:, 0:LANES]
                + (KD + cx) * pltpu.roll(mid, 1, 1)[:, 0:LANES]
                + (KD - cy) * firsts[y + 2][:, 0:LANES]
                + (KD + cy) * firsts[y][:, 0:LANES]
            )
            kern = stats[1][4 + y : 5 + y, 0:LANES]
            new.append(sums[y] + kern * out)
        stat_b = jnp.where(odd, stats[2], stats[0])
        cx_b = 0.5 * jnp.where(odd, stat_b[0:1], stat_b[1:2])
        cx_0 = 0.5 * jnp.where(odd, stats[1][1:2], stats[1][0:1])
        cy_0 = jnp.where(odd, -0.5, 0.5) * jnp.where(odd, stats[1][3:4], stats[1][2:3])
        kern = jnp.where(odd, stats[1][5:6], stats[1][4:5]) * weight_b
        sides = []
        for sign, shift in ((0.5, 1), (-0.5, W - 1)):
            first = (KD + 2 * sign * cx_b) * (KD + cy_0) * near_b
            second = pltpu.roll((KD + cy_0) * near_0, shift, 1) * (KD + 2 * sign * cx_0)
            sides.append(jnp.where(head_0, kern * (first + second), 0.0)[:, 0:LANES])
        left = pltpu.roll(sides[0], 8 * l + 1, 1)
        right = pltpu.roll(sides[1], 8 * l + 3, 1)
        lane = iota((NK, LANES), 1)
        corner = jnp.where(
            lane == 8 * l + 1, left, jnp.where(lane == 8 * l + 2, right, sums[2])
        )
        return tuple(new) + (corner,)

    misc = ext_ref[1, z.levels]
    misc_b = jnp.where(odd, ext_ref[2, z.levels], ext_ref[0, z.levels])
    mech_0 = jnp.where(odd, misc[1:2], misc[0:1])
    mech_b = jnp.where(odd, misc_b[0:1], misc_b[1:2])
    weight_b = jnp.where(odd, misc[5:6], misc[4:5])
    near_0 = (mech_0 == (k_of + 1).astype(F32)).astype(F32)
    near_b = (mech_b == (k_of + 1).astype(F32)).astype(F32)
    head_0 = mech_0 == (iota((NK, W), 0) % NM + 1).astype(F32)
    none = jnp.zeros((8, LANES), F32)
    sums = lax.fori_loop(0, z.levels, level, (none, none, zero), unroll=UNROLL)
    corner_ref[...] = sums[2]
    pixels = LANES // 2
    sub = iota((pixels, LANES), 0)
    lane = iota((pixels, LANES), 1)
    wide8 = iota((8, LANES), 0)
    lane8 = iota((8, LANES), 1)
    total = jnp.zeros((8, LANES), F32)
    base = z.base
    for y in range(2):
        column = jnp.sum(jnp.where(final[y], sums[y], 0.0), axis=0, keepdims=True)
        column = column * st_ref[base + 4 + y : base + 5 + y, :]
        pix = st_ref[base + 2 + y : base + 3 + y, :]
        hit = jnp.where(pix == sub.astype(F32), column, 0.0)
        tall = jnp.sum(hit, axis=1, keepdims=True)
        row = jnp.sum(jnp.where(sub == lane, tall, 0.0), axis=0, keepdims=True)
        owner = st_ref[base + 6 + y : base + 7 + y, :]
        total = total + jnp.where(owner == wide8.astype(F32), row, 0.0)
    prec = st_ref[z.st : z.st + 1, :]
    part_ref[...] = jnp.where(
        lane8 < pixels, total, jnp.where(wide8 == swath, prec, 0.0)
    )


def corner_kernel(z, part_ref, corner_ref, far_ref, st_ref, ext_ref, out_ref, full_ref, block, sem):
    _, _, t = z.place()
    odd = t % 2 == 1
    has_b = jnp.logical_and(t > 0, t < z.nt - 1)
    far = jnp.where(has_b, far_ref[...].astype(F32), 0.0)
    side = (far[NK : NK + 16] + far[NK + 16 :])[0:8]
    for l in range(z.levels + 1):
        block[l] = spread(z, side, l)
    slot = jnp.where(odd, 2, 0)
    copy = pltpu.make_async_copy(block, full_ref.at[slot, :, :, pl.ds(LANES, LANES)], sem)
    copy.start()
    g = far[0:NK]
    g = jnp.where(odd, g, pltpu.roll(g, LANES - 4, 1))
    share = jnp.sum(corner_ref[...] * g, axis=0, keepdims=True)
    lane = iota((1, LANES), 1)
    sub8 = iota((8, LANES), 0)
    lane8 = iota((8, LANES), 1)
    st = st_ref[z.base : z.base + 8, :]
    pixel = jnp.where(odd, st[3:4], st[2:3])
    owner = jnp.where(odd, st[7:8], st[6:7])
    total = part_ref[...]
    for c, column in ((1, 0), (2, LANES - 1)):
        value = jnp.sum(jnp.where(lane % 8 == c, share, 0.0), axis=1, keepdims=True)
        at = slice(column, column + 1)
        hit = (lane8.astype(F32) == pixel[:, at]) & (sub8.astype(F32) == owner[:, at])
        total = total + jnp.where(hit, value, 0.0)
    out_ref[...] = total
    copy.wait()


def product_kernel(z, own_ref, x0_ref, x1_ref, ext_ref, d_ref, out_ref, dep_ref, v3, tall):
    gx, swath, _ = z.place()
    W = 2 * LANES
    pixels = LANES // 2
    left, right = sides_of(z, gx, x0_ref[...], x1_ref[...])

    def weigh(v):
        return v * lane_roll(v, pixels)

    deps = [weigh(v) for v in (own_ref[...], left, right)]
    sub = iota((8, LANES), 0)
    dep_ref[...] = jnp.sum(jnp.where(sub == swath, deps[0][0:8], 0.0), axis=0, keepdims=True)[
        :, 0:pixels
    ]
    outer = ((sub < 2) & (swath == 0)) | ((sub >= 4) & (swath == z.nsw - 1))

    def stack(f):
        out = jnp.zeros((8, W), F32)
        for s in range(3):
            for y in range(2):
                row = ext_ref[s, z.levels, 2 * f + y : 2 * f + y + 1, :]
                out = jnp.where(iota((8, W), 0) == 2 * s + y, row, out)
        return out

    owner = stack(3)
    index = stack(1).astype(jnp.int32)
    weight = stack(2)

    def find(dep, owner, index):
        found = jnp.zeros((8, LANES), F32)
        for o in range(z.nsw):
            row = jnp.where(outer, dep[8 + o : 9 + o, :], dep[o : o + 1, :])
            value = jnp.take_along_axis(row, index, axis=1)
            found = jnp.where(owner == float(o), value, found)
        return found

    lane = iota((8, LANES), 1)
    far = (owner[:, LANES:], index[:, LANES:])
    beside = jnp.where(
        lane < 2, find(deps[2], *far), jnp.where(lane >= LANES - 2, find(deps[1], *far), 0.0)
    )
    near = find(deps[0], owner[:, 0:LANES], index[:, 0:LANES])
    back = weight * jnp.concatenate([near, beside], axis=1)
    place = [(s, y) for s in range(3) for y in range(2)]
    k_of = iota((NK, W), 0) // NM
    m_of = iota((8, W), 0) % NM
    drive = []
    for i, (s, y) in enumerate(place):
        mech = ext_ref[s, z.levels, y : y + 1, :]
        drive.append(jnp.where(mech == (m_of + 1).astype(F32), back[i : i + 1, :], 0.0))
    masks = [
        ext_ref[s, z.levels, y : y + 1, :] == (k_of + 1).astype(F32) for s, y in place[1:5]
    ]

    def unadvect(mid, cx, up, cy_up, down, cy_down):
        return (
            (1.0 - 4.0 * KD) * mid
            + pltpu.roll((KD - cx) * mid, 1, 1)
            + pltpu.roll((KD + cx) * mid, W - 1, 1)
            + (KD - cy_up) * up
            + (KD + cy_down) * down
        )

    def level(l, carry):
        stats = [ext_ref[s, l] for s in range(3)]
        cx = [0.5 * stats[s][y : y + 1] for s, y in place]
        cy = [0.5 * stats[s][2 + y : 3 + y] for s, y in place]
        kern = [stats[s][4 + y : 5 + y] for s, y in place]
        w = [kern[i] * drive[i] for i in range(6)]
        u = []
        for i in range(1, 5):
            mid = unadvect(w[i], cx[i], w[i - 1], cy[i - 1], w[i + 1], cy[i + 1])
            twice = jnp.concatenate([mid, mid], axis=0)
            u.append(jnp.where(masks[i - 1], twice, 0.0))
        for y in range(2):
            i = 2 + y
            v = unadvect(u[i - 1], cx[i], u[i - 2], cy[i - 1], u[i], cy[i + 1])[:, 0:LANES]
            high, low = split(v)
            at = pl.ds(pl.multiple_of((2 * l + y) * LANES, LANES), LANES)
            v3[0:NK, at] = high
            v3[NK : 2 * NK, at] = low
            v3[2 * NK :, at] = high
        return carry

    lax.fori_loop(0, z.levels, level, 0, unroll=UNROLL)
    d = d_ref[...]
    for r in range(0, z.rows, 2):
        both = lax.dot_general(
            d, v3[:, r * LANES : (r + 2) * LANES], (((0,), (0,)), ((), ())),
            preferred_element_type=F32,
        )
        tall[pl.ds(r, z.species, stride=z.rows), :] = both[:, 0:LANES]
        tall[pl.ds(r + 1, z.species, stride=z.rows), :] = both[:, LANES:]
    out_ref[...] = tall[...].astype(BF)


def shape(*dims, dtype=F32):
    return jax.ShapeDtypeStruct(dims, dtype)


LIMIT = pltpu.CompilerParams(vmem_limit_bytes=32 * 1024 * 1024)


def swaps_of(sizes):
    ngx, ngy, nsw = sizes
    nt = ngy * nsw

    def pairs(f):
        return [(g * nt + t, f(g, t)) for g in range(ngx) for t in range(nt)]

    def other(i, parity):
        return i + 1 if i % 2 == parity else i - 1

    def along_x(parity, flip):
        def to(g, t):
            n = other(g, parity)
            return n * nt + (t ^ flip) if 0 <= n < ngx else g * nt + (t ^ 1)

        return pairs(to)

    def along_y(parity):
        def to(g, t):
            n = other(t, parity)
            return g * nt + n if 0 <= n < nt else (g ^ 1) * nt + t

        return pairs(to)

    def along_z(g, t):
        gy, s = divmod(t, nsw)
        chip, core = divmod(s, 2)
        last = nsw // 2 - 1
        up = 1 if chip == 0 else -1
        if chip in (0, last) and 0 <= gy + up < ngy:
            gy, core = gy + up, 1 - core
        elif gy == ngy - 1 and chip < last:
            chip += 1
        elif gy == 0 and chip > 0:
            chip -= 1
        else:
            core = 1 - core
        return g * nt + gy * nsw + 2 * chip + core

    return along_x, along_y, pairs(along_z)


def per_device(
    sizes,
    direction,
    courant_x,
    courant_y,
    kernel,
    mechanism,
    propagator,
    footprint_pixel,
    footprint_weight,
    footprint_owner,
    precision,
):
    species, levels = direction.shape[:2]
    z = Sizes(sizes, species, levels)
    along_x, along_y, along_z = swaps_of(sizes)
    nsw = z.nsw

    def move(v, perm):
        return lax.ppermute(v, ALL, perm)

    cells = (species * z.rows, LANES)
    pixels = precision.shape[0]
    g, msg, edge, st, d = pl.pallas_call(
        functools.partial(project_kernel, z),
        out_shape=(
            shape(z.o_st, LANES),
            shape(z.msg, LANES, dtype=BF),
            shape(z.edge, LANES),
            shape(z.st16, LANES),
            shape(3 * NK, species, dtype=BF),
        ),
        in_specs=[HBM] * 10,
        out_specs=(VMEM,) * 5,
        scratch_shapes=[
            pltpu.VMEM(cells, BF),
            pltpu.VMEM(propagator.shape, BF),
            pltpu.VMEM(courant_x.shape, F32),
            pltpu.VMEM(courant_x.shape, F32),
            pltpu.VMEM(courant_x.shape, F32),
            pltpu.VMEM(mechanism.shape, jnp.int32),
            pltpu.VMEM(mechanism.shape, jnp.int32),
            pltpu.VMEM(mechanism.shape, F32),
            pltpu.VMEM((1, 2), jnp.int32),
            pltpu.VMEM((1, pixels), F32),
            pltpu.VMEM(cells, F32),
            pltpu.SemaphoreType.DMA((10,)),
        ],
        compiler_params=LIMIT,
        name="project",
    )(
        *(
            pltpu.with_memory_space_constraint(v, pltpu.HBM)
            for v in (
                direction.reshape(cells), propagator, courant_x, courant_y, kernel, mechanism,
                footprint_pixel, footprint_weight, footprint_owner.reshape(1, 2),
                precision.reshape(1, -1),
            )
        )
    )
    edges, msg = pl.pallas_call(
        functools.partial(join_kernel, z),
        out_shape=(shape(2 * z.edge, LANES), shape(z.msg, LANES, dtype=BF)),
        in_specs=[VMEM, VMEM, ANY],
        out_specs=(VMEM, ANY),
        input_output_aliases={2: 1},
        compiler_params=LIMIT,
        name="join",
    )(edge, move(edge, along_y(0)), msg)
    e0 = move(edges, along_x(0, 1))
    e1 = move(edges, along_x(1, 1))
    m_b = move(msg, along_y(1))
    m_a = move(msg, along_y(0))
    side, far = pl.pallas_call(
        functools.partial(edges_kernel, z),
        out_shape=(shape(2 * z.edge, LANES), shape(z.far, LANES, dtype=BF)),
        in_specs=[VMEM, VMEM],
        out_specs=(VMEM, VMEM),
        compiler_params=LIMIT,
        cost_estimate=pl.CostEstimate(
            flops=20_000_000_000, bytes_accessed=1024, transcendentals=0
        ),
        name="edges",
    )(e0, e1)
    far_b = move(far, along_y(1))
    part, ext, corner = pl.pallas_call(
        functools.partial(columns_kernel, z),
        out_shape=(
            shape(8, LANES), shape(3, levels + 1, 8, 2 * LANES), shape(NK, LANES)
        ),
        in_specs=[VMEM] * 5,
        out_specs=(VMEM,) * 3,
        scratch_shapes=[
            pltpu.VMEM((3 * z.o_st, LANES), F32),
            pltpu.VMEM((3 * NK, LANES), F32),
        ],
        compiler_params=LIMIT,
        name="columns",
    )(m_a, m_b, g, st, side)
    part, ext = pl.pallas_call(
        functools.partial(corner_kernel, z),
        out_shape=(shape(8, LANES), shape(3, levels + 1, 8, 2 * LANES)),
        in_specs=[VMEM] * 4 + [ANY],
        out_specs=(VMEM, ANY),
        scratch_shapes=[pltpu.VMEM((levels + 1, 8, LANES), F32), pltpu.SemaphoreType.DMA],
        input_output_aliases={4: 1},
        compiler_params=LIMIT,
        name="corner",
    )(part, corner, far_b, st, ext)
    part = part + lax.ppermute(part, "swath", [(i, i ^ 1) for i in range(nsw)])
    turns = [
        lax.ppermute(part, "swath", [(i, (i + 2 * k) % nsw ^ 1) for i in range(nsw)])
        for k in range(1, nsw // 2)
    ]
    for turn in turns:
        part = part + turn
    both = jnp.concatenate([part, move(part, along_z)], axis=0)
    b0 = move(both, along_x(0, 1))
    b1 = move(both, along_x(1, 1))
    product, dep = pl.pallas_call(
        functools.partial(product_kernel, z),
        out_shape=(shape(*cells, dtype=BF), shape(1, pixels)),
        in_specs=[VMEM] * 5,
        out_specs=(VMEM, VMEM),
        scratch_shapes=[
            pltpu.VMEM((3 * NK, z.rows * LANES), BF),
            pltpu.VMEM(cells, F32),
        ],
        compiler_params=LIMIT,
        name="product",
    )(both, b0, b1, ext, d)
    return product.reshape(direction.shape), dep.reshape(-1)


def solution(mesh):
    placed = (
        P(None, None, ("gy", "swath"), "gx"),
        P(None, ("gy", "swath"), "gx"),
        P(None, ("gy", "swath"), "gx"),
        P(None, ("gy", "swath"), "gx"),
        P(("gy", "swath"), "gx"),
        P(),
        P(("gy", "swath"), "gx"),
        P(("gy", "swath"), "gx"),
        P(("gx", "gy", "swath"), None),
        P(("gx", "gy", "swath")),
    )
    sizes = tuple(mesh.shape[a] for a in ALL)
    return jax.shard_map(
        functools.partial(per_device, sizes),
        mesh=mesh,
        in_specs=placed,
        out_specs=(P(None, None, ("gy", "swath"), "gx"), P(("gx", "gy", "swath"))),
        check_vma=False,
    )
```

time: 51.8 us -> 33.9 us (0.65)
  the two profiles are of different devices: /device:TPU:24 before, /device:TPU:97 now
where the time goes in v1:
time: 33.9 us; the launch traced here: 33.6 us
  starting transfers between devices  17.2 us (51%)
  waiting for transfers between devices  9.8 us (29%)
  Pallas kernels  5.86 us (17%)
  between operations  0.69 us (2%)
    ppermute x9, starting transfers between devices, move(): return lax.ppermute(v, ALL, perm)  10.1 us
    ppermute x9, waiting for transfers between devices, move(): return lax.ppermute(v, ALL, perm)  5.25 us
    ppermute x3, starting transfers between devices, per_device(): lax.ppermute(part, 'swath', [(i, (i + 2 * k) % nsw ^ 1) for i in range(ns...  4.55 us
    ppermute x3, waiting for transfers between devices, per_device(): lax.ppermute(part, 'swath', [(i, (i + 2 * k) % nsw ^ 1) for i in range(ns...  3.73 us
    ppermute x1, starting transfers between devices, per_device(): part = part + lax.ppermute(part, 'swath', [(i, i ^ 1) for i in range(nsw)])  2.54 us
    pallas_call x1, Pallas kernels, per_device(): pl.pallas_call(functools.partial(columns_kernel, z), out_shape=(shape(8,...  2.06 us
    pallas_call x1, Pallas kernels, per_device(): pl.pallas_call(functools.partial(project_kernel, z), out_shape=(shape(z.o...  1.76 us
    pallas_call x1, Pallas kernels, per_device(): pl.pallas_call(functools.partial(product_kernel, z), out_shape=(shape(*ce...  1.74 us
  transfers between devices with their start and end apart: 13, of which 6 were waited for; matrix products, arithmetic and copies ran while one was open for 0% of the time, Pallas kernels for 6%

profile of v1, /device:TPU:97, one launch (start us, length us, event | category | flops | bytes accessed | tf_op | source)
XLA Modules:
  0.0 33.6 jit_solution(3066481727432589372)
XLA Ops:
  0.6 1.8 %project.1 = (f32[320,128]{1,0:T(8,128)S(1)}, bf16[512,128]{1,0:T(8,128)(2,1)S(1)}, f32[24,128]{1,0:T(8,128)S(1)}, f32[96,128]{1,0:T(8,128)S(1)}, bf16[48,120]{1,0:T(8,128)(2,1)S(1)}) custom-call(bf16[2400,128]{1,0:T(8,128)(2,1)} %bitcast.5, bf16[4,120,120]{2,1,0:T(8,128)(2,1)} %prop_hbm.1, f32[10,2,128]{2,1,0:T(2,128)} %cx_hbm.1, f32[10,2,128]{2,1,0:T(2,128)} %cy_hbm.1, ...), custom_call_target="tpu_custom_call" | custom-call | tf_op jit(solution)/shard_map/project/pallas_call | solution.py:494
  2.4 0.8 %collective-permute-start = (f32[24,128]{1,0:T(8,128)S(1)}, f32[24,128]{1,0:T(8,128)S(1)}, u32[]{:S(2)}, u32[]{:S(2)}) collective-permute-start(f32[24,128]{1,0:T(8,128)S(1)} %get-tuple-element.18.own_ref), channel_id=1, source_target_pairs={{0,1},{1,0},{2,3},{3,2},{4,5},{5,4},{6,7},{7,6},{8,9},{9,8},{10,11... | collective-permute-start | bytes 36872 | tf_op jit(solution)/shard_map/ppermute | solution.py:490
  3.2 0.8 %collective-permute-done.other_ref = f32[24,128]{1,0:T(8,128)S(1)} collective-permute-done((f32[24,128]{1,0:T(8,128)S(1)}, f32[24,128]{1,0:T(8,128)S(1)}, u32[]{:S(2)}, u32[]{:S(2)}) %collective-permute-start) | collective-permute-done | bytes 12320 | tf_op jit(solution)/shard_map/ppermute | solution.py:490
  4.0 0.3 %collective-permute-start.4 = (f32[48,128]{1,0:T(8,128)S(1)}, f32[48,128]{1,0:T(8,128)S(1)}, u32[]{:S(2)}, u32[]{:S(2)}) collective-permute-start(f32[48,128]{1,0:T(8,128)S(1)} %get-tuple-element.23), channel_id=1, source_target_pairs={{0,1},{1,0},{2,3},{3,2},{4,5},{5,4},{6,7},{7,6},{8,9},{9,8},{10,11... | collective-permute-start | bytes 73736 | tf_op jit(solution)/shard_map/ppermute | solution.py:490
  4.3 2.5 %collective-permute-start.3 = (f32[48,128]{1,0:T(8,128)S(1)}, f32[48,128]{1,0:T(8,128)S(1)}, u32[]{:S(2)}, u32[]{:S(2)}) collective-permute-start(f32[48,128]{1,0:T(8,128)S(1)} %get-tuple-element.23), channel_id=1, source_target_pairs={{0,65},{1,64},{2,67},{3,66},{4,69},{5,68},{6,71},{7,70},{8,73},{9,... | collective-permute-start | bytes 73736 | tf_op jit(solution)/shard_map/ppermute | solution.py:490
  6.9 1.4 %collective-permute-start.2 = (bf16[512,128]{1,0:T(8,128)(2,1)S(1)}, bf16[512,128]{1,0:T(8,128)(2,1)S(1)}, u32[]{:S(2)}, u32[]{:S(2)}) collective-permute-start(bf16[512,128]{1,0:T(8,128)(2,1)S(1)} %get-tuple-element.20), channel_id=1, source_target_pairs={{0,64},{1,2},{2,1},{3,4},{4,3},{5,6},{6,5},{7,8},{8,7},{9,10},{10,... | collective-permute-start | bytes 393224 | tf_op jit(solution)/shard_map/ppermute | solution.py:490
  8.3 1.0 %collective-permute-start.1 = (bf16[512,128]{1,0:T(8,128)(2,1)S(1)}, bf16[512,128]{1,0:T(8,128)(2,1)S(1)}, u32[]{:S(2)}, u32[]{:S(2)}) collective-permute-start(bf16[512,128]{1,0:T(8,128)(2,1)S(1)} %get-tuple-element.20), channel_id=1, source_target_pairs={{0,1},{1,0},{2,3},{3,2},{4,5},{5,4},{6,7},{7,6},{8,9},{9,8},{10,11... | collective-permute-start | bytes 393224 | tf_op jit(solution)/shard_map/ppermute | solution.py:490
  9.3 0.0 collective-permute-done.4.x1_ref
  9.3 0.0 collective-permute-done.3.x0_ref
  9.3 0.7 %collective-permute-start.5 = (bf16[48,128]{1,0:T(8,128)(2,1)S(1)}, bf16[48,128]{1,0:T(8,128)(2,1)S(1)}, u32[]{:S(2)}, u32[]{:S(2)}) collective-permute-start(bf16[48,128]{1,0:T(8,128)(2,1)S(1)} %get-tuple-element.27), channel_id=1, source_target_pairs={{0,64},{1,2},{2,1},{3,4},{4,3},{5,6},{6,5},{7,8},{8,7},{9,10},{10,... | collective-permute-start | bytes 36872 | tf_op jit(solution)/shard_map/ppermute | solution.py:490
  10.0 1.2 %collective-permute-done.2.b_ref = bf16[512,128]{1,0:T(8,128)(2,1)S(1)} collective-permute-done((bf16[512,128]{1,0:T(8,128)(2,1)S(1)}, bf16[512,128]{1,0:T(8,128)(2,1)S(1)}, u32[]{:S(2)}, u32[]{:S(2)}) %collective-permute-start.2) | collective-permute-done | bytes 131104 | tf_op jit(solution)/shard_map/ppermute | solution.py:490
  11.3 0.0 collective-permute-done.1.a_ref
  11.3 2.1 %columns.1 = (f32[8,128]{1,0:T(8,128)S(1)}, f32[3,11,8,256]{3,2,1,0:T(8,128)S(1)}, f32[16,128]{1,0:T(8,128)S(1)}) custom-call(bf16[512,128]{1,0:T(8,128)(2,1)S(1)} %collective-permute-done.1.a_ref, bf16[512,128]{1,0:T(8,128)(2,1)S(1)} %collective-permute-done.2.b_ref, f32[320,128]{1,0:T(8,128)S(1)} %get-tuple-element.21.g_ref, ...), custom_call_target="tpu_custom_call" | custom-call | tf_op jit(solution)/shard_map/columns/pallas_call | solution.py:556
  13.3 0.0 collective-permute-done.5.far_ref
  13.3 0.3 corner.1
  13.6 2.5 %collective-permute-start.6 = (f32[8,128]{1,0:T(8,128)S(1)}, f32[8,128]{1,0:T(8,128)S(1)}, u32[]{:S(2)}, u32[]{:S(2)}) collective-permute-start(f32[8,128]{1,0:T(8,128)S(1)} %get-tuple-element.29), channel_id=1, source_target_pairs={{0,1},{1,0},{2,3},{3,2},{4,5},{5,4},{6,7},{7,6},{8,9},{9,8},{10,11... | collective-permute-start | bytes 12296 | tf_op jit(solution)/shard_map/ppermute | solution.py:580
  16.2 0.8 %collective-permute-done.6 = f32[8,128]{1,0:T(8,128)S(1)} collective-permute-done((f32[8,128]{1,0:T(8,128)S(1)}, f32[8,128]{1,0:T(8,128)S(1)}, u32[]{:S(2)}, u32[]{:S(2)}) %collective-permute-start.6) | collective-permute-done | bytes 4128 | tf_op jit(solution)/shard_map/ppermute | solution.py:580
  17.0 3.7 %collective-permute-start.9 = (f32[8,128]{1,0:T(8,128)S(1)}, f32[8,128]{1,0:T(8,128)S(1)}, u32[]{:S(2)}, u32[]{:S(2)}) collective-permute-start(f32[8,128]{1,0:T(8,128)S(1)} %add.12), channel_id=1, source_target_pairs={{0,7},{1,6},{2,1},{3,0},{4,3},{5,2},{6,5},{7,4},{8,15},{9,14},{10,... | collective-permute-start | bytes 12296 | tf_op jit(solution)/shard_map/ppermute | solution.py:582
  20.7 0.0 collective-permute-start.8
  20.7 0.8 %collective-permute-start.7 = (f32[8,128]{1,0:T(8,128)S(1)}, f32[8,128]{1,0:T(8,128)S(1)}, u32[]{:S(2)}, u32[]{:S(2)}) collective-permute-start(f32[8,128]{1,0:T(8,128)S(1)} %add.12), channel_id=1, source_target_pairs={{0,3},{1,2},{2,5},{3,4},{4,7},{5,6},{6,1},{7,0},{8,11},{9,10},{10,... | collective-permute-start | bytes 12296 | tf_op jit(solution)/shard_map/ppermute | solution.py:582
  21.5 0.0 collective-permute-done.9
  21.5 3.7 %collective-permute-done.8 = f32[8,128]{1,0:T(8,128)S(1)} collective-permute-done((f32[8,128]{1,0:T(8,128)S(1)}, f32[8,128]{1,0:T(8,128)S(1)}, u32[]{:S(2)}, u32[]{:S(2)}) %collective-permute-start.8) | collective-permute-done | bytes 4128 | tf_op jit(solution)/shard_map/ppermute | solution.py:582
  25.3 0.0 collective-permute-done.7
  25.3 1.9 %collective-permute-start.10 = (f32[8,128]{1,0:T(8,128)S(1)}, f32[8,128]{1,0:T(8,128)S(1)}, u32[]{:S(2)}, u32[]{:S(2)}) collective-permute-start(f32[8,128]{1,0:T(8,128)S(1)} %add_add_fusion), channel_id=1, source_target_pairs={{0,9},{1,8},{2,0},{3,1},{4,2},{5,3},{6,4},{7,5},{8,17},{9,16},{10,... | collective-permute-start | bytes 12296 | tf_op jit(solution)/shard_map/ppermute | solution.py:490
  27.2 1.2 %collective-permute-done.10 = f32[8,128]{1,0:T(8,128)S(1)} collective-permute-done((f32[8,128]{1,0:T(8,128)S(1)}, f32[8,128]{1,0:T(8,128)S(1)}, u32[]{:S(2)}, u32[]{:S(2)}) %collective-permute-start.10) | collective-permute-done | bytes 4128 | tf_op jit(solution)/shard_map/ppermute | solution.py:490
  28.4 0.3 %collective-permute-start.12 = (f32[16,128]{1,0:T(8,128)S(1)}, f32[16,128]{1,0:T(8,128)S(1)}, u32[]{:S(2)}, u32[]{:S(2)}) collective-permute-start(f32[16,128]{1,0:T(8,128)S(1)} %pad_maximum_fusion.own_ref), channel_id=1, source_target_pairs={{0,1},{1,0},{2,3},{3,2},{4,5},{5,4},{6,7},{7,6},{8,9},{9,8},{10,11... | collective-permute-start | bytes 24584 | tf_op jit(solution)/shard_map/ppermute | solution.py:490
  28.7 1.1 %collective-permute-start.11 = (f32[16,128]{1,0:T(8,128)S(1)}, f32[16,128]{1,0:T(8,128)S(1)}, u32[]{:S(2)}, u32[]{:S(2)}) collective-permute-start(f32[16,128]{1,0:T(8,128)S(1)} %pad_maximum_fusion.own_ref), channel_id=1, source_target_pairs={{0,65},{1,64},{2,67},{3,66},{4,69},{5,68},{6,71},{7,70},{8,73},{9,... | collective-permute-start | bytes 24584 | tf_op jit(solution)/shard_map/ppermute | solution.py:490
  29.8 0.0 collective-permute-done.12.x1_ref
  29.8 2.0 %collective-permute-done.11.x0_ref = f32[16,128]{1,0:T(8,128)S(1)} collective-permute-done((f32[16,128]{1,0:T(8,128)S(1)}, f32[16,128]{1,0:T(8,128)S(1)}, u32[]{:S(2)}, u32[]{:S(2)}) %collective-permute-start.11) | collective-permute-done | bytes 8224 | tf_op jit(solution)/shard_map/ppermute | solution.py:490
  31.8 1.7 %product.1 = (bf16[2400,128]{1,0:T(8,128)(2,1)}, f32[1,64]{1,0:T(1,128)}) custom-call(f32[16,128]{1,0:T(8,128)S(1)} %pad_maximum_fusion.own_ref, f32[16,128]{1,0:T(8,128)S(1)} %collective-permute-done.11.x0_ref, f32[16,128]{1,0:T(8,128)S(1)} %collective-permute-done.12.x1_ref, f32[3,11,8,256]{3,2,1,0:T(8,128)S(1)} %get-tuple-element.30.ext_ref, ...), custom_call_target="tpu_custom_call" | custom-call | tf_op jit(solution)/shard_map/product/pallas_call | solution.py:590
  (5 shorter events, 0.0 us)
Async XLA Ops:
  2.4 1.6 %collective-permute-start = (f32[24,128]{1,0:T(8,128)S(1)}, f32[24,128]{1,0:T(8,128)S(1)}, u32[]{:S(2)}, u32[]{:S(2)}) collective-permute-start(f32[24,128]{1,0:T(8,128)S(1)} %get-tuple-element.18.own_ref), channel_id=1, source_target_pairs={{0,1},{1,0},{2,3},{3,2},{4,5},{5,4},{6,7},{7,6},{8,9},{9,8},{10,11... | collective-permute-start | bytes 36872 | tf_op jit(solution)/shard_map/ppermute | solution.py:490
  4.0 5.3 %collective-permute-start.4 = (f32[48,128]{1,0:T(8,128)S(1)}, f32[48,128]{1,0:T(8,128)S(1)}, u32[]{:S(2)}, u32[]{:S(2)}) collective-permute-start(f32[48,128]{1,0:T(8,128)S(1)} %get-tuple-element.23), channel_id=1, source_target_pairs={{0,1},{1,0},{2,3},{3,2},{4,5},{5,4},{6,7},{7,6},{8,9},{9,8},{10,11... | collective-permute-start | bytes 73736 | tf_op jit(solution)/shard_map/ppermute | solution.py:490
  4.3 5.0 %collective-permute-start.3 = (f32[48,128]{1,0:T(8,128)S(1)}, f32[48,128]{1,0:T(8,128)S(1)}, u32[]{:S(2)}, u32[]{:S(2)}) collective-permute-start(f32[48,128]{1,0:T(8,128)S(1)} %get-tuple-element.23), channel_id=1, source_target_pairs={{0,65},{1,64},{2,67},{3,66},{4,69},{5,68},{6,71},{7,70},{8,73},{9,... | collective-permute-start | bytes 73736 | tf_op jit(solution)/shard_map/ppermute | solution.py:490
  6.9 4.4 %collective-permute-start.2 = (bf16[512,128]{1,0:T(8,128)(2,1)S(1)}, bf16[512,128]{1,0:T(8,128)(2,1)S(1)}, u32[]{:S(2)}, u32[]{:S(2)}) collective-permute-start(bf16[512,128]{1,0:T(8,128)(2,1)S(1)} %get-tuple-element.20), channel_id=1, source_target_pairs={{0,64},{1,2},{2,1},{3,4},{4,3},{5,6},{6,5},{7,8},{8,7},{9,10},{10,... | collective-permute-start | bytes 393224 | tf_op jit(solution)/shard_map/ppermute | solution.py:490
  8.3 3.0 %collective-permute-start.1 = (bf16[512,128]{1,0:T(8,128)(2,1)S(1)}, bf16[512,128]{1,0:T(8,128)(2,1)S(1)}, u32[]{:S(2)}, u32[]{:S(2)}) collective-permute-start(bf16[512,128]{1,0:T(8,128)(2,1)S(1)} %get-tuple-element.20), channel_id=1, source_target_pairs={{0,1},{1,0},{2,3},{3,2},{4,5},{5,4},{6,7},{7,6},{8,9},{9,8},{10,11... | collective-permute-start | bytes 393224 | tf_op jit(solution)/shard_map/ppermute | solution.py:490
  9.3 4.0 %collective-permute-start.5 = (bf16[48,128]{1,0:T(8,128)(2,1)S(1)}, bf16[48,128]{1,0:T(8,128)(2,1)S(1)}, u32[]{:S(2)}, u32[]{:S(2)}) collective-permute-start(bf16[48,128]{1,0:T(8,128)(2,1)S(1)} %get-tuple-element.27), channel_id=1, source_target_pairs={{0,64},{1,2},{2,1},{3,4},{4,3},{5,6},{6,5},{7,8},{8,7},{9,10},{10,... | collective-permute-start | bytes 36872 | tf_op jit(solution)/shard_map/ppermute | solution.py:490
  13.6 3.4 %collective-permute-start.6 = (f32[8,128]{1,0:T(8,128)S(1)}, f32[8,128]{1,0:T(8,128)S(1)}, u32[]{:S(2)}, u32[]{:S(2)}) collective-permute-start(f32[8,128]{1,0:T(8,128)S(1)} %get-tuple-element.29), channel_id=1, source_target_pairs={{0,1},{1,0},{2,3},{3,2},{4,5},{5,4},{6,7},{7,6},{8,9},{9,8},{10,11... | collective-permute-start | bytes 12296 | tf_op jit(solution)/shard_map/ppermute | solution.py:580
  17.0 4.6 %collective-permute-start.9 = (f32[8,128]{1,0:T(8,128)S(1)}, f32[8,128]{1,0:T(8,128)S(1)}, u32[]{:S(2)}, u32[]{:S(2)}) collective-permute-start(f32[8,128]{1,0:T(8,128)S(1)} %add.12), channel_id=1, source_target_pairs={{0,7},{1,6},{2,1},{3,0},{4,3},{5,2},{6,5},{7,4},{8,15},{9,14},{10,... | collective-permute-start | bytes 12296 | tf_op jit(solution)/shard_map/ppermute | solution.py:582
  20.7 4.5 %collective-permute-start.8 = (f32[8,128]{1,0:T(8,128)S(1)}, f32[8,128]{1,0:T(8,128)S(1)}, u32[]{:S(2)}, u32[]{:S(2)}) collective-permute-start(f32[8,128]{1,0:T(8,128)S(1)} %add.12), channel_id=1, source_target_pairs={{0,5},{1,4},{2,7},{3,6},{4,1},{5,0},{6,3},{7,2},{8,13},{9,12},{10,... | collective-permute-start | bytes 12296 | tf_op jit(solution)/shard_map/ppermute | solution.py:582
  20.7 4.5 %collective-permute-start.7 = (f32[8,128]{1,0:T(8,128)S(1)}, f32[8,128]{1,0:T(8,128)S(1)}, u32[]{:S(2)}, u32[]{:S(2)}) collective-permute-start(f32[8,128]{1,0:T(8,128)S(1)} %add.12), channel_id=1, source_target_pairs={{0,3},{1,2},{2,5},{3,4},{4,7},{5,6},{6,1},{7,0},{8,11},{9,10},{10,... | collective-permute-start | bytes 12296 | tf_op jit(solution)/shard_map/ppermute | solution.py:582
  25.3 3.1 %collective-permute-start.10 = (f32[8,128]{1,0:T(8,128)S(1)}, f32[8,128]{1,0:T(8,128)S(1)}, u32[]{:S(2)}, u32[]{:S(2)}) collective-permute-start(f32[8,128]{1,0:T(8,128)S(1)} %add_add_fusion), channel_id=1, source_target_pairs={{0,9},{1,8},{2,0},{3,1},{4,2},{5,3},{6,4},{7,5},{8,17},{9,16},{10,... | collective-permute-start | bytes 12296 | tf_op jit(solution)/shard_map/ppermute | solution.py:490
  28.4 1.4 %collective-permute-start.12 = (f32[16,128]{1,0:T(8,128)S(1)}, f32[16,128]{1,0:T(8,128)S(1)}, u32[]{:S(2)}, u32[]{:S(2)}) collective-permute-start(f32[16,128]{1,0:T(8,128)S(1)} %pad_maximum_fusion.own_ref), channel_id=1, source_target_pairs={{0,1},{1,0},{2,3},{3,2},{4,5},{5,4},{6,7},{7,6},{8,9},{9,8},{10,11... | collective-permute-start | bytes 24584 | tf_op jit(solution)/shard_map/ppermute | solution.py:490
  28.7 3.1 %collective-permute-start.11 = (f32[16,128]{1,0:T(8,128)S(1)}, f32[16,128]{1,0:T(8,128)S(1)}, u32[]{:S(2)}, u32[]{:S(2)}) collective-permute-start(f32[16,128]{1,0:T(8,128)S(1)} %pad_maximum_fusion.own_ref), channel_id=1, source_target_pairs={{0,65},{1,64},{2,67},{3,66},{4,69},{5,68},{6,71},{7,70},{8,73},{9,... | collective-permute-start | bytes 24584 | tf_op jit(solution)/shard_map/ppermute | solution.py:490

commit v2 on v1

--- a/solution.py
+++ b/solution.py
@@ -9,6 +9,7 @@
 
 KD = 0.2
 UNROLL = 10
+TURNS = (1, 3, 2)
 ALL = ("gx", "gy", "swath")
 LANES = 128
 NM = 4
@@ -137,20 +138,13 @@
     return jnp.where(gx > 0, left, 0.0), jnp.where(gx < z.ngx - 1, right, 0.0)
 
 
-def join_kernel(z, own_ref, other_ref, msg_ref, edges_ref, out_ref):
-    edges_ref[0 : z.edge, :] = own_ref[...]
-    edges_ref[z.edge :, :] = other_ref[...]
-
-
 def edges_kernel(z, x0_ref, x1_ref, side_ref, far_ref):
     gx, _, _ = z.place()
     left, right = sides_of(z, gx, x0_ref[...], x1_ref[...])
     side = jnp.where(iota(left.shape, 1) % 4 < 2, left, right)
-    side_ref[z.edge :, :] = side[0 : z.edge]
-    own = side[z.edge :]
-    side_ref[0 : z.edge, :] = own
-    far_ref[0:NK, :] = own[0:NK].astype(BF)
-    high, low = split(jnp.concatenate([own[NK:], jnp.zeros((8, LANES), F32)], axis=0))
+    side_ref[...] = side
+    far_ref[0:NK, :] = side[0:NK].astype(BF)
+    high, low = split(jnp.concatenate([side[NK:], jnp.zeros((8, LANES), F32)], axis=0))
     far_ref[NK : NK + 16, :] = high
     far_ref[NK + 16 :, :] = low
 
@@ -159,160 +153,197 @@
     return lane_roll(side, LANES - (4 * l + 2))
 
 
-def columns_kernel(
-    z, a_ref, b_ref, g_ref, st_ref, side_ref,
-    part_ref, ext_ref, corner_ref, gx3, hg3,
-):
-    _, swath, t = z.place()
+def edge_lanes(z, l, left, right, old):
+    lane = iota((NK, LANES), 1)
+    left = pltpu.roll(left, 8 * l + 1, 1)
+    right = pltpu.roll(right, 8 * l + 3, 1)
+    return jnp.where(lane == 8 * l + 1, left, jnp.where(lane == 8 * l + 2, right, old))
+
+
+def fold(v):
+    half = v[0:8] + v[8:16]
+    return half + pltpu.roll(half, 4, 0)
+
+
+def row_of(stats, odd, first):
+    return jnp.where(odd, stats[first ^ 1 : (first ^ 1) + 1], stats[first : first + 1])
+
+
+def columns_kernel(z, a_ref, g_ref, st_ref, side_ref, far_ref, sums_ref, ext_ref, corner_ref, ga, ha):
+    _, _, t = z.place()
     odd = t % 2 == 1
-    has_b = jnp.logical_and(t > 0, t < z.nt - 1)
-    n = z.o_st
-    zero = jnp.zeros((NK, LANES), F32)
-    for slot in range(3):
-        if slot == 1:
-            gx3[n : 2 * n, :] = g_ref[...]
-            hg3[NK : 2 * NK, :] = side_ref[0:NK, :]
-            stat = st_ref[...]
-            side = side_ref[NK : z.edge, :]
-        else:
-            is_a = odd if slot == 0 else jnp.logical_not(odd)
-
-            def pick(lo, hi, is_a=is_a):
-                beyond = jnp.where(has_b, b_ref[lo:hi, :].astype(F32), 0.0)
-                return jnp.where(is_a, a_ref[lo:hi, :].astype(F32), beyond)
-
-            gx3[slot * n : (slot + 1) * n, :] = pick(0, n)
-            hg3[slot * NK : (slot + 1) * NK, :] = jnp.where(
-                is_a, side_ref[z.edge : z.edge + NK, :], zero
-            )
-            stat = pick(z.o_st, z.o_st + z.st16) + pick(z.o_st + z.st16, z.msg)
-            side = jnp.where(is_a, side_ref[z.edge + NK :, :], zero[0:8])
-        for l in range(z.levels + 1):
-            ext_ref[slot, l, :, 0:LANES] = stat[8 * l : 8 * l + 8]
-            ext_ref[slot, l, :, LANES:] = spread(z, side, l)
+    even = jnp.where(odd, 0, 1)
+    sg = jnp.where(odd, -0.5, 0.5)
     W = 2 * LANES
-    k_of = iota((NK, W), 0) // NM
-    m_of = iota((8, LANES), 0)
-    place = ((0, 1), (1, 0), (1, 1), (2, 0))
-    masks = [
-        ext_ref[s, z.levels, y : y + 1, :] == (k_of + 1).astype(F32) for s, y in place
-    ]
-    final = [
-        ext_ref[1, z.levels, y : y + 1, 0:LANES] == (m_of + 1).astype(F32) for y in range(2)
-    ]
-
-    def level(l, sums):
-        def field(s, y):
+    ga[...] = a_ref[0 : z.o_st, :].astype(F32)
+    ha[...] = far_ref[0:NK, :]
+    stat_a = a_ref[z.o_st : z.o_st + z.st16, :].astype(F32) + a_ref[
+        z.o_st + z.st16 : z.msg, :
+    ].astype(F32)
+    for l in range(z.levels + 1):
+        ext_ref[0, l, :, 0:LANES] = st_ref[8 * l : 8 * l + 8, :]
+        ext_ref[0, l, :, LANES:] = spread(z, side_ref[NK:, :], l)
+        ext_ref[1, l, :, 0:LANES] = stat_a[8 * l : 8 * l + 8]
+        ext_ref[1, l, :, LANES:] = spread(z, far_ref[NK:, :], l)
+    k_of = iota((NK, W), 0)
+    misc = ext_ref[0, z.levels]
+    misc_a = ext_ref[1, z.levels]
+
+    def sort(mech):
+        return mech == (k_of // NM + 1).astype(F32)
+
+    mech_0 = row_of(misc, odd, 0)
+    mask_0, mask_1, mask_a = sort(mech_0), sort(row_of(misc, odd, 1)), sort(row_of(misc_a, odd, 0))
+    head_0 = mech_0 == (k_of % NM + 1).astype(F32)
+    weight_0 = row_of(misc, odd, 4)
+
+    def level(l, carry):
+        def field(ref, side, y):
             r = 2 * l + y
-            own = gx3[pl.ds(pl.multiple_of((s * z.rows + r) * NK, NK), NK), :]
-            side = pltpu.roll(hg3[s * NK : (s + 1) * NK, :], LANES - 2 - 4 * r, 1)
-            return jnp.concatenate([own, side], axis=1)
-
-        stats = [ext_ref[s, l] for s in range(3)]
-
-        def winds(s, y):
-            return 0.5 * stats[s][y : y + 1, :], 0.5 * stats[s][2 + y : 3 + y, :]
-
-        fields = [field(s, y) for s in range(3) for y in range(2)]
-        firsts = []
-        for i, (s, y) in enumerate(place):
-            cx, cy = winds(s, y)
-            mid = fields[i + 1]
-            out = (
+            own = ref[pl.ds(pl.multiple_of(r * NK, NK), NK), :]
+            return jnp.concatenate([own, pltpu.roll(side, LANES - 2 - 4 * r, 1)], axis=1)
+
+        side = side_ref[0:NK, :]
+        q0, q1 = field(g_ref, side, 1 - even), field(g_ref, side, even)
+        a1, a2 = field(ga, ha[...], 1 - even), field(ga, ha[...], even)
+        own, other = ext_ref[0, l], ext_ref[1, l]
+        cx_0, cx_1, cx_a = (
+            0.5 * row_of(own, odd, 0), 0.5 * row_of(own, odd, 1), 0.5 * row_of(other, odd, 0)
+        )
+        cy_0, cy_1, cy_a = (
+            sg * row_of(own, odd, 2), sg * row_of(own, odd, 3), sg * row_of(other, odd, 2)
+        )
+
+        def along(mid, cx):
+            return (
                 (1.0 - 4.0 * KD) * mid
                 + (KD - cx) * pltpu.roll(mid, W - 1, 1)
                 + (KD + cx) * pltpu.roll(mid, 1, 1)
-                + (KD - cy) * fields[i + 2]
-                + (KD + cy) * fields[i]
             )
-            out = jnp.where(masks[i], out, 0.0)
-            half = out[0:8] + out[8:16]
-            firsts.append(half + pltpu.roll(half, 4, 0))
-        new = []
-        for y in range(2):
-            cx, cy = winds(1, y)
-            cx, cy = cx[:, 0:LANES], cy[:, 0:LANES]
-            mid = firsts[y + 1]
-            out = (
-                (1.0 - 4.0 * KD) * mid[:, 0:LANES]
-                + (KD - cx) * pltpu.roll(mid, W - 1, 1)[:, 0:LANES]
-                + (KD + cx) * pltpu.roll(mid, 1, 1)[:, 0:LANES]
-                + (KD - cy) * firsts[y + 2][:, 0:LANES]
-                + (KD + cy) * firsts[y][:, 0:LANES]
-            )
-            kern = stats[1][4 + y : 5 + y, 0:LANES]
-            new.append(sums[y] + kern * out)
-        stat_b = jnp.where(odd, stats[2], stats[0])
-        cx_b = 0.5 * jnp.where(odd, stat_b[0:1], stat_b[1:2])
-        cx_0 = 0.5 * jnp.where(odd, stats[1][1:2], stats[1][0:1])
-        cy_0 = jnp.where(odd, -0.5, 0.5) * jnp.where(odd, stats[1][3:4], stats[1][2:3])
-        kern = jnp.where(odd, stats[1][5:6], stats[1][4:5]) * weight_b
-        sides = []
-        for sign, shift in ((0.5, 1), (-0.5, W - 1)):
-            first = (KD + 2 * sign * cx_b) * (KD + cy_0) * near_b
-            second = pltpu.roll((KD + cy_0) * near_0, shift, 1) * (KD + 2 * sign * cx_0)
-            sides.append(jnp.where(head_0, kern * (first + second), 0.0)[:, 0:LANES])
-        left = pltpu.roll(sides[0], 8 * l + 1, 1)
-        right = pltpu.roll(sides[1], 8 * l + 3, 1)
-        lane = iota((NK, LANES), 1)
-        corner = jnp.where(
-            lane == 8 * l + 1, left, jnp.where(lane == 8 * l + 2, right, sums[2])
-        )
-        return tuple(new) + (corner,)
-
-    misc = ext_ref[1, z.levels]
-    misc_b = jnp.where(odd, ext_ref[2, z.levels], ext_ref[0, z.levels])
-    mech_0 = jnp.where(odd, misc[1:2], misc[0:1])
-    mech_b = jnp.where(odd, misc_b[0:1], misc_b[1:2])
-    weight_b = jnp.where(odd, misc[5:6], misc[4:5])
-    near_0 = (mech_0 == (k_of + 1).astype(F32)).astype(F32)
-    near_b = (mech_b == (k_of + 1).astype(F32)).astype(F32)
-    head_0 = mech_0 == (iota((NK, W), 0) % NM + 1).astype(F32)
+
+        f0 = along(q0, cx_0) + (KD - cy_0) * q1
+        f1 = along(q1, cx_1) + (KD - cy_1) * a1 + (KD + cy_1) * q0
+        fa = along(a1, cx_a) + (KD - cy_a) * a2 + (KD + cy_a) * q1
+        f0, f1, fa = (
+            fold(jnp.where(m, f, 0.0)) for m, f in ((mask_0, f0), (mask_1, f1), (mask_a, fa))
+        )
+        h0 = along(f0, cx_0) + (KD - cy_0) * f1
+        h1 = along(f1, cx_1) + (KD - cy_1) * fa + (KD + cy_1) * f0
+        kern_0, kern_1 = row_of(own, odd, 4), row_of(own, odd, 5)
+        s0 = carry[0] + (kern_0 * h0)[:, 0:LANES]
+        s1 = carry[1] + (kern_1 * h1)[:, 0:LANES]
+        step = jnp.where(mask_0, KD + cy_0, 0.0)
+        scale = jnp.where(head_0, kern_0 * weight_0, 0.0)
+        left = (scale * pltpu.roll(step, 1, 1) * (KD + cx_0))[:, 0:LANES]
+        right = (scale * pltpu.roll(step, W - 1, 1) * (KD - cx_0))[:, 0:LANES]
+        return s0, s1, edge_lanes(z, l, left, right, carry[2])
+
     none = jnp.zeros((8, LANES), F32)
-    sums = lax.fori_loop(0, z.levels, level, (none, none, zero), unroll=UNROLL)
-    corner_ref[...] = sums[2]
+    s0, s1, corner = lax.fori_loop(
+        0, z.levels, level, (none, none, jnp.zeros((NK, LANES), F32)), unroll=UNROLL
+    )
+    sums_ref[0:8, :] = s0
+    sums_ref[8:16, :] = s1
+    corner_ref[...] = corner
+
+
+def beyond_kernel(z, b_ref, g_ref, st_ref, sums_ref, old_ref, part_ref, corner_ref, stat_ref):
+    _, swath, t = z.place()
+    odd = t % 2 == 1
+    even = jnp.where(odd, 0, 1)
+    has_b = jnp.logical_and(t > 0, t < z.nt - 1)
+    sg = jnp.where(odd, -0.5, 0.5)
+    for l in range(z.levels + 1):
+        high = z.o_st + 8 * l
+        both = b_ref[high : high + 8, :].astype(F32) + b_ref[
+            high + z.st16 : high + z.st16 + 8, :
+        ].astype(F32)
+        stat_ref[l] = jnp.where(has_b, both, 0.0)
+    k_of = iota((NK, LANES), 0)
+    lane = iota((NK, LANES), 1)
+    lane8 = iota((8, LANES), 1)
+    sub8 = iota((8, LANES), 0)
+    misc = st_ref[z.base : z.base + 8, :]
+    mech_0 = row_of(misc, odd, 0)
+    mech_b = row_of(stat_ref[z.levels], odd, 1)
+    mask_0 = (mech_0 == (k_of // NM + 1).astype(F32)) & has_b
+    mask_b = mech_b == (k_of // NM + 1).astype(F32)
+    head_0 = mech_0 == (k_of % NM + 1).astype(F32)
+    weight_0 = row_of(misc, odd, 4)
+
+    def level(l, carry):
+        def field(ref, y):
+            at = pl.ds(pl.multiple_of((2 * l + y) * NK, NK), NK)
+            return ref[at, :].astype(F32)
+
+        q0 = field(g_ref, 1 - even)
+        b1, b2 = field(b_ref, even), field(b_ref, 1 - even)
+        own = st_ref[pl.ds(pl.multiple_of(8 * l, 8), 8), :]
+        other = stat_ref[l]
+        cx_0, cx_b = 0.5 * row_of(own, odd, 0), 0.5 * row_of(other, odd, 1)
+        cy_0, cy_1, cy_b = (
+            sg * row_of(own, odd, 2), sg * row_of(own, odd, 3), sg * row_of(other, odd, 3)
+        )
+
+        def along(mid, cx, lane):
+            east = jnp.where(lane < LANES - 1, pltpu.roll(mid, LANES - 1, 1), 0.0)
+            west = jnp.where(lane > 0, pltpu.roll(mid, 1, 1), 0.0)
+            return (1.0 - 4.0 * KD) * mid + (KD - cx) * east + (KD + cx) * west
+
+        fb = along(b1, cx_b, lane) + (KD - cy_b) * q0 + (KD + cy_b) * b2
+        fb = fold(jnp.where(mask_b, fb, 0.0))
+        f0 = fold(jnp.where(mask_0, (KD + cy_0) * b1, 0.0))
+        kern_0, kern_1 = row_of(own, odd, 4), row_of(own, odd, 5)
+        s0 = carry[0] + kern_0 * (along(f0, cx_0, lane8) + (KD + cy_0) * fb)
+        s1 = carry[1] + kern_1 * (KD + cy_1) * f0
+        step = jnp.where(head_0 & mask_b, kern_0 * weight_0 * (KD + cy_0), 0.0)
+        left, right = step * (KD + cx_b), step * (KD - cx_b)
+        corner = edge_lanes(z, l, left, right, carry[2])
+        return s0, s1, corner
+
+    s0, s1, corner = lax.fori_loop(
+        0,
+        z.levels,
+        level,
+        (sums_ref[0:8, :], sums_ref[8:16, :], jnp.zeros((NK, LANES), F32)),
+        unroll=UNROLL,
+    )
+    corner_ref[...] = corner + old_ref[...]
     pixels = LANES // 2
     sub = iota((pixels, LANES), 0)
-    lane = iota((pixels, LANES), 1)
-    wide8 = iota((8, LANES), 0)
-    lane8 = iota((8, LANES), 1)
     total = jnp.zeros((8, LANES), F32)
-    base = z.base
-    for y in range(2):
-        column = jnp.sum(jnp.where(final[y], sums[y], 0.0), axis=0, keepdims=True)
-        column = column * st_ref[base + 4 + y : base + 5 + y, :]
-        pix = st_ref[base + 2 + y : base + 3 + y, :]
-        hit = jnp.where(pix == sub.astype(F32), column, 0.0)
+    for y, sums in ((0, s0), (1, s1)):
+        final = row_of(misc, odd, y) == (sub8 + 1).astype(F32)
+        column = jnp.sum(jnp.where(final, sums, 0.0), axis=0, keepdims=True)
+        column = column * row_of(misc, odd, 4 + y)
+        hit = jnp.where(row_of(misc, odd, 2 + y) == sub.astype(F32), column, 0.0)
         tall = jnp.sum(hit, axis=1, keepdims=True)
-        row = jnp.sum(jnp.where(sub == lane, tall, 0.0), axis=0, keepdims=True)
-        owner = st_ref[base + 6 + y : base + 7 + y, :]
-        total = total + jnp.where(owner == wide8.astype(F32), row, 0.0)
-    prec = st_ref[z.st : z.st + 1, :]
+        row = jnp.sum(
+            jnp.where(sub == iota((pixels, LANES), 1), tall, 0.0), axis=0, keepdims=True
+        )
+        total = total + jnp.where(row_of(misc, odd, 6 + y) == sub8.astype(F32), row, 0.0)
     part_ref[...] = jnp.where(
-        lane8 < pixels, total, jnp.where(wide8 == swath, prec, 0.0)
-    )
-
-
-def corner_kernel(z, part_ref, corner_ref, far_ref, st_ref, ext_ref, out_ref, full_ref, block, sem):
+        lane8 < pixels, total, jnp.where(sub8 == swath, st_ref[z.st : z.st + 1, :], 0.0)
+    )
+
+
+def corner_kernel(z, part_ref, corner_ref, far_ref, st_ref, out_ref, block_ref):
     _, _, t = z.place()
     odd = t % 2 == 1
     has_b = jnp.logical_and(t > 0, t < z.nt - 1)
     far = jnp.where(has_b, far_ref[...].astype(F32), 0.0)
     side = (far[NK : NK + 16] + far[NK + 16 :])[0:8]
     for l in range(z.levels + 1):
-        block[l] = spread(z, side, l)
-    slot = jnp.where(odd, 2, 0)
-    copy = pltpu.make_async_copy(block, full_ref.at[slot, :, :, pl.ds(LANES, LANES)], sem)
-    copy.start()
+        block_ref[l] = spread(z, side, l)
     g = far[0:NK]
     g = jnp.where(odd, g, pltpu.roll(g, LANES - 4, 1))
     share = jnp.sum(corner_ref[...] * g, axis=0, keepdims=True)
     lane = iota((1, LANES), 1)
     sub8 = iota((8, LANES), 0)
     lane8 = iota((8, LANES), 1)
-    st = st_ref[z.base : z.base + 8, :]
-    pixel = jnp.where(odd, st[3:4], st[2:3])
-    owner = jnp.where(odd, st[7:8], st[6:7])
+    misc = st_ref[z.base : z.base + 8, :]
+    pixel = row_of(misc, odd, 2)
+    owner = row_of(misc, odd, 6)
     total = part_ref[...]
     for c, column in ((1, 0), (2, LANES - 1)):
         value = jnp.sum(jnp.where(lane % 8 == c, share, 0.0), axis=1, keepdims=True)
@@ -320,11 +351,20 @@
         hit = (lane8.astype(F32) == pixel[:, at]) & (sub8.astype(F32) == owner[:, at])
         total = total + jnp.where(hit, value, 0.0)
     out_ref[...] = total
-    copy.wait()
-
-
-def product_kernel(z, own_ref, x0_ref, x1_ref, ext_ref, d_ref, out_ref, dep_ref, v3, tall):
-    gx, swath, _ = z.place()
+
+
+def product_kernel(
+    z, own_ref, x0_ref, x1_ref, oa_ref, stat_ref, block_ref, d_ref, out_ref, dep_ref, v3, tall
+):
+    gx, swath, t = z.place()
+    odd = t % 2 == 1
+
+    def tiles(l):
+        a = oa_ref[1, l]
+        b = jnp.concatenate([stat_ref[l], block_ref[l]], axis=1)
+        return jnp.where(odd, a, b), oa_ref[0, l], jnp.where(odd, b, a)
+
+    miscs = tiles(z.levels)
     W = 2 * LANES
     pixels = LANES // 2
     left, right = sides_of(z, gx, x0_ref[...], x1_ref[...])
@@ -343,7 +383,7 @@
         out = jnp.zeros((8, W), F32)
         for s in range(3):
             for y in range(2):
-                row = ext_ref[s, z.levels, 2 * f + y : 2 * f + y + 1, :]
+                row = miscs[s][2 * f + y : 2 * f + y + 1]
                 out = jnp.where(iota((8, W), 0) == 2 * s + y, row, out)
         return out
 
@@ -371,10 +411,10 @@
     m_of = iota((8, W), 0) % NM
     drive = []
     for i, (s, y) in enumerate(place):
-        mech = ext_ref[s, z.levels, y : y + 1, :]
+        mech = miscs[s][y : y + 1]
         drive.append(jnp.where(mech == (m_of + 1).astype(F32), back[i : i + 1, :], 0.0))
     masks = [
-        ext_ref[s, z.levels, y : y + 1, :] == (k_of + 1).astype(F32) for s, y in place[1:5]
+        miscs[s][y : y + 1] == (k_of + 1).astype(F32) for s, y in place[1:5]
     ]
 
     def unadvect(mid, cx, up, cy_up, down, cy_down):
@@ -387,7 +427,7 @@
         )
 
     def level(l, carry):
-        stats = [ext_ref[s, l] for s in range(3)]
+        stats = tiles(l)
         cx = [0.5 * stats[s][y : y + 1] for s, y in place]
         cy = [0.5 * stats[s][2 + y : 3 + y] for s, y in place]
         kern = [stats[s][4 + y : 5 + y] for s, y in place]
@@ -528,22 +568,13 @@
             )
         )
     )
-    edges, msg = pl.pallas_call(
-        functools.partial(join_kernel, z),
-        out_shape=(shape(2 * z.edge, LANES), shape(z.msg, LANES, dtype=BF)),
-        in_specs=[VMEM, VMEM, ANY],
-        out_specs=(VMEM, ANY),
-        input_output_aliases={2: 1},
-        compiler_params=LIMIT,
-        name="join",
-    )(edge, move(edge, along_y(0)), msg)
-    e0 = move(edges, along_x(0, 1))
-    e1 = move(edges, along_x(1, 1))
+    e0 = move(edge, along_x(0, 0))
+    e1 = move(edge, along_x(1, 0))
     m_b = move(msg, along_y(1))
     m_a = move(msg, along_y(0))
     side, far = pl.pallas_call(
         functools.partial(edges_kernel, z),
-        out_shape=(shape(2 * z.edge, LANES), shape(z.far, LANES, dtype=BF)),
+        out_shape=(shape(z.edge, LANES), shape(z.far, LANES, dtype=BF)),
         in_specs=[VMEM, VMEM],
         out_specs=(VMEM, VMEM),
         compiler_params=LIMIT,
@@ -553,34 +584,37 @@
         name="edges",
     )(e0, e1)
     far_b = move(far, along_y(1))
-    part, ext, corner = pl.pallas_call(
+    sums, ext, corner = pl.pallas_call(
         functools.partial(columns_kernel, z),
         out_shape=(
-            shape(8, LANES), shape(3, levels + 1, 8, 2 * LANES), shape(NK, LANES)
+            shape(16, LANES), shape(2, levels + 1, 8, 2 * LANES), shape(NK, LANES)
         ),
         in_specs=[VMEM] * 5,
         out_specs=(VMEM,) * 3,
-        scratch_shapes=[
-            pltpu.VMEM((3 * z.o_st, LANES), F32),
-            pltpu.VMEM((3 * NK, LANES), F32),
-        ],
+        scratch_shapes=[pltpu.VMEM((z.o_st, LANES), F32), pltpu.VMEM((NK, LANES), F32)],
         compiler_params=LIMIT,
         name="columns",
-    )(m_a, m_b, g, st, side)
-    part, ext = pl.pallas_call(
+    )(m_a, g, st, side, move(side, along_y(0)))
+    part, corner, stat = pl.pallas_call(
+        functools.partial(beyond_kernel, z),
+        out_shape=(shape(8, LANES), shape(NK, LANES), shape(levels + 1, 8, LANES)),
+        in_specs=[VMEM] * 5,
+        out_specs=(VMEM,) * 3,
+        compiler_params=LIMIT,
+        name="beyond",
+    )(m_b, g, st, sums, corner)
+    part, block = pl.pallas_call(
         functools.partial(corner_kernel, z),
-        out_shape=(shape(8, LANES), shape(3, levels + 1, 8, 2 * LANES)),
-        in_specs=[VMEM] * 4 + [ANY],
-        out_specs=(VMEM, ANY),
-        scratch_shapes=[pltpu.VMEM((levels + 1, 8, LANES), F32), pltpu.SemaphoreType.DMA],
-        input_output_aliases={4: 1},
+        out_shape=(shape(8, LANES), shape(levels + 1, 8, LANES)),
+        in_specs=[VMEM] * 4,
+        out_specs=(VMEM, VMEM),
         compiler_params=LIMIT,
         name="corner",
-    )(part, corner, far_b, st, ext)
+    )(part, corner, far_b, st)
     part = part + lax.ppermute(part, "swath", [(i, i ^ 1) for i in range(nsw)])
     turns = [
         lax.ppermute(part, "swath", [(i, (i + 2 * k) % nsw ^ 1) for i in range(nsw)])
-        for k in range(1, nsw // 2)
+        for k in TURNS
     ]
     for turn in turns:
         part = part + turn
@@ -590,7 +624,7 @@
     product, dep = pl.pallas_call(
         functools.partial(product_kernel, z),
         out_shape=(shape(*cells, dtype=BF), shape(1, pixels)),
-        in_specs=[VMEM] * 5,
+        in_specs=[VMEM] * 7,
         out_specs=(VMEM, VMEM),
         scratch_shapes=[
             pltpu.VMEM((3 * NK, z.rows * LANES), BF),
@@ -598,7 +632,7 @@
         ],
         compiler_params=LIMIT,
         name="product",
-    )(both, b0, b1, ext, d)
+    )(both, b0, b1, ext, stat, block, d)
     return product.reshape(direction.shape), dep.reshape(-1)
 
 

time: 33.9 us -> 32.1 us (0.947)
  starting transfers between devices: 17.2 us -> 16 us
    ppermute x9, starting transfers between devices: 10.1 us -> 8.87 us  [move(): return lax.ppermute(v, ALL, perm)]
    ppermute x3, starting transfers between devices: 4.55 us -> 5.12 us  [per_device(): lax.ppermute(part, 'swath', [(i, (i + 2 * k) % nsw ^ 1) for i in range(ns...]
    ppermute x1, starting transfers between devices: 2.54 us -> 1.97 us  [per_device(): part = part + lax.ppermute(part, 'swath', [(i, i ^ 1) for i in range(nsw)])]
  transfers between devices with their start and end apart: 13 -> 13, of which waited for: 6 -> 7; matrix products, arithmetic and copies ran while one was open for 0% -> 0% of each run, Pallas kernels for 6% -> 6%
where the time goes in v2:
time: 32.1 us; the launch traced here: 32 us
  starting transfers between devices  16 us (50%)
  waiting for transfers between devices  9.6 us (30%)
  Pallas kernels  5.73 us (18%)
  between operations  0.68 us (2%)
    ppermute x9, starting transfers between devices, move(): return lax.ppermute(v, ALL, perm)  8.87 us
    ppermute x9, waiting for transfers between devices, move(): return lax.ppermute(v, ALL, perm)  5.34 us
    ppermute x3, starting transfers between devices, per_device(): lax.ppermute(part, 'swath', [(i, (i + 2 * k) % nsw ^ 1) for i in range(ns...  5.12 us
    ppermute x3, waiting for transfers between devices, per_device(): lax.ppermute(part, 'swath', [(i, (i + 2 * k) % nsw ^ 1) for i in range(ns...  3.44 us
    ppermute x1, starting transfers between devices, per_device(): part = part + lax.ppermute(part, 'swath', [(i, i ^ 1) for i in range(nsw)])  1.97 us
    pallas_call x1, Pallas kernels, per_device(): pl.pallas_call(functools.partial(columns_kernel, z), out_shape=(shape(16,...  1.79 us
    pallas_call x1, Pallas kernels, per_device(): pl.pallas_call(functools.partial(project_kernel, z), out_shape=(shape(z.o...  1.76 us
    pallas_call x1, Pallas kernels, per_device(): pl.pallas_call(functools.partial(product_kernel, z), out_shape=(shape(*ce...  1.73 us
  transfers between devices with their start and end apart: 13, of which 7 were waited for; matrix products, arithmetic and copies ran while one was open for 0% of the time, Pallas kernels for 6%

profile of v2, /device:TPU:97, one launch (start us, length us, event | category | flops | bytes accessed | tf_op | source)
XLA Modules:
  0.0 32.0 jit_solution(11205680557923907830)
XLA Ops:
  0.6 1.8 %project.1 = (f32[320,128]{1,0:T(8,128)S(1)}, bf16[512,128]{1,0:T(8,128)(2,1)S(1)}, f32[24,128]{1,0:T(8,128)S(1)}, f32[96,128]{1,0:T(8,128)S(1)}, bf16[48,120]{1,0:T(8,128)(2,1)S(1)}) custom-call(bf16[2400,128]{1,0:T(8,128)(2,1)} %bitcast.5, bf16[4,120,120]{2,1,0:T(8,128)(2,1)} %prop_hbm.1, f32[10,2,128]{2,1,0:T(2,128)} %cx_hbm.1, f32[10,2,128]{2,1,0:T(2,128)} %cy_hbm.1, ...), custom_call_target="tpu_custom_call" | custom-call | tf_op jit(solution)/shard_map/project/pallas_call | solution.py:534
  2.4 0.8 %collective-permute-start.3 = (f32[24,128]{1,0:T(8,128)S(1)}, f32[24,128]{1,0:T(8,128)S(1)}, u32[]{:S(2)}, u32[]{:S(2)}) collective-permute-start(f32[24,128]{1,0:T(8,128)S(1)} %get-tuple-element.22), channel_id=1, source_target_pairs={{0,1},{1,0},{2,3},{3,2},{4,5},{5,4},{6,7},{7,6},{8,9},{9,8},{10,11... | collective-permute-start | bytes 36872 | tf_op jit(solution)/shard_map/ppermute | solution.py:530
  3.2 1.9 %collective-permute-start.2 = (f32[24,128]{1,0:T(8,128)S(1)}, f32[24,128]{1,0:T(8,128)S(1)}, u32[]{:S(2)}, u32[]{:S(2)}) collective-permute-start(f32[24,128]{1,0:T(8,128)S(1)} %get-tuple-element.22), channel_id=1, source_target_pairs={{0,64},{1,65},{2,66},{3,67},{4,68},{5,69},{6,70},{7,71},{8,72},{9,... | collective-permute-start | bytes 36872 | tf_op jit(solution)/shard_map/ppermute | solution.py:530
  5.1 1.2 %collective-permute-start.1 = (bf16[512,128]{1,0:T(8,128)(2,1)S(1)}, bf16[512,128]{1,0:T(8,128)(2,1)S(1)}, u32[]{:S(2)}, u32[]{:S(2)}) collective-permute-start(bf16[512,128]{1,0:T(8,128)(2,1)S(1)} %get-tuple-element.19), channel_id=1, source_target_pairs={{0,1},{1,0},{2,3},{3,2},{4,5},{5,4},{6,7},{7,6},{8,9},{9,8},{10,11... | collective-permute-start | bytes 393224 | tf_op jit(solution)/shard_map/ppermute | solution.py:530
  6.3 1.1 %collective-permute-start = (bf16[512,128]{1,0:T(8,128)(2,1)S(1)}, bf16[512,128]{1,0:T(8,128)(2,1)S(1)}, u32[]{:S(2)}, u32[]{:S(2)}) collective-permute-start(bf16[512,128]{1,0:T(8,128)(2,1)S(1)} %get-tuple-element.19), channel_id=1, source_target_pairs={{0,64},{1,2},{2,1},{3,4},{4,3},{5,6},{6,5},{7,8},{8,7},{9,10},{10,... | collective-permute-start | bytes 393224 | tf_op jit(solution)/shard_map/ppermute | solution.py:530
  7.4 0.0 collective-permute-done.3.x1_ref
  7.4 0.0 collective-permute-done.2.x0_ref
  7.5 1.4 %collective-permute-start.4 = (f32[24,128]{1,0:T(8,128)S(1)}, f32[24,128]{1,0:T(8,128)S(1)}, u32[]{:S(2)}, u32[]{:S(2)}) collective-permute-start(f32[24,128]{1,0:T(8,128)S(1)} %get-tuple-element.23.side_ref), channel_id=1, source_target_pairs={{0,1},{1,0},{2,3},{3,2},{4,5},{5,4},{6,7},{7,6},{8,9},{9,8},{10,11... | collective-permute-start | bytes 36872 | tf_op jit(solution)/shard_map/ppermute | solution.py:530
  8.9 0.4 %collective-permute-start.5 = (bf16[48,128]{1,0:T(8,128)(2,1)S(1)}, bf16[48,128]{1,0:T(8,128)(2,1)S(1)}, u32[]{:S(2)}, u32[]{:S(2)}) collective-permute-start(bf16[48,128]{1,0:T(8,128)(2,1)S(1)} %get-tuple-element.28), channel_id=1, source_target_pairs={{0,64},{1,2},{2,1},{3,4},{4,3},{5,6},{6,5},{7,8},{8,7},{9,10},{10,... | collective-permute-start | bytes 36872 | tf_op jit(solution)/shard_map/ppermute | solution.py:530
  9.3 0.4 %collective-permute-done.4.far_ref = f32[24,128]{1,0:T(8,128)S(1)} collective-permute-done((f32[24,128]{1,0:T(8,128)S(1)}, f32[24,128]{1,0:T(8,128)S(1)}, u32[]{:S(2)}, u32[]{:S(2)}) %collective-permute-start.4) | collective-permute-done | bytes 12320 | tf_op jit(solution)/shard_map/ppermute | solution.py:530
  9.7 0.0 collective-permute-done.1.a_ref
  9.7 1.8 %columns.1 = (f32[16,128]{1,0:T(8,128)S(1)}, f32[2,11,8,256]{3,2,1,0:T(8,128)S(1)}, f32[16,128]{1,0:T(8,128)S(1)}) custom-call(bf16[512,128]{1,0:T(8,128)(2,1)S(1)} %collective-permute-done.1.a_ref, f32[320,128]{1,0:T(8,128)S(1)} %get-tuple-element.20.g_ref, f32[96,128]{1,0:T(8,128)S(1)} %get-tuple-element.21.st_ref, ...), custom_call_target="tpu_custom_call" | custom-call | tf_op jit(solution)/shard_map/columns/pallas_call | solution.py:587
  11.5 0.0 collective-permute-done.b_ref
  11.5 0.3 beyond.1
  11.8 0.5 %collective-permute-done.5.far_ref = bf16[48,128]{1,0:T(8,128)(2,1)S(1)} collective-permute-done((bf16[48,128]{1,0:T(8,128)(2,1)S(1)}, bf16[48,128]{1,0:T(8,128)(2,1)S(1)}, u32[]{:S(2)}, u32[]{:S(2)}) %collective-permute-start.5) | collective-permute-done | bytes 12320 | tf_op jit(solution)/shard_map/ppermute | solution.py:530
  12.3 0.2 corner.1
  12.4 2.0 %collective-permute-start.6 = (f32[8,128]{1,0:T(8,128)S(1)}, f32[8,128]{1,0:T(8,128)S(1)}, u32[]{:S(2)}, u32[]{:S(2)}) collective-permute-start(f32[8,128]{1,0:T(8,128)S(1)} %get-tuple-element.29), channel_id=1, source_target_pairs={{0,1},{1,0},{2,3},{3,2},{4,5},{5,4},{6,7},{7,6},{8,9},{9,8},{10,11... | collective-permute-start | bytes 12296 | tf_op jit(solution)/shard_map/ppermute | solution.py:614
  14.4 0.8 %collective-permute-done.6 = f32[8,128]{1,0:T(8,128)S(1)} collective-permute-done((f32[8,128]{1,0:T(8,128)S(1)}, f32[8,128]{1,0:T(8,128)S(1)}, u32[]{:S(2)}, u32[]{:S(2)}) %collective-permute-start.6) | collective-permute-done | bytes 4128 | tf_op jit(solution)/shard_map/ppermute | solution.py:614
  15.2 1.5 %collective-permute-start.9 = (f32[8,128]{1,0:T(8,128)S(1)}, f32[8,128]{1,0:T(8,128)S(1)}, u32[]{:S(2)}, u32[]{:S(2)}) collective-permute-start(f32[8,128]{1,0:T(8,128)S(1)} %add.12), channel_id=1, source_target_pairs={{0,5},{1,4},{2,7},{3,6},{4,1},{5,0},{6,3},{7,2},{8,13},{9,12},{10,... | collective-permute-start | bytes 12296 | tf_op jit(solution)/shard_map/ppermute | solution.py:616
  16.7 2.9 %collective-permute-start.8 = (f32[8,128]{1,0:T(8,128)S(1)}, f32[8,128]{1,0:T(8,128)S(1)}, u32[]{:S(2)}, u32[]{:S(2)}) collective-permute-start(f32[8,128]{1,0:T(8,128)S(1)} %add.12), channel_id=1, source_target_pairs={{0,7},{1,6},{2,1},{3,0},{4,3},{5,2},{6,5},{7,4},{8,15},{9,14},{10,... | collective-permute-start | bytes 12296 | tf_op jit(solution)/shard_map/ppermute | solution.py:616
  19.6 0.8 %collective-permute-start.7 = (f32[8,128]{1,0:T(8,128)S(1)}, f32[8,128]{1,0:T(8,128)S(1)}, u32[]{:S(2)}, u32[]{:S(2)}) collective-permute-start(f32[8,128]{1,0:T(8,128)S(1)} %add.12), channel_id=1, source_target_pairs={{0,3},{1,2},{2,5},{3,4},{4,7},{5,6},{6,1},{7,0},{8,11},{9,10},{10,... | collective-permute-start | bytes 12296 | tf_op jit(solution)/shard_map/ppermute | solution.py:616
  20.4 0.0 collective-permute-done.9
  20.4 1.3 %collective-permute-done.8 = f32[8,128]{1,0:T(8,128)S(1)} collective-permute-done((f32[8,128]{1,0:T(8,128)S(1)}, f32[8,128]{1,0:T(8,128)S(1)}, u32[]{:S(2)}, u32[]{:S(2)}) %collective-permute-start.8) | collective-permute-done | bytes 4128 | tf_op jit(solution)/shard_map/ppermute | solution.py:616
  21.7 2.1 %collective-permute-done.7 = f32[8,128]{1,0:T(8,128)S(1)} collective-permute-done((f32[8,128]{1,0:T(8,128)S(1)}, f32[8,128]{1,0:T(8,128)S(1)}, u32[]{:S(2)}, u32[]{:S(2)}) %collective-permute-start.7) | collective-permute-done | bytes 4128 | tf_op jit(solution)/shard_map/ppermute | solution.py:616
  23.8 0.8 %collective-permute-start.10 = (f32[8,128]{1,0:T(8,128)S(1)}, f32[8,128]{1,0:T(8,128)S(1)}, u32[]{:S(2)}, u32[]{:S(2)}) collective-permute-start(f32[8,128]{1,0:T(8,128)S(1)} %add_add_fusion), channel_id=1, source_target_pairs={{0,9},{1,8},{2,0},{3,1},{4,2},{5,3},{6,4},{7,5},{8,17},{9,16},{10,... | collective-permute-start | bytes 12296 | tf_op jit(solution)/shard_map/ppermute | solution.py:530
  24.6 2.3 %collective-permute-done.10 = f32[8,128]{1,0:T(8,128)S(1)} collective-permute-done((f32[8,128]{1,0:T(8,128)S(1)}, f32[8,128]{1,0:T(8,128)S(1)}, u32[]{:S(2)}, u32[]{:S(2)}) %collective-permute-start.10) | collective-permute-done | bytes 4128 | tf_op jit(solution)/shard_map/ppermute | solution.py:530
  26.8 0.3 %collective-permute-start.12 = (f32[16,128]{1,0:T(8,128)S(1)}, f32[16,128]{1,0:T(8,128)S(1)}, u32[]{:S(2)}, u32[]{:S(2)}) collective-permute-start(f32[16,128]{1,0:T(8,128)S(1)} %pad_maximum_fusion.own_ref), channel_id=1, source_target_pairs={{0,1},{1,0},{2,3},{3,2},{4,5},{5,4},{6,7},{7,6},{8,9},{9,8},{10,11... | collective-permute-start | bytes 24584 | tf_op jit(solution)/shard_map/ppermute | solution.py:530
  27.2 0.9 %collective-permute-start.11 = (f32[16,128]{1,0:T(8,128)S(1)}, f32[16,128]{1,0:T(8,128)S(1)}, u32[]{:S(2)}, u32[]{:S(2)}) collective-permute-start(f32[16,128]{1,0:T(8,128)S(1)} %pad_maximum_fusion.own_ref), channel_id=1, source_target_pairs={{0,65},{1,64},{2,67},{3,66},{4,69},{5,68},{6,71},{7,70},{8,73},{9,... | collective-permute-start | bytes 24584 | tf_op jit(solution)/shard_map/ppermute | solution.py:530
  28.1 0.0 collective-permute-done.12.x1_ref
  28.1 2.2 %collective-permute-done.11.x0_ref = f32[16,128]{1,0:T(8,128)S(1)} collective-permute-done((f32[16,128]{1,0:T(8,128)S(1)}, f32[16,128]{1,0:T(8,128)S(1)}, u32[]{:S(2)}, u32[]{:S(2)}) %collective-permute-start.11) | collective-permute-done | bytes 8224 | tf_op jit(solution)/shard_map/ppermute | solution.py:530
  30.3 1.7 %product.1 = (bf16[2400,128]{1,0:T(8,128)(2,1)}, f32[1,64]{1,0:T(1,128)}) custom-call(f32[16,128]{1,0:T(8,128)S(1)} %pad_maximum_fusion.own_ref, f32[16,128]{1,0:T(8,128)S(1)} %collective-permute-done.11.x0_ref, f32[16,128]{1,0:T(8,128)S(1)} %collective-permute-done.12.x1_ref, f32[2,11,8,256]{3,2,1,0:T(8,128)S(1)} %get-tuple-element.30.oa_ref, ...), custom_call_target="tpu_custom_call" | custom-call | tf_op jit(solution)/shard_map/product/pallas_call | solution.py:624
  (4 shorter events, 0.0 us)
Async XLA Ops:
  2.4 5.0 %collective-permute-start.3 = (f32[24,128]{1,0:T(8,128)S(1)}, f32[24,128]{1,0:T(8,128)S(1)}, u32[]{:S(2)}, u32[]{:S(2)}) collective-permute-start(f32[24,128]{1,0:T(8,128)S(1)} %get-tuple-element.22), channel_id=1, source_target_pairs={{0,1},{1,0},{2,3},{3,2},{4,5},{5,4},{6,7},{7,6},{8,9},{9,8},{10,11... | collective-permute-start | bytes 36872 | tf_op jit(solution)/shard_map/ppermute | solution.py:530
  3.2 4.3 %collective-permute-start.2 = (f32[24,128]{1,0:T(8,128)S(1)}, f32[24,128]{1,0:T(8,128)S(1)}, u32[]{:S(2)}, u32[]{:S(2)}) collective-permute-start(f32[24,128]{1,0:T(8,128)S(1)} %get-tuple-element.22), channel_id=1, source_target_pairs={{0,64},{1,65},{2,66},{3,67},{4,68},{5,69},{6,70},{7,71},{8,72},{9,... | collective-permute-start | bytes 36872 | tf_op jit(solution)/shard_map/ppermute | solution.py:530
  5.1 4.6 %collective-permute-start.1 = (bf16[512,128]{1,0:T(8,128)(2,1)S(1)}, bf16[512,128]{1,0:T(8,128)(2,1)S(1)}, u32[]{:S(2)}, u32[]{:S(2)}) collective-permute-start(bf16[512,128]{1,0:T(8,128)(2,1)S(1)} %get-tuple-element.19), channel_id=1, source_target_pairs={{0,1},{1,0},{2,3},{3,2},{4,5},{5,4},{6,7},{7,6},{8,9},{9,8},{10,11... | collective-permute-start | bytes 393224 | tf_op jit(solution)/shard_map/ppermute | solution.py:530
  6.3 5.2 %collective-permute-start = (bf16[512,128]{1,0:T(8,128)(2,1)S(1)}, bf16[512,128]{1,0:T(8,128)(2,1)S(1)}, u32[]{:S(2)}, u32[]{:S(2)}) collective-permute-start(bf16[512,128]{1,0:T(8,128)(2,1)S(1)} %get-tuple-element.19), channel_id=1, source_target_pairs={{0,64},{1,2},{2,1},{3,4},{4,3},{5,6},{6,5},{7,8},{8,7},{9,10},{10,... | collective-permute-start | bytes 393224 | tf_op jit(solution)/shard_map/ppermute | solution.py:530
  7.5 2.2 %collective-permute-start.4 = (f32[24,128]{1,0:T(8,128)S(1)}, f32[24,128]{1,0:T(8,128)S(1)}, u32[]{:S(2)}, u32[]{:S(2)}) collective-permute-start(f32[24,128]{1,0:T(8,128)S(1)} %get-tuple-element.23.side_ref), channel_id=1, source_target_pairs={{0,1},{1,0},{2,3},{3,2},{4,5},{5,4},{6,7},{7,6},{8,9},{9,8},{10,11... | collective-permute-start | bytes 36872 | tf_op jit(solution)/shard_map/ppermute | solution.py:530
  8.9 3.4 %collective-permute-start.5 = (bf16[48,128]{1,0:T(8,128)(2,1)S(1)}, bf16[48,128]{1,0:T(8,128)(2,1)S(1)}, u32[]{:S(2)}, u32[]{:S(2)}) collective-permute-start(bf16[48,128]{1,0:T(8,128)(2,1)S(1)} %get-tuple-element.28), channel_id=1, source_target_pairs={{0,64},{1,2},{2,1},{3,4},{4,3},{5,6},{6,5},{7,8},{8,7},{9,10},{10,... | collective-permute-start | bytes 36872 | tf_op jit(solution)/shard_map/ppermute | solution.py:530
  12.4 2.8 %collective-permute-start.6 = (f32[8,128]{1,0:T(8,128)S(1)}, f32[8,128]{1,0:T(8,128)S(1)}, u32[]{:S(2)}, u32[]{:S(2)}) collective-permute-start(f32[8,128]{1,0:T(8,128)S(1)} %get-tuple-element.29), channel_id=1, source_target_pairs={{0,1},{1,0},{2,3},{3,2},{4,5},{5,4},{6,7},{7,6},{8,9},{9,8},{10,11... | collective-permute-start | bytes 12296 | tf_op jit(solution)/shard_map/ppermute | solution.py:614
  15.2 5.1 %collective-permute-start.9 = (f32[8,128]{1,0:T(8,128)S(1)}, f32[8,128]{1,0:T(8,128)S(1)}, u32[]{:S(2)}, u32[]{:S(2)}) collective-permute-start(f32[8,128]{1,0:T(8,128)S(1)} %add.12), channel_id=1, source_target_pairs={{0,5},{1,4},{2,7},{3,6},{4,1},{5,0},{6,3},{7,2},{8,13},{9,12},{10,... | collective-permute-start | bytes 12296 | tf_op jit(solution)/shard_map/ppermute | solution.py:616
  16.7 5.0 %collective-permute-start.8 = (f32[8,128]{1,0:T(8,128)S(1)}, f32[8,128]{1,0:T(8,128)S(1)}, u32[]{:S(2)}, u32[]{:S(2)}) collective-permute-start(f32[8,128]{1,0:T(8,128)S(1)} %add.12), channel_id=1, source_target_pairs={{0,7},{1,6},{2,1},{3,0},{4,3},{5,2},{6,5},{7,4},{8,15},{9,14},{10,... | collective-permute-start | bytes 12296 | tf_op jit(solution)/shard_map/ppermute | solution.py:616
  19.6 4.2 %collective-permute-start.7 = (f32[8,128]{1,0:T(8,128)S(1)}, f32[8,128]{1,0:T(8,128)S(1)}, u32[]{:S(2)}, u32[]{:S(2)}) collective-permute-start(f32[8,128]{1,0:T(8,128)S(1)} %add.12), channel_id=1, source_target_pairs={{0,3},{1,2},{2,5},{3,4},{4,7},{5,6},{6,1},{7,0},{8,11},{9,10},{10,... | collective-permute-start | bytes 12296 | tf_op jit(solution)/shard_map/ppermute | solution.py:616
  23.8 3.0 %collective-permute-start.10 = (f32[8,128]{1,0:T(8,128)S(1)}, f32[8,128]{1,0:T(8,128)S(1)}, u32[]{:S(2)}, u32[]{:S(2)}) collective-permute-start(f32[8,128]{1,0:T(8,128)S(1)} %add_add_fusion), channel_id=1, source_target_pairs={{0,9},{1,8},{2,0},{3,1},{4,2},{5,3},{6,4},{7,5},{8,17},{9,16},{10,... | collective-permute-start | bytes 12296 | tf_op jit(solution)/shard_map/ppermute | solution.py:530
  26.8 1.3 %collective-permute-start.12 = (f32[16,128]{1,0:T(8,128)S(1)}, f32[16,128]{1,0:T(8,128)S(1)}, u32[]{:S(2)}, u32[]{:S(2)}) collective-permute-start(f32[16,128]{1,0:T(8,128)S(1)} %pad_maximum_fusion.own_ref), channel_id=1, source_target_pairs={{0,1},{1,0},{2,3},{3,2},{4,5},{5,4},{6,7},{7,6},{8,9},{9,8},{10,11... | collective-permute-start | bytes 24584 | tf_op jit(solution)/shard_map/ppermute | solution.py:530
  27.2 3.1 %collective-permute-start.11 = (f32[16,128]{1,0:T(8,128)S(1)}, f32[16,128]{1,0:T(8,128)S(1)}, u32[]{:S(2)}, u32[]{:S(2)}) collective-permute-start(f32[16,128]{1,0:T(8,128)S(1)} %pad_maximum_fusion.own_ref), channel_id=1, source_target_pairs={{0,65},{1,64},{2,67},{3,66},{4,69},{5,68},{6,71},{7,70},{8,73},{9,... | collective-permute-start | bytes 24584 | tf_op jit(solution)/shard_map/ppermute | solution.py:530

commit v3 on v2

--- a/solution.py
+++ b/solution.py
@@ -613,8 +613,8 @@
     )(part, corner, far_b, st)
     part = part + lax.ppermute(part, "swath", [(i, i ^ 1) for i in range(nsw)])
     turns = [
-        lax.ppermute(part, "swath", [(i, (i + 2 * k) % nsw ^ 1) for i in range(nsw)])
-        for k in TURNS
+        lax.ppermute(part, "swath", [(i, i ^ (2 * k) ^ 1) for i in range(nsw)])
+        for k in (1, 3, 2)
     ]
     for turn in turns:
         part = part + turn

time: 32.1 us -> 31 us (0.966)
  waiting for transfers between devices: 9.6 us -> 7.61 us
  starting transfers between devices: 16 us -> 16.7 us
    ppermute x3, waiting for transfers between devices: 3.44 us -> 2.23 us  [per_device(): lax.ppermute(part, 'swath', [(i, i ^ 2 * k ^ 1) for i in range(nsw)])]
    ppermute x9, waiting for transfers between devices: 5.34 us -> 4.56 us  [move(): return lax.ppermute(v, ALL, perm)]
    ppermute x9, starting transfers between devices: 8.87 us -> 9.66 us  [move(): return lax.ppermute(v, ALL, perm)]
  transfers between devices with their start and end apart: 13 -> 13, of which waited for: 7 -> 7; matrix products, arithmetic and copies ran while one was open for 0% -> 0% of each run, Pallas kernels for 6% -> 7%
where the time goes in v3:
time: 31 us; the launch traced here: 30.8 us
  starting transfers between devices  16.7 us (54%)
  waiting for transfers between devices  7.61 us (25%)
  Pallas kernels  5.74 us (19%)
  between operations  0.68 us (2%)
    ppermute x9, starting transfers between devices, move(): return lax.ppermute(v, ALL, perm)  9.66 us
    ppermute x3, starting transfers between devices, per_device(): lax.ppermute(part, 'swath', [(i, i ^ 2 * k ^ 1) for i in range(nsw)])  5.12 us
    ppermute x9, waiting for transfers between devices, move(): return lax.ppermute(v, ALL, perm)  4.56 us
    ppermute x3, waiting for transfers between devices, per_device(): lax.ppermute(part, 'swath', [(i, i ^ 2 * k ^ 1) for i in range(nsw)])  2.23 us
    ppermute x1, starting transfers between devices, per_device(): part = part + lax.ppermute(part, 'swath', [(i, i ^ 1) for i in range(nsw)])  1.97 us
    pallas_call x1, Pallas kernels, per_device(): pl.pallas_call(functools.partial(columns_kernel, z), out_shape=(shape(16,...  1.79 us
    pallas_call x1, Pallas kernels, per_device(): pl.pallas_call(functools.partial(project_kernel, z), out_shape=(shape(z.o...  1.76 us
    pallas_call x1, Pallas kernels, per_device(): pl.pallas_call(functools.partial(product_kernel, z), out_shape=(shape(*ce...  1.74 us
  transfers between devices with their start and end apart: 13, of which 7 were waited for; matrix products, arithmetic and copies ran while one was open for 0% of the time, Pallas kernels for 7%

profile of v3, /device:TPU:97, one launch (start us, length us, event | category | flops | bytes accessed | tf_op | source)
XLA Modules:
  0.0 30.8 jit_solution(7573584001191128598)
XLA Ops:
  0.6 1.8 %project.1 = (f32[320,128]{1,0:T(8,128)S(1)}, bf16[512,128]{1,0:T(8,128)(2,1)S(1)}, f32[24,128]{1,0:T(8,128)S(1)}, f32[96,128]{1,0:T(8,128)S(1)}, bf16[48,120]{1,0:T(8,128)(2,1)S(1)}) custom-call(bf16[2400,128]{1,0:T(8,128)(2,1)} %bitcast.5, bf16[4,120,120]{2,1,0:T(8,128)(2,1)} %prop_hbm.1, f32[10,2,128]{2,1,0:T(2,128)} %cx_hbm.1, f32[10,2,128]{2,1,0:T(2,128)} %cy_hbm.1, ...), custom_call_target="tpu_custom_call" | custom-call | tf_op jit(solution)/shard_map/project/pallas_call | solution.py:534
  2.4 0.8 %collective-permute-start.3 = (f32[24,128]{1,0:T(8,128)S(1)}, f32[24,128]{1,0:T(8,128)S(1)}, u32[]{:S(2)}, u32[]{:S(2)}) collective-permute-start(f32[24,128]{1,0:T(8,128)S(1)} %get-tuple-element.22), channel_id=1, source_target_pairs={{0,1},{1,0},{2,3},{3,2},{4,5},{5,4},{6,7},{7,6},{8,9},{9,8},{10,11... | collective-permute-start | bytes 36872 | tf_op jit(solution)/shard_map/ppermute | solution.py:530
  3.2 1.9 %collective-permute-start.2 = (f32[24,128]{1,0:T(8,128)S(1)}, f32[24,128]{1,0:T(8,128)S(1)}, u32[]{:S(2)}, u32[]{:S(2)}) collective-permute-start(f32[24,128]{1,0:T(8,128)S(1)} %get-tuple-element.22), channel_id=1, source_target_pairs={{0,64},{1,65},{2,66},{3,67},{4,68},{5,69},{6,70},{7,71},{8,72},{9,... | collective-permute-start | bytes 36872 | tf_op jit(solution)/shard_map/ppermute | solution.py:530
  5.1 1.2 %collective-permute-start.1 = (bf16[512,128]{1,0:T(8,128)(2,1)S(1)}, bf16[512,128]{1,0:T(8,128)(2,1)S(1)}, u32[]{:S(2)}, u32[]{:S(2)}) collective-permute-start(bf16[512,128]{1,0:T(8,128)(2,1)S(1)} %get-tuple-element.19), channel_id=1, source_target_pairs={{0,1},{1,0},{2,3},{3,2},{4,5},{5,4},{6,7},{7,6},{8,9},{9,8},{10,11... | collective-permute-start | bytes 393224 | tf_op jit(solution)/shard_map/ppermute | solution.py:530
  6.3 1.1 %collective-permute-start = (bf16[512,128]{1,0:T(8,128)(2,1)S(1)}, bf16[512,128]{1,0:T(8,128)(2,1)S(1)}, u32[]{:S(2)}, u32[]{:S(2)}) collective-permute-start(bf16[512,128]{1,0:T(8,128)(2,1)S(1)} %get-tuple-element.19), channel_id=1, source_target_pairs={{0,64},{1,2},{2,1},{3,4},{4,3},{5,6},{6,5},{7,8},{8,7},{9,10},{10,... | collective-permute-start | bytes 393224 | tf_op jit(solution)/shard_map/ppermute | solution.py:530
  7.4 0.0 collective-permute-done.3.x1_ref
  7.4 0.0 collective-permute-done.2.x0_ref
  7.5 1.4 %collective-permute-start.4 = (f32[24,128]{1,0:T(8,128)S(1)}, f32[24,128]{1,0:T(8,128)S(1)}, u32[]{:S(2)}, u32[]{:S(2)}) collective-permute-start(f32[24,128]{1,0:T(8,128)S(1)} %get-tuple-element.23.side_ref), channel_id=1, source_target_pairs={{0,1},{1,0},{2,3},{3,2},{4,5},{5,4},{6,7},{7,6},{8,9},{9,8},{10,11... | collective-permute-start | bytes 36872 | tf_op jit(solution)/shard_map/ppermute | solution.py:530
  8.9 0.4 %collective-permute-start.5 = (bf16[48,128]{1,0:T(8,128)(2,1)S(1)}, bf16[48,128]{1,0:T(8,128)(2,1)S(1)}, u32[]{:S(2)}, u32[]{:S(2)}) collective-permute-start(bf16[48,128]{1,0:T(8,128)(2,1)S(1)} %get-tuple-element.28), channel_id=1, source_target_pairs={{0,64},{1,2},{2,1},{3,4},{4,3},{5,6},{6,5},{7,8},{8,7},{9,10},{10,... | collective-permute-start | bytes 36872 | tf_op jit(solution)/shard_map/ppermute | solution.py:530
  9.3 0.4 %collective-permute-done.4.far_ref = f32[24,128]{1,0:T(8,128)S(1)} collective-permute-done((f32[24,128]{1,0:T(8,128)S(1)}, f32[24,128]{1,0:T(8,128)S(1)}, u32[]{:S(2)}, u32[]{:S(2)}) %collective-permute-start.4) | collective-permute-done | bytes 12320 | tf_op jit(solution)/shard_map/ppermute | solution.py:530
  9.7 0.0 collective-permute-done.1.a_ref
  9.7 1.8 %columns.1 = (f32[16,128]{1,0:T(8,128)S(1)}, f32[2,11,8,256]{3,2,1,0:T(8,128)S(1)}, f32[16,128]{1,0:T(8,128)S(1)}) custom-call(bf16[512,128]{1,0:T(8,128)(2,1)S(1)} %collective-permute-done.1.a_ref, f32[320,128]{1,0:T(8,128)S(1)} %get-tuple-element.20.g_ref, f32[96,128]{1,0:T(8,128)S(1)} %get-tuple-element.21.st_ref, ...), custom_call_target="tpu_custom_call" | custom-call | tf_op jit(solution)/shard_map/columns/pallas_call | solution.py:587
  11.5 0.0 collective-permute-done.b_ref
  11.5 0.3 beyond.1
  11.8 0.5 %collective-permute-done.5.far_ref = bf16[48,128]{1,0:T(8,128)(2,1)S(1)} collective-permute-done((bf16[48,128]{1,0:T(8,128)(2,1)S(1)}, bf16[48,128]{1,0:T(8,128)(2,1)S(1)}, u32[]{:S(2)}, u32[]{:S(2)}) %collective-permute-start.5) | collective-permute-done | bytes 12320 | tf_op jit(solution)/shard_map/ppermute | solution.py:530
  12.3 0.2 corner.1
  12.4 2.0 %collective-permute-start.6 = (f32[8,128]{1,0:T(8,128)S(1)}, f32[8,128]{1,0:T(8,128)S(1)}, u32[]{:S(2)}, u32[]{:S(2)}) collective-permute-start(f32[8,128]{1,0:T(8,128)S(1)} %get-tuple-element.29), channel_id=1, source_target_pairs={{0,1},{1,0},{2,3},{3,2},{4,5},{5,4},{6,7},{7,6},{8,9},{9,8},{10,11... | collective-permute-start | bytes 12296 | tf_op jit(solution)/shard_map/ppermute | solution.py:614
  14.4 0.8 %collective-permute-done.6 = f32[8,128]{1,0:T(8,128)S(1)} collective-permute-done((f32[8,128]{1,0:T(8,128)S(1)}, f32[8,128]{1,0:T(8,128)S(1)}, u32[]{:S(2)}, u32[]{:S(2)}) %collective-permute-start.6) | collective-permute-done | bytes 4128 | tf_op jit(solution)/shard_map/ppermute | solution.py:614
  15.2 1.5 %collective-permute-start.9 = (f32[8,128]{1,0:T(8,128)S(1)}, f32[8,128]{1,0:T(8,128)S(1)}, u32[]{:S(2)}, u32[]{:S(2)}) collective-permute-start(f32[8,128]{1,0:T(8,128)S(1)} %add.12), channel_id=1, source_target_pairs={{0,5},{1,4},{2,7},{3,6},{4,1},{5,0},{6,3},{7,2},{8,13},{9,12},{10,... | collective-permute-start | bytes 12296 | tf_op jit(solution)/shard_map/ppermute | solution.py:616
  16.7 2.9 %collective-permute-start.8 = (f32[8,128]{1,0:T(8,128)S(1)}, f32[8,128]{1,0:T(8,128)S(1)}, u32[]{:S(2)}, u32[]{:S(2)}) collective-permute-start(f32[8,128]{1,0:T(8,128)S(1)} %add.12), channel_id=1, source_target_pairs={{0,7},{1,6},{2,5},{3,4},{4,3},{5,2},{6,1},{7,0},{8,15},{9,14},{10,... | collective-permute-start | bytes 12296 | tf_op jit(solution)/shard_map/ppermute | solution.py:616
  19.6 0.8 %collective-permute-start.7 = (f32[8,128]{1,0:T(8,128)S(1)}, f32[8,128]{1,0:T(8,128)S(1)}, u32[]{:S(2)}, u32[]{:S(2)}) collective-permute-start(f32[8,128]{1,0:T(8,128)S(1)} %add.12), channel_id=1, source_target_pairs={{0,3},{1,2},{2,1},{3,0},{4,7},{5,6},{6,5},{7,4},{8,11},{9,10},{10,... | collective-permute-start | bytes 12296 | tf_op jit(solution)/shard_map/ppermute | solution.py:616
  20.4 0.0 collective-permute-done.9
  20.4 0.6 %collective-permute-done.8 = f32[8,128]{1,0:T(8,128)S(1)} collective-permute-done((f32[8,128]{1,0:T(8,128)S(1)}, f32[8,128]{1,0:T(8,128)S(1)}, u32[]{:S(2)}, u32[]{:S(2)}) %collective-permute-start.8) | collective-permute-done | bytes 4128 | tf_op jit(solution)/shard_map/ppermute | solution.py:616
  20.9 1.6 %collective-permute-done.7 = f32[8,128]{1,0:T(8,128)S(1)} collective-permute-done((f32[8,128]{1,0:T(8,128)S(1)}, f32[8,128]{1,0:T(8,128)S(1)}, u32[]{:S(2)}, u32[]{:S(2)}) %collective-permute-start.7) | collective-permute-done | bytes 4128 | tf_op jit(solution)/shard_map/ppermute | solution.py:616
  22.6 1.6 %collective-permute-start.10 = (f32[8,128]{1,0:T(8,128)S(1)}, f32[8,128]{1,0:T(8,128)S(1)}, u32[]{:S(2)}, u32[]{:S(2)}) collective-permute-start(f32[8,128]{1,0:T(8,128)S(1)} %add_add_fusion), channel_id=1, source_target_pairs={{0,9},{1,8},{2,0},{3,1},{4,2},{5,3},{6,4},{7,5},{8,17},{9,16},{10,... | collective-permute-start | bytes 12296 | tf_op jit(solution)/shard_map/ppermute | solution.py:530
  24.1 1.5 %collective-permute-done.10 = f32[8,128]{1,0:T(8,128)S(1)} collective-permute-done((f32[8,128]{1,0:T(8,128)S(1)}, f32[8,128]{1,0:T(8,128)S(1)}, u32[]{:S(2)}, u32[]{:S(2)}) %collective-permute-start.10) | collective-permute-done | bytes 4128 | tf_op jit(solution)/shard_map/ppermute | solution.py:530
  25.6 0.3 %collective-permute-start.12 = (f32[16,128]{1,0:T(8,128)S(1)}, f32[16,128]{1,0:T(8,128)S(1)}, u32[]{:S(2)}, u32[]{:S(2)}) collective-permute-start(f32[16,128]{1,0:T(8,128)S(1)} %pad_maximum_fusion.own_ref), channel_id=1, source_target_pairs={{0,1},{1,0},{2,3},{3,2},{4,5},{5,4},{6,7},{7,6},{8,9},{9,8},{10,11... | collective-permute-start | bytes 24584 | tf_op jit(solution)/shard_map/ppermute | solution.py:530
  26.0 0.9 %collective-permute-start.11 = (f32[16,128]{1,0:T(8,128)S(1)}, f32[16,128]{1,0:T(8,128)S(1)}, u32[]{:S(2)}, u32[]{:S(2)}) collective-permute-start(f32[16,128]{1,0:T(8,128)S(1)} %pad_maximum_fusion.own_ref), channel_id=1, source_target_pairs={{0,65},{1,64},{2,67},{3,66},{4,69},{5,68},{6,71},{7,70},{8,73},{9,... | collective-permute-start | bytes 24584 | tf_op jit(solution)/shard_map/ppermute | solution.py:530
  26.9 0.0 collective-permute-done.12.x1_ref
  26.9 2.2 %collective-permute-done.11.x0_ref = f32[16,128]{1,0:T(8,128)S(1)} collective-permute-done((f32[16,128]{1,0:T(8,128)S(1)}, f32[16,128]{1,0:T(8,128)S(1)}, u32[]{:S(2)}, u32[]{:S(2)}) %collective-permute-start.11) | collective-permute-done | bytes 8224 | tf_op jit(solution)/shard_map/ppermute | solution.py:530
  29.0 1.7 %product.1 = (bf16[2400,128]{1,0:T(8,128)(2,1)}, f32[1,64]{1,0:T(1,128)}) custom-call(f32[16,128]{1,0:T(8,128)S(1)} %pad_maximum_fusion.own_ref, f32[16,128]{1,0:T(8,128)S(1)} %collective-permute-done.11.x0_ref, f32[16,128]{1,0:T(8,128)S(1)} %collective-permute-done.12.x1_ref, f32[2,11,8,256]{3,2,1,0:T(8,128)S(1)} %get-tuple-element.30.oa_ref, ...), custom_call_target="tpu_custom_call" | custom-call | tf_op jit(solution)/shard_map/product/pallas_call | solution.py:624
  (4 shorter events, 0.0 us)
Async XLA Ops:
  2.4 5.0 %collective-permute-start.3 = (f32[24,128]{1,0:T(8,128)S(1)}, f32[24,128]{1,0:T(8,128)S(1)}, u32[]{:S(2)}, u32[]{:S(2)}) collective-permute-start(f32[24,128]{1,0:T(8,128)S(1)} %get-tuple-element.22), channel_id=1, source_target_pairs={{0,1},{1,0},{2,3},{3,2},{4,5},{5,4},{6,7},{7,6},{8,9},{9,8},{10,11... | collective-permute-start | bytes 36872 | tf_op jit(solution)/shard_map/ppermute | solution.py:530
  3.2 4.3 %collective-permute-start.2 = (f32[24,128]{1,0:T(8,128)S(1)}, f32[24,128]{1,0:T(8,128)S(1)}, u32[]{:S(2)}, u32[]{:S(2)}) collective-permute-start(f32[24,128]{1,0:T(8,128)S(1)} %get-tuple-element.22), channel_id=1, source_target_pairs={{0,64},{1,65},{2,66},{3,67},{4,68},{5,69},{6,70},{7,71},{8,72},{9,... | collective-permute-start | bytes 36872 | tf_op jit(solution)/shard_map/ppermute | solution.py:530
  5.1 4.6 %collective-permute-start.1 = (bf16[512,128]{1,0:T(8,128)(2,1)S(1)}, bf16[512,128]{1,0:T(8,128)(2,1)S(1)}, u32[]{:S(2)}, u32[]{:S(2)}) collective-permute-start(bf16[512,128]{1,0:T(8,128)(2,1)S(1)} %get-tuple-element.19), channel_id=1, source_target_pairs={{0,1},{1,0},{2,3},{3,2},{4,5},{5,4},{6,7},{7,6},{8,9},{9,8},{10,11... | collective-permute-start | bytes 393224 | tf_op jit(solution)/shard_map/ppermute | solution.py:530
  6.3 5.2 %collective-permute-start = (bf16[512,128]{1,0:T(8,128)(2,1)S(1)}, bf16[512,128]{1,0:T(8,128)(2,1)S(1)}, u32[]{:S(2)}, u32[]{:S(2)}) collective-permute-start(bf16[512,128]{1,0:T(8,128)(2,1)S(1)} %get-tuple-element.19), channel_id=1, source_target_pairs={{0,64},{1,2},{2,1},{3,4},{4,3},{5,6},{6,5},{7,8},{8,7},{9,10},{10,... | collective-permute-start | bytes 393224 | tf_op jit(solution)/shard_map/ppermute | solution.py:530
  7.5 2.2 %collective-permute-start.4 = (f32[24,128]{1,0:T(8,128)S(1)}, f32[24,128]{1,0:T(8,128)S(1)}, u32[]{:S(2)}, u32[]{:S(2)}) collective-permute-start(f32[24,128]{1,0:T(8,128)S(1)} %get-tuple-element.23.side_ref), channel_id=1, source_target_pairs={{0,1},{1,0},{2,3},{3,2},{4,5},{5,4},{6,7},{7,6},{8,9},{9,8},{10,11... | collective-permute-start | bytes 36872 | tf_op jit(solution)/shard_map/ppermute | solution.py:530
  8.9 3.4 %collective-permute-start.5 = (bf16[48,128]{1,0:T(8,128)(2,1)S(1)}, bf16[48,128]{1,0:T(8,128)(2,1)S(1)}, u32[]{:S(2)}, u32[]{:S(2)}) collective-permute-start(bf16[48,128]{1,0:T(8,128)(2,1)S(1)} %get-tuple-element.28), channel_id=1, source_target_pairs={{0,64},{1,2},{2,1},{3,4},{4,3},{5,6},{6,5},{7,8},{8,7},{9,10},{10,... | collective-permute-start | bytes 36872 | tf_op jit(solution)/shard_map/ppermute | solution.py:530
  12.4 2.8 %collective-permute-start.6 = (f32[8,128]{1,0:T(8,128)S(1)}, f32[8,128]{1,0:T(8,128)S(1)}, u32[]{:S(2)}, u32[]{:S(2)}) collective-permute-start(f32[8,128]{1,0:T(8,128)S(1)} %get-tuple-element.29), channel_id=1, source_target_pairs={{0,1},{1,0},{2,3},{3,2},{4,5},{5,4},{6,7},{7,6},{8,9},{9,8},{10,11... | collective-permute-start | bytes 12296 | tf_op jit(solution)/shard_map/ppermute | solution.py:614
  15.2 5.1 %collective-permute-start.9 = (f32[8,128]{1,0:T(8,128)S(1)}, f32[8,128]{1,0:T(8,128)S(1)}, u32[]{:S(2)}, u32[]{:S(2)}) collective-permute-start(f32[8,128]{1,0:T(8,128)S(1)} %add.12), channel_id=1, source_target_pairs={{0,5},{1,4},{2,7},{3,6},{4,1},{5,0},{6,3},{7,2},{8,13},{9,12},{10,... | collective-permute-start | bytes 12296 | tf_op jit(solution)/shard_map/ppermute | solution.py:616
  16.7 4.2 %collective-permute-start.8 = (f32[8,128]{1,0:T(8,128)S(1)}, f32[8,128]{1,0:T(8,128)S(1)}, u32[]{:S(2)}, u32[]{:S(2)}) collective-permute-start(f32[8,128]{1,0:T(8,128)S(1)} %add.12), channel_id=1, source_target_pairs={{0,7},{1,6},{2,5},{3,4},{4,3},{5,2},{6,1},{7,0},{8,15},{9,14},{10,... | collective-permute-start | bytes 12296 | tf_op jit(solution)/shard_map/ppermute | solution.py:616
  19.6 3.0 %collective-permute-start.7 = (f32[8,128]{1,0:T(8,128)S(1)}, f32[8,128]{1,0:T(8,128)S(1)}, u32[]{:S(2)}, u32[]{:S(2)}) collective-permute-start(f32[8,128]{1,0:T(8,128)S(1)} %add.12), channel_id=1, source_target_pairs={{0,3},{1,2},{2,1},{3,0},{4,7},{5,6},{6,5},{7,4},{8,11},{9,10},{10,... | collective-permute-start | bytes 12296 | tf_op jit(solution)/shard_map/ppermute | solution.py:616
  22.6 3.0 %collective-permute-start.10 = (f32[8,128]{1,0:T(8,128)S(1)}, f32[8,128]{1,0:T(8,128)S(1)}, u32[]{:S(2)}, u32[]{:S(2)}) collective-permute-start(f32[8,128]{1,0:T(8,128)S(1)} %add_add_fusion), channel_id=1, source_target_pairs={{0,9},{1,8},{2,0},{3,1},{4,2},{5,3},{6,4},{7,5},{8,17},{9,16},{10,... | collective-permute-start | bytes 12296 | tf_op jit(solution)/shard_map/ppermute | solution.py:530
  25.6 1.3 %collective-permute-start.12 = (f32[16,128]{1,0:T(8,128)S(1)}, f32[16,128]{1,0:T(8,128)S(1)}, u32[]{:S(2)}, u32[]{:S(2)}) collective-permute-start(f32[16,128]{1,0:T(8,128)S(1)} %pad_maximum_fusion.own_ref), channel_id=1, source_target_pairs={{0,1},{1,0},{2,3},{3,2},{4,5},{5,4},{6,7},{7,6},{8,9},{9,8},{10,11... | collective-permute-start | bytes 24584 | tf_op jit(solution)/shard_map/ppermute | solution.py:530
  26.0 3.1 %collective-permute-start.11 = (f32[16,128]{1,0:T(8,128)S(1)}, f32[16,128]{1,0:T(8,128)S(1)}, u32[]{:S(2)}, u32[]{:S(2)}) collective-permute-start(f32[16,128]{1,0:T(8,128)S(1)} %pad_maximum_fusion.own_ref), channel_id=1, source_target_pairs={{0,65},{1,64},{2,67},{3,66},{4,69},{5,68},{6,71},{7,70},{8,73},{9,... | collective-permute-start | bytes 24584 | tf_op jit(solution)/shard_map/ppermute | solution.py:530

commit v4 on v3

--- a/solution.py
+++ b/solution.py
@@ -138,7 +138,7 @@
     return jnp.where(gx > 0, left, 0.0), jnp.where(gx < z.ngx - 1, right, 0.0)
 
 
-def edges_kernel(z, x0_ref, x1_ref, side_ref, far_ref):
+def edges_kernel(z, x1_ref, x0_ref, side_ref, far_ref):
     gx, _, _ = z.place()
     left, right = sides_of(z, gx, x0_ref[...], x1_ref[...])
     side = jnp.where(iota(left.shape, 1) % 4 < 2, left, right)
@@ -354,7 +354,7 @@
 
 
 def product_kernel(
-    z, own_ref, x0_ref, x1_ref, oa_ref, stat_ref, block_ref, d_ref, out_ref, dep_ref, v3, tall
+    z, own_ref, x1_ref, x0_ref, oa_ref, stat_ref, block_ref, d_ref, out_ref, dep_ref, v3, tall
 ):
     gx, swath, t = z.place()
     odd = t % 2 == 1
@@ -582,7 +582,7 @@
             flops=20_000_000_000, bytes_accessed=1024, transcendentals=0
         ),
         name="edges",
-    )(e0, e1)
+    )(e1, e0)
     far_b = move(far, along_y(1))
     sums, ext, corner = pl.pallas_call(
         functools.partial(columns_kernel, z),
@@ -632,7 +632,7 @@
         ],
         compiler_params=LIMIT,
         name="product",
-    )(both, b0, b1, ext, stat, block, d)
+    )(both, b1, b0, ext, stat, block, d)
     return product.reshape(direction.shape), dep.reshape(-1)
 
 

time: 31 us -> 30.5 us (0.984); the launches traced: 30.8 us -> 29.9 us
  waiting for transfers between devices: 7.61 us -> 6.66 us
    ppermute x9, waiting for transfers between devices: 4.56 us -> 3.61 us  [move(): return lax.ppermute(v, ALL, perm)]
    ppermute x3, starting transfers between devices: 5.12 us -> 5.63 us  [per_device(): lax.ppermute(part, 'swath', [(i, i ^ 2 * k ^ 1) for i in range(nsw)])]
    ppermute x9, starting transfers between devices: 9.66 us -> 9.24 us  [move(): return lax.ppermute(v, ALL, perm)]
  transfers between devices with their start and end apart: 13 -> 13, of which waited for: 7 -> 6; matrix products, arithmetic and copies ran while one was open for 0% -> 0% of each run, Pallas kernels for 7% -> 7%
where the time goes in v4:
time: 30.5 us; the launch traced here: 29.9 us
  starting transfers between devices  16.8 us (55%)
  waiting for transfers between devices  6.66 us (22%)
  Pallas kernels  5.74 us (19%)
  between operations  0.68 us (2%)
    ppermute x9, starting transfers between devices, move(): return lax.ppermute(v, ALL, perm)  9.24 us
    ppermute x3, starting transfers between devices, per_device(): lax.ppermute(part, 'swath', [(i, i ^ 2 * k ^ 1) for i in range(nsw)])  5.63 us
    ppermute x9, waiting for transfers between devices, move(): return lax.ppermute(v, ALL, perm)  3.61 us
    ppermute x3, waiting for transfers between devices, per_device(): lax.ppermute(part, 'swath', [(i, i ^ 2 * k ^ 1) for i in range(nsw)])  2.23 us
    ppermute x1, starting transfers between devices, per_device(): part = part + lax.ppermute(part, 'swath', [(i, i ^ 1) for i in range(nsw)])  1.97 us
    pallas_call x1, Pallas kernels, per_device(): pl.pallas_call(functools.partial(columns_kernel, z), out_shape=(shape(16,...  1.79 us
    pallas_call x1, Pallas kernels, per_device(): pl.pallas_call(functools.partial(project_kernel, z), out_shape=(shape(z.o...  1.76 us
    pallas_call x1, Pallas kernels, per_device(): pl.pallas_call(functools.partial(product_kernel, z), out_shape=(shape(*ce...  1.74 us
  transfers between devices with their start and end apart: 13, of which 6 were waited for; matrix products, arithmetic and copies ran while one was open for 0% of the time, Pallas kernels for 7%

profile of v4, /device:TPU:97, one launch (start us, length us, event | category | flops | bytes accessed | tf_op | source)
XLA Modules:
  0.0 29.9 jit_solution(4569331260613427917)
XLA Ops:
  0.6 1.8 %project.1 = (f32[320,128]{1,0:T(8,128)S(1)}, bf16[512,128]{1,0:T(8,128)(2,1)S(1)}, f32[24,128]{1,0:T(8,128)S(1)}, f32[96,128]{1,0:T(8,128)S(1)}, bf16[48,120]{1,0:T(8,128)(2,1)S(1)}) custom-call(bf16[2400,128]{1,0:T(8,128)(2,1)} %bitcast.5, bf16[4,120,120]{2,1,0:T(8,128)(2,1)} %prop_hbm.1, f32[10,2,128]{2,1,0:T(2,128)} %cx_hbm.1, f32[10,2,128]{2,1,0:T(2,128)} %cy_hbm.1, ...), custom_call_target="tpu_custom_call" | custom-call | tf_op jit(solution)/shard_map/project/pallas_call | solution.py:534
  2.4 1.4 %collective-permute-start.3 = (f32[24,128]{1,0:T(8,128)S(1)}, f32[24,128]{1,0:T(8,128)S(1)}, u32[]{:S(2)}, u32[]{:S(2)}) collective-permute-start(f32[24,128]{1,0:T(8,128)S(1)} %get-tuple-element.22), channel_id=1, source_target_pairs={{0,64},{1,65},{2,66},{3,67},{4,68},{5,69},{6,70},{7,71},{8,72},{9,... | collective-permute-start | bytes 36872 | tf_op jit(solution)/shard_map/ppermute | solution.py:530
  3.8 1.0 %collective-permute-start.2 = (f32[24,128]{1,0:T(8,128)S(1)}, f32[24,128]{1,0:T(8,128)S(1)}, u32[]{:S(2)}, u32[]{:S(2)}) collective-permute-start(f32[24,128]{1,0:T(8,128)S(1)} %get-tuple-element.22), channel_id=1, source_target_pairs={{0,1},{1,0},{2,3},{3,2},{4,5},{5,4},{6,7},{7,6},{8,9},{9,8},{10,11... | collective-permute-start | bytes 36872 | tf_op jit(solution)/shard_map/ppermute | solution.py:530
  4.7 0.0 collective-permute-start.1
  4.7 1.6 %collective-permute-start = (bf16[512,128]{1,0:T(8,128)(2,1)S(1)}, bf16[512,128]{1,0:T(8,128)(2,1)S(1)}, u32[]{:S(2)}, u32[]{:S(2)}) collective-permute-start(bf16[512,128]{1,0:T(8,128)(2,1)S(1)} %get-tuple-element.19), channel_id=1, source_target_pairs={{0,64},{1,2},{2,1},{3,4},{4,3},{5,6},{6,5},{7,8},{8,7},{9,10},{10,... | collective-permute-start | bytes 393224 | tf_op jit(solution)/shard_map/ppermute | solution.py:530
  6.3 0.0 collective-permute-done.3.x0_ref
  6.4 0.0 collective-permute-done.2.x1_ref
  6.4 0.9 %collective-permute-start.4 = (f32[24,128]{1,0:T(8,128)S(1)}, f32[24,128]{1,0:T(8,128)S(1)}, u32[]{:S(2)}, u32[]{:S(2)}) collective-permute-start(f32[24,128]{1,0:T(8,128)S(1)} %get-tuple-element.23.side_ref), channel_id=1, source_target_pairs={{0,1},{1,0},{2,3},{3,2},{4,5},{5,4},{6,7},{7,6},{8,9},{9,8},{10,11... | collective-permute-start | bytes 36872 | tf_op jit(solution)/shard_map/ppermute | solution.py:530
  7.3 0.9 %collective-permute-start.5 = (bf16[48,128]{1,0:T(8,128)(2,1)S(1)}, bf16[48,128]{1,0:T(8,128)(2,1)S(1)}, u32[]{:S(2)}, u32[]{:S(2)}) collective-permute-start(bf16[48,128]{1,0:T(8,128)(2,1)S(1)} %get-tuple-element.28), channel_id=1, source_target_pairs={{0,64},{1,2},{2,1},{3,4},{4,3},{5,6},{6,5},{7,8},{8,7},{9,10},{10,... | collective-permute-start | bytes 36872 | tf_op jit(solution)/shard_map/ppermute | solution.py:530
  8.2 0.0 collective-permute-done.4.far_ref
  8.2 0.0 collective-permute-done.1.a_ref
  8.2 1.8 %columns.1 = (f32[16,128]{1,0:T(8,128)S(1)}, f32[2,11,8,256]{3,2,1,0:T(8,128)S(1)}, f32[16,128]{1,0:T(8,128)S(1)}) custom-call(bf16[512,128]{1,0:T(8,128)(2,1)S(1)} %collective-permute-done.1.a_ref, f32[320,128]{1,0:T(8,128)S(1)} %get-tuple-element.20.g_ref, f32[96,128]{1,0:T(8,128)S(1)} %get-tuple-element.21.st_ref, ...), custom_call_target="tpu_custom_call" | custom-call | tf_op jit(solution)/shard_map/columns/pallas_call | solution.py:587
  10.0 0.0 collective-permute-done.b_ref
  10.0 0.3 beyond.1
  10.2 0.5 %collective-permute-done.5.far_ref = bf16[48,128]{1,0:T(8,128)(2,1)S(1)} collective-permute-done((bf16[48,128]{1,0:T(8,128)(2,1)S(1)}, bf16[48,128]{1,0:T(8,128)(2,1)S(1)}, u32[]{:S(2)}, u32[]{:S(2)}) %collective-permute-start.5) | collective-permute-done | bytes 12320 | tf_op jit(solution)/shard_map/ppermute | solution.py:530
  10.7 0.2 corner.1
  10.9 2.0 %collective-permute-start.6 = (f32[8,128]{1,0:T(8,128)S(1)}, f32[8,128]{1,0:T(8,128)S(1)}, u32[]{:S(2)}, u32[]{:S(2)}) collective-permute-start(f32[8,128]{1,0:T(8,128)S(1)} %get-tuple-element.29), channel_id=1, source_target_pairs={{0,1},{1,0},{2,3},{3,2},{4,5},{5,4},{6,7},{7,6},{8,9},{9,8},{10,11... | collective-permute-start | bytes 12296 | tf_op jit(solution)/shard_map/ppermute | solution.py:614
  12.8 0.8 %collective-permute-done.6 = f32[8,128]{1,0:T(8,128)S(1)} collective-permute-done((f32[8,128]{1,0:T(8,128)S(1)}, f32[8,128]{1,0:T(8,128)S(1)}, u32[]{:S(2)}, u32[]{:S(2)}) %collective-permute-start.6) | collective-permute-done | bytes 4128 | tf_op jit(solution)/shard_map/ppermute | solution.py:614
  13.7 2.0 %collective-permute-start.9 = (f32[8,128]{1,0:T(8,128)S(1)}, f32[8,128]{1,0:T(8,128)S(1)}, u32[]{:S(2)}, u32[]{:S(2)}) collective-permute-start(f32[8,128]{1,0:T(8,128)S(1)} %add.12), channel_id=1, source_target_pairs={{0,5},{1,4},{2,7},{3,6},{4,1},{5,0},{6,3},{7,2},{8,13},{9,12},{10,... | collective-permute-start | bytes 12296 | tf_op jit(solution)/shard_map/ppermute | solution.py:616
  15.6 2.9 %collective-permute-start.8 = (f32[8,128]{1,0:T(8,128)S(1)}, f32[8,128]{1,0:T(8,128)S(1)}, u32[]{:S(2)}, u32[]{:S(2)}) collective-permute-start(f32[8,128]{1,0:T(8,128)S(1)} %add.12), channel_id=1, source_target_pairs={{0,7},{1,6},{2,5},{3,4},{4,3},{5,2},{6,1},{7,0},{8,15},{9,14},{10,... | collective-permute-start | bytes 12296 | tf_op jit(solution)/shard_map/ppermute | solution.py:616
  18.5 0.8 %collective-permute-start.7 = (f32[8,128]{1,0:T(8,128)S(1)}, f32[8,128]{1,0:T(8,128)S(1)}, u32[]{:S(2)}, u32[]{:S(2)}) collective-permute-start(f32[8,128]{1,0:T(8,128)S(1)} %add.12), channel_id=1, source_target_pairs={{0,3},{1,2},{2,1},{3,0},{4,7},{5,6},{6,5},{7,4},{8,11},{9,10},{10,... | collective-permute-start | bytes 12296 | tf_op jit(solution)/shard_map/ppermute | solution.py:616
  19.3 0.0 collective-permute-done.9
  19.3 0.6 %collective-permute-done.8 = f32[8,128]{1,0:T(8,128)S(1)} collective-permute-done((f32[8,128]{1,0:T(8,128)S(1)}, f32[8,128]{1,0:T(8,128)S(1)}, u32[]{:S(2)}, u32[]{:S(2)}) %collective-permute-start.8) | collective-permute-done | bytes 4128 | tf_op jit(solution)/shard_map/ppermute | solution.py:616
  19.9 1.6 %collective-permute-done.7 = f32[8,128]{1,0:T(8,128)S(1)} collective-permute-done((f32[8,128]{1,0:T(8,128)S(1)}, f32[8,128]{1,0:T(8,128)S(1)}, u32[]{:S(2)}, u32[]{:S(2)}) %collective-permute-start.7) | collective-permute-done | bytes 4128 | tf_op jit(solution)/shard_map/ppermute | solution.py:616
  21.5 1.1 %collective-permute-start.10 = (f32[8,128]{1,0:T(8,128)S(1)}, f32[8,128]{1,0:T(8,128)S(1)}, u32[]{:S(2)}, u32[]{:S(2)}) collective-permute-start(f32[8,128]{1,0:T(8,128)S(1)} %add_add_fusion), channel_id=1, source_target_pairs={{0,9},{1,8},{2,0},{3,1},{4,2},{5,3},{6,4},{7,5},{8,17},{9,16},{10,... | collective-permute-start | bytes 12296 | tf_op jit(solution)/shard_map/ppermute | solution.py:530
  22.6 2.0 %collective-permute-done.10 = f32[8,128]{1,0:T(8,128)S(1)} collective-permute-done((f32[8,128]{1,0:T(8,128)S(1)}, f32[8,128]{1,0:T(8,128)S(1)}, u32[]{:S(2)}, u32[]{:S(2)}) %collective-permute-start.10) | collective-permute-done | bytes 4128 | tf_op jit(solution)/shard_map/ppermute | solution.py:530
  24.6 2.3 %collective-permute-start.12 = (f32[16,128]{1,0:T(8,128)S(1)}, f32[16,128]{1,0:T(8,128)S(1)}, u32[]{:S(2)}, u32[]{:S(2)}) collective-permute-start(f32[16,128]{1,0:T(8,128)S(1)} %pad_maximum_fusion.own_ref), channel_id=1, source_target_pairs={{0,65},{1,64},{2,67},{3,66},{4,69},{5,68},{6,71},{7,70},{8,73},{9,... | collective-permute-start | bytes 24584 | tf_op jit(solution)/shard_map/ppermute | solution.py:530
  26.9 0.2 collective-permute-start.11
  27.0 1.2 %collective-permute-done.12.x0_ref = f32[16,128]{1,0:T(8,128)S(1)} collective-permute-done((f32[16,128]{1,0:T(8,128)S(1)}, f32[16,128]{1,0:T(8,128)S(1)}, u32[]{:S(2)}, u32[]{:S(2)}) %collective-permute-start.12) | collective-permute-done | bytes 8224 | tf_op jit(solution)/shard_map/ppermute | solution.py:530
  28.2 0.0 collective-permute-done.11.x1_ref
  28.2 1.7 %product.1 = (bf16[2400,128]{1,0:T(8,128)(2,1)}, f32[1,64]{1,0:T(1,128)}) custom-call(f32[16,128]{1,0:T(8,128)S(1)} %pad_maximum_fusion.own_ref, f32[16,128]{1,0:T(8,128)S(1)} %collective-permute-done.11.x1_ref, f32[16,128]{1,0:T(8,128)S(1)} %collective-permute-done.12.x0_ref, f32[2,11,8,256]{3,2,1,0:T(8,128)S(1)} %get-tuple-element.30.oa_ref, ...), custom_call_target="tpu_custom_call" | custom-call | tf_op jit(solution)/shard_map/product/pallas_call | solution.py:624
  (4 shorter events, 0.0 us)
Async XLA Ops:
  2.4 3.9 %collective-permute-start.3 = (f32[24,128]{1,0:T(8,128)S(1)}, f32[24,128]{1,0:T(8,128)S(1)}, u32[]{:S(2)}, u32[]{:S(2)}) collective-permute-start(f32[24,128]{1,0:T(8,128)S(1)} %get-tuple-element.22), channel_id=1, source_target_pairs={{0,64},{1,65},{2,66},{3,67},{4,68},{5,69},{6,70},{7,71},{8,72},{9,... | collective-permute-start | bytes 36872 | tf_op jit(solution)/shard_map/ppermute | solution.py:530
  3.8 2.6 %collective-permute-start.2 = (f32[24,128]{1,0:T(8,128)S(1)}, f32[24,128]{1,0:T(8,128)S(1)}, u32[]{:S(2)}, u32[]{:S(2)}) collective-permute-start(f32[24,128]{1,0:T(8,128)S(1)} %get-tuple-element.22), channel_id=1, source_target_pairs={{0,1},{1,0},{2,3},{3,2},{4,5},{5,4},{6,7},{7,6},{8,9},{9,8},{10,11... | collective-permute-start | bytes 36872 | tf_op jit(solution)/shard_map/ppermute | solution.py:530
  4.7 3.4 %collective-permute-start.1 = (bf16[512,128]{1,0:T(8,128)(2,1)S(1)}, bf16[512,128]{1,0:T(8,128)(2,1)S(1)}, u32[]{:S(2)}, u32[]{:S(2)}) collective-permute-start(bf16[512,128]{1,0:T(8,128)(2,1)S(1)} %get-tuple-element.19), channel_id=1, source_target_pairs={{0,1},{1,0},{2,3},{3,2},{4,5},{5,4},{6,7},{7,6},{8,9},{9,8},{10,11... | collective-permute-start | bytes 393224 | tf_op jit(solution)/shard_map/ppermute | solution.py:530
  4.7 5.2 %collective-permute-start = (bf16[512,128]{1,0:T(8,128)(2,1)S(1)}, bf16[512,128]{1,0:T(8,128)(2,1)S(1)}, u32[]{:S(2)}, u32[]{:S(2)}) collective-permute-start(bf16[512,128]{1,0:T(8,128)(2,1)S(1)} %get-tuple-element.19), channel_id=1, source_target_pairs={{0,64},{1,2},{2,1},{3,4},{4,3},{5,6},{6,5},{7,8},{8,7},{9,10},{10,... | collective-permute-start | bytes 393224 | tf_op jit(solution)/shard_map/ppermute | solution.py:530
  6.4 1.8 %collective-permute-start.4 = (f32[24,128]{1,0:T(8,128)S(1)}, f32[24,128]{1,0:T(8,128)S(1)}, u32[]{:S(2)}, u32[]{:S(2)}) collective-permute-start(f32[24,128]{1,0:T(8,128)S(1)} %get-tuple-element.23.side_ref), channel_id=1, source_target_pairs={{0,1},{1,0},{2,3},{3,2},{4,5},{5,4},{6,7},{7,6},{8,9},{9,8},{10,11... | collective-permute-start | bytes 36872 | tf_op jit(solution)/shard_map/ppermute | solution.py:530
  7.3 3.4 %collective-permute-start.5 = (bf16[48,128]{1,0:T(8,128)(2,1)S(1)}, bf16[48,128]{1,0:T(8,128)(2,1)S(1)}, u32[]{:S(2)}, u32[]{:S(2)}) collective-permute-start(bf16[48,128]{1,0:T(8,128)(2,1)S(1)} %get-tuple-element.28), channel_id=1, source_target_pairs={{0,64},{1,2},{2,1},{3,4},{4,3},{5,6},{6,5},{7,8},{8,7},{9,10},{10,... | collective-permute-start | bytes 36872 | tf_op jit(solution)/shard_map/ppermute | solution.py:530
  10.9 2.8 %collective-permute-start.6 = (f32[8,128]{1,0:T(8,128)S(1)}, f32[8,128]{1,0:T(8,128)S(1)}, u32[]{:S(2)}, u32[]{:S(2)}) collective-permute-start(f32[8,128]{1,0:T(8,128)S(1)} %get-tuple-element.29), channel_id=1, source_target_pairs={{0,1},{1,0},{2,3},{3,2},{4,5},{5,4},{6,7},{7,6},{8,9},{9,8},{10,11... | collective-permute-start | bytes 12296 | tf_op jit(solution)/shard_map/ppermute | solution.py:614
  13.7 5.6 %collective-permute-start.9 = (f32[8,128]{1,0:T(8,128)S(1)}, f32[8,128]{1,0:T(8,128)S(1)}, u32[]{:S(2)}, u32[]{:S(2)}) collective-permute-start(f32[8,128]{1,0:T(8,128)S(1)} %add.12), channel_id=1, source_target_pairs={{0,5},{1,4},{2,7},{3,6},{4,1},{5,0},{6,3},{7,2},{8,13},{9,12},{10,... | collective-permute-start | bytes 12296 | tf_op jit(solution)/shard_map/ppermute | solution.py:616
  15.6 4.2 %collective-permute-start.8 = (f32[8,128]{1,0:T(8,128)S(1)}, f32[8,128]{1,0:T(8,128)S(1)}, u32[]{:S(2)}, u32[]{:S(2)}) collective-permute-start(f32[8,128]{1,0:T(8,128)S(1)} %add.12), channel_id=1, source_target_pairs={{0,7},{1,6},{2,5},{3,4},{4,3},{5,2},{6,1},{7,0},{8,15},{9,14},{10,... | collective-permute-start | bytes 12296 | tf_op jit(solution)/shard_map/ppermute | solution.py:616
  18.5 3.0 %collective-permute-start.7 = (f32[8,128]{1,0:T(8,128)S(1)}, f32[8,128]{1,0:T(8,128)S(1)}, u32[]{:S(2)}, u32[]{:S(2)}) collective-permute-start(f32[8,128]{1,0:T(8,128)S(1)} %add.12), channel_id=1, source_target_pairs={{0,3},{1,2},{2,1},{3,0},{4,7},{5,6},{6,5},{7,4},{8,11},{9,10},{10,... | collective-permute-start | bytes 12296 | tf_op jit(solution)/shard_map/ppermute | solution.py:616
  21.5 3.0 %collective-permute-start.10 = (f32[8,128]{1,0:T(8,128)S(1)}, f32[8,128]{1,0:T(8,128)S(1)}, u32[]{:S(2)}, u32[]{:S(2)}) collective-permute-start(f32[8,128]{1,0:T(8,128)S(1)} %add_add_fusion), channel_id=1, source_target_pairs={{0,9},{1,8},{2,0},{3,1},{4,2},{5,3},{6,4},{7,5},{8,17},{9,16},{10,... | collective-permute-start | bytes 12296 | tf_op jit(solution)/shard_map/ppermute | solution.py:530
  24.6 3.6 %collective-permute-start.12 = (f32[16,128]{1,0:T(8,128)S(1)}, f32[16,128]{1,0:T(8,128)S(1)}, u32[]{:S(2)}, u32[]{:S(2)}) collective-permute-start(f32[16,128]{1,0:T(8,128)S(1)} %pad_maximum_fusion.own_ref), channel_id=1, source_target_pairs={{0,65},{1,64},{2,67},{3,66},{4,69},{5,68},{6,71},{7,70},{8,73},{9,... | collective-permute-start | bytes 24584 | tf_op jit(solution)/shard_map/ppermute | solution.py:530
  26.9 1.3 %collective-permute-start.11 = (f32[16,128]{1,0:T(8,128)S(1)}, f32[16,128]{1,0:T(8,128)S(1)}, u32[]{:S(2)}, u32[]{:S(2)}) collective-permute-start(f32[16,128]{1,0:T(8,128)S(1)} %pad_maximum_fusion.own_ref), channel_id=1, source_target_pairs={{0,1},{1,0},{2,3},{3,2},{4,5},{5,4},{6,7},{7,6},{8,9},{9,8},{10,11... | collective-permute-start | bytes 24584 | tf_op jit(solution)/shard_map/ppermute | solution.py:530

commit v5 on v4

--- a/solution.py
+++ b/solution.py
@@ -9,7 +9,6 @@
 
 KD = 0.2
 UNROLL = 10
-TURNS = (1, 3, 2)
 ALL = ("gx", "gy", "swath")
 LANES = 128
 NM = 4
@@ -17,7 +16,6 @@
 BF = jnp.bfloat16
 F32 = jnp.float32
 VMEM = pl.BlockSpec(memory_space=pltpu.VMEM)
-ANY = pl.BlockSpec(memory_space=pl.ANY)
 HBM = pl.BlockSpec(memory_space=pltpu.HBM)
 
 
@@ -253,12 +251,12 @@
     even = jnp.where(odd, 0, 1)
     has_b = jnp.logical_and(t > 0, t < z.nt - 1)
     sg = jnp.where(odd, -0.5, 0.5)
+    stat_b = b_ref[z.o_st : z.o_st + z.st16, :].astype(F32) + b_ref[
+        z.o_st + z.st16 : z.msg, :
+    ].astype(F32)
+    stat_b = jnp.where(has_b, stat_b, 0.0)
     for l in range(z.levels + 1):
-        high = z.o_st + 8 * l
-        both = b_ref[high : high + 8, :].astype(F32) + b_ref[
-            high + z.st16 : high + z.st16 + 8, :
-        ].astype(F32)
-        stat_ref[l] = jnp.where(has_b, both, 0.0)
+        stat_ref[l] = stat_b[8 * l : 8 * l + 8]
     k_of = iota((NK, LANES), 0)
     lane = iota((NK, LANES), 1)
     lane8 = iota((8, LANES), 1)

time: 30.5 us -> 30.5 us (level)
  no operation moved by 1% of the time
where the time goes in v5:
time: 30.5 us; the launch traced here: 29.9 us
  starting transfers between devices  16.8 us (55%)
  waiting for transfers between devices  6.66 us (22%)
  Pallas kernels  5.74 us (19%)
  between operations  0.68 us (2%)
    ppermute x9, starting transfers between devices, move(): return lax.ppermute(v, ALL, perm)  9.24 us
    ppermute x3, starting transfers between devices, per_device(): lax.ppermute(part, 'swath', [(i, i ^ 2 * k ^ 1) for i in range(nsw)])  5.63 us
    ppermute x9, waiting for transfers between devices, move(): return lax.ppermute(v, ALL, perm)  3.61 us
    ppermute x3, waiting for transfers between devices, per_device(): lax.ppermute(part, 'swath', [(i, i ^ 2 * k ^ 1) for i in range(nsw)])  2.23 us
    ppermute x1, starting transfers between devices, per_device(): part = part + lax.ppermute(part, 'swath', [(i, i ^ 1) for i in range(nsw)])  1.97 us
    pallas_call x1, Pallas kernels, per_device(): pl.pallas_call(functools.partial(columns_kernel, z), out_shape=(shape(16,...  1.79 us
    pallas_call x1, Pallas kernels, per_device(): pl.pallas_call(functools.partial(project_kernel, z), out_shape=(shape(z.o...  1.76 us
    pallas_call x1, Pallas kernels, per_device(): pl.pallas_call(functools.partial(product_kernel, z), out_shape=(shape(*ce...  1.74 us
  transfers between devices with their start and end apart: 13, of which 6 were waited for; matrix products, arithmetic and copies ran while one was open for 0% of the time, Pallas kernels for 7%

profile of v5, /device:TPU:97, one launch (start us, length us, event | category | flops | bytes accessed | tf_op | source)
XLA Modules:
  0.0 29.9 jit_solution(8857401025215728067)
XLA Ops:
  0.6 1.8 %project.1 = (f32[320,128]{1,0:T(8,128)S(1)}, bf16[512,128]{1,0:T(8,128)(2,1)S(1)}, f32[24,128]{1,0:T(8,128)S(1)}, f32[96,128]{1,0:T(8,128)S(1)}, bf16[48,120]{1,0:T(8,128)(2,1)S(1)}) custom-call(bf16[2400,128]{1,0:T(8,128)(2,1)} %bitcast.5, bf16[4,120,120]{2,1,0:T(8,128)(2,1)} %prop_hbm.1, f32[10,2,128]{2,1,0:T(2,128)} %cx_hbm.1, f32[10,2,128]{2,1,0:T(2,128)} %cy_hbm.1, ...), custom_call_target="tpu_custom_call" | custom-call | tf_op jit(solution)/shard_map/project/pallas_call | solution.py:532
  2.4 1.4 %collective-permute-start.3 = (f32[24,128]{1,0:T(8,128)S(1)}, f32[24,128]{1,0:T(8,128)S(1)}, u32[]{:S(2)}, u32[]{:S(2)}) collective-permute-start(f32[24,128]{1,0:T(8,128)S(1)} %get-tuple-element.22), channel_id=1, source_target_pairs={{0,64},{1,65},{2,66},{3,67},{4,68},{5,69},{6,70},{7,71},{8,72},{9,... | collective-permute-start | bytes 36872 | tf_op jit(solution)/shard_map/ppermute | solution.py:528
  3.8 1.0 %collective-permute-start.2 = (f32[24,128]{1,0:T(8,128)S(1)}, f32[24,128]{1,0:T(8,128)S(1)}, u32[]{:S(2)}, u32[]{:S(2)}) collective-permute-start(f32[24,128]{1,0:T(8,128)S(1)} %get-tuple-element.22), channel_id=1, source_target_pairs={{0,1},{1,0},{2,3},{3,2},{4,5},{5,4},{6,7},{7,6},{8,9},{9,8},{10,11... | collective-permute-start | bytes 36872 | tf_op jit(solution)/shard_map/ppermute | solution.py:528
  4.7 0.0 collective-permute-start.1
  4.7 1.6 %collective-permute-start = (bf16[512,128]{1,0:T(8,128)(2,1)S(1)}, bf16[512,128]{1,0:T(8,128)(2,1)S(1)}, u32[]{:S(2)}, u32[]{:S(2)}) collective-permute-start(bf16[512,128]{1,0:T(8,128)(2,1)S(1)} %get-tuple-element.19), channel_id=1, source_target_pairs={{0,64},{1,2},{2,1},{3,4},{4,3},{5,6},{6,5},{7,8},{8,7},{9,10},{10,... | collective-permute-start | bytes 393224 | tf_op jit(solution)/shard_map/ppermute | solution.py:528
  6.3 0.0 collective-permute-done.3.x0_ref
  6.4 0.0 collective-permute-done.2.x1_ref
  6.4 0.9 %collective-permute-start.4 = (f32[24,128]{1,0:T(8,128)S(1)}, f32[24,128]{1,0:T(8,128)S(1)}, u32[]{:S(2)}, u32[]{:S(2)}) collective-permute-start(f32[24,128]{1,0:T(8,128)S(1)} %get-tuple-element.23.side_ref), channel_id=1, source_target_pairs={{0,1},{1,0},{2,3},{3,2},{4,5},{5,4},{6,7},{7,6},{8,9},{9,8},{10,11... | collective-permute-start | bytes 36872 | tf_op jit(solution)/shard_map/ppermute | solution.py:528
  7.3 0.9 %collective-permute-start.5 = (bf16[48,128]{1,0:T(8,128)(2,1)S(1)}, bf16[48,128]{1,0:T(8,128)(2,1)S(1)}, u32[]{:S(2)}, u32[]{:S(2)}) collective-permute-start(bf16[48,128]{1,0:T(8,128)(2,1)S(1)} %get-tuple-element.28), channel_id=1, source_target_pairs={{0,64},{1,2},{2,1},{3,4},{4,3},{5,6},{6,5},{7,8},{8,7},{9,10},{10,... | collective-permute-start | bytes 36872 | tf_op jit(solution)/shard_map/ppermute | solution.py:528
  8.2 0.0 collective-permute-done.4.far_ref
  8.2 0.0 collective-permute-done.1.a_ref
  8.2 1.8 %columns.1 = (f32[16,128]{1,0:T(8,128)S(1)}, f32[2,11,8,256]{3,2,1,0:T(8,128)S(1)}, f32[16,128]{1,0:T(8,128)S(1)}) custom-call(bf16[512,128]{1,0:T(8,128)(2,1)S(1)} %collective-permute-done.1.a_ref, f32[320,128]{1,0:T(8,128)S(1)} %get-tuple-element.20.g_ref, f32[96,128]{1,0:T(8,128)S(1)} %get-tuple-element.21.st_ref, ...), custom_call_target="tpu_custom_call" | custom-call | tf_op jit(solution)/shard_map/columns/pallas_call | solution.py:585
  10.0 0.0 collective-permute-done.b_ref
  10.0 0.3 beyond.1
  10.2 0.5 %collective-permute-done.5.far_ref = bf16[48,128]{1,0:T(8,128)(2,1)S(1)} collective-permute-done((bf16[48,128]{1,0:T(8,128)(2,1)S(1)}, bf16[48,128]{1,0:T(8,128)(2,1)S(1)}, u32[]{:S(2)}, u32[]{:S(2)}) %collective-permute-start.5) | collective-permute-done | bytes 12320 | tf_op jit(solution)/shard_map/ppermute | solution.py:528
  10.7 0.2 corner.1
  10.9 2.0 %collective-permute-start.6 = (f32[8,128]{1,0:T(8,128)S(1)}, f32[8,128]{1,0:T(8,128)S(1)}, u32[]{:S(2)}, u32[]{:S(2)}) collective-permute-start(f32[8,128]{1,0:T(8,128)S(1)} %get-tuple-element.29), channel_id=1, source_target_pairs={{0,1},{1,0},{2,3},{3,2},{4,5},{5,4},{6,7},{7,6},{8,9},{9,8},{10,11... | collective-permute-start | bytes 12296 | tf_op jit(solution)/shard_map/ppermute | solution.py:612
  12.8 0.8 %collective-permute-done.6 = f32[8,128]{1,0:T(8,128)S(1)} collective-permute-done((f32[8,128]{1,0:T(8,128)S(1)}, f32[8,128]{1,0:T(8,128)S(1)}, u32[]{:S(2)}, u32[]{:S(2)}) %collective-permute-start.6) | collective-permute-done | bytes 4128 | tf_op jit(solution)/shard_map/ppermute | solution.py:612
  13.7 2.0 %collective-permute-start.9 = (f32[8,128]{1,0:T(8,128)S(1)}, f32[8,128]{1,0:T(8,128)S(1)}, u32[]{:S(2)}, u32[]{:S(2)}) collective-permute-start(f32[8,128]{1,0:T(8,128)S(1)} %add.12), channel_id=1, source_target_pairs={{0,5},{1,4},{2,7},{3,6},{4,1},{5,0},{6,3},{7,2},{8,13},{9,12},{10,... | collective-permute-start | bytes 12296 | tf_op jit(solution)/shard_map/ppermute | solution.py:614
  15.6 2.9 %collective-permute-start.8 = (f32[8,128]{1,0:T(8,128)S(1)}, f32[8,128]{1,0:T(8,128)S(1)}, u32[]{:S(2)}, u32[]{:S(2)}) collective-permute-start(f32[8,128]{1,0:T(8,128)S(1)} %add.12), channel_id=1, source_target_pairs={{0,7},{1,6},{2,5},{3,4},{4,3},{5,2},{6,1},{7,0},{8,15},{9,14},{10,... | collective-permute-start | bytes 12296 | tf_op jit(solution)/shard_map/ppermute | solution.py:614
  18.5 0.8 %collective-permute-start.7 = (f32[8,128]{1,0:T(8,128)S(1)}, f32[8,128]{1,0:T(8,128)S(1)}, u32[]{:S(2)}, u32[]{:S(2)}) collective-permute-start(f32[8,128]{1,0:T(8,128)S(1)} %add.12), channel_id=1, source_target_pairs={{0,3},{1,2},{2,1},{3,0},{4,7},{5,6},{6,5},{7,4},{8,11},{9,10},{10,... | collective-permute-start | bytes 12296 | tf_op jit(solution)/shard_map/ppermute | solution.py:614
  19.3 0.0 collective-permute-done.9
  19.3 0.6 %collective-permute-done.8 = f32[8,128]{1,0:T(8,128)S(1)} collective-permute-done((f32[8,128]{1,0:T(8,128)S(1)}, f32[8,128]{1,0:T(8,128)S(1)}, u32[]{:S(2)}, u32[]{:S(2)}) %collective-permute-start.8) | collective-permute-done | bytes 4128 | tf_op jit(solution)/shard_map/ppermute | solution.py:614
  19.9 1.6 %collective-permute-done.7 = f32[8,128]{1,0:T(8,128)S(1)} collective-permute-done((f32[8,128]{1,0:T(8,128)S(1)}, f32[8,128]{1,0:T(8,128)S(1)}, u32[]{:S(2)}, u32[]{:S(2)}) %collective-permute-start.7) | collective-permute-done | bytes 4128 | tf_op jit(solution)/shard_map/ppermute | solution.py:614
  21.5 1.1 %collective-permute-start.10 = (f32[8,128]{1,0:T(8,128)S(1)}, f32[8,128]{1,0:T(8,128)S(1)}, u32[]{:S(2)}, u32[]{:S(2)}) collective-permute-start(f32[8,128]{1,0:T(8,128)S(1)} %add_add_fusion), channel_id=1, source_target_pairs={{0,9},{1,8},{2,0},{3,1},{4,2},{5,3},{6,4},{7,5},{8,17},{9,16},{10,... | collective-permute-start | bytes 12296 | tf_op jit(solution)/shard_map/ppermute | solution.py:528
  22.6 2.0 %collective-permute-done.10 = f32[8,128]{1,0:T(8,128)S(1)} collective-permute-done((f32[8,128]{1,0:T(8,128)S(1)}, f32[8,128]{1,0:T(8,128)S(1)}, u32[]{:S(2)}, u32[]{:S(2)}) %collective-permute-start.10) | collective-permute-done | bytes 4128 | tf_op jit(solution)/shard_map/ppermute | solution.py:528
  24.6 2.3 %collective-permute-start.12 = (f32[16,128]{1,0:T(8,128)S(1)}, f32[16,128]{1,0:T(8,128)S(1)}, u32[]{:S(2)}, u32[]{:S(2)}) collective-permute-start(f32[16,128]{1,0:T(8,128)S(1)} %pad_maximum_fusion.own_ref), channel_id=1, source_target_pairs={{0,65},{1,64},{2,67},{3,66},{4,69},{5,68},{6,71},{7,70},{8,73},{9,... | collective-permute-start | bytes 24584 | tf_op jit(solution)/shard_map/ppermute | solution.py:528
  26.9 0.2 collective-permute-start.11
  27.0 1.2 %collective-permute-done.12.x0_ref = f32[16,128]{1,0:T(8,128)S(1)} collective-permute-done((f32[16,128]{1,0:T(8,128)S(1)}, f32[16,128]{1,0:T(8,128)S(1)}, u32[]{:S(2)}, u32[]{:S(2)}) %collective-permute-start.12) | collective-permute-done | bytes 8224 | tf_op jit(solution)/shard_map/ppermute | solution.py:528
  28.2 0.0 collective-permute-done.11.x1_ref
  28.2 1.7 %product.1 = (bf16[2400,128]{1,0:T(8,128)(2,1)}, f32[1,64]{1,0:T(1,128)}) custom-call(f32[16,128]{1,0:T(8,128)S(1)} %pad_maximum_fusion.own_ref, f32[16,128]{1,0:T(8,128)S(1)} %collective-permute-done.11.x1_ref, f32[16,128]{1,0:T(8,128)S(1)} %collective-permute-done.12.x0_ref, f32[2,11,8,256]{3,2,1,0:T(8,128)S(1)} %get-tuple-element.30.oa_ref, ...), custom_call_target="tpu_custom_call" | custom-call | tf_op jit(solution)/shard_map/product/pallas_call | solution.py:622
  (4 shorter events, 0.0 us)
Async XLA Ops:
  2.4 3.9 %collective-permute-start.3 = (f32[24,128]{1,0:T(8,128)S(1)}, f32[24,128]{1,0:T(8,128)S(1)}, u32[]{:S(2)}, u32[]{:S(2)}) collective-permute-start(f32[24,128]{1,0:T(8,128)S(1)} %get-tuple-element.22), channel_id=1, source_target_pairs={{0,64},{1,65},{2,66},{3,67},{4,68},{5,69},{6,70},{7,71},{8,72},{9,... | collective-permute-start | bytes 36872 | tf_op jit(solution)/shard_map/ppermute | solution.py:528
  3.8 2.6 %collective-permute-start.2 = (f32[24,128]{1,0:T(8,128)S(1)}, f32[24,128]{1,0:T(8,128)S(1)}, u32[]{:S(2)}, u32[]{:S(2)}) collective-permute-start(f32[24,128]{1,0:T(8,128)S(1)} %get-tuple-element.22), channel_id=1, source_target_pairs={{0,1},{1,0},{2,3},{3,2},{4,5},{5,4},{6,7},{7,6},{8,9},{9,8},{10,11... | collective-permute-start | bytes 36872 | tf_op jit(solution)/shard_map/ppermute | solution.py:528
  4.7 3.4 %collective-permute-start.1 = (bf16[512,128]{1,0:T(8,128)(2,1)S(1)}, bf16[512,128]{1,0:T(8,128)(2,1)S(1)}, u32[]{:S(2)}, u32[]{:S(2)}) collective-permute-start(bf16[512,128]{1,0:T(8,128)(2,1)S(1)} %get-tuple-element.19), channel_id=1, source_target_pairs={{0,1},{1,0},{2,3},{3,2},{4,5},{5,4},{6,7},{7,6},{8,9},{9,8},{10,11... | collective-permute-start | bytes 393224 | tf_op jit(solution)/shard_map/ppermute | solution.py:528
  4.7 5.2 %collective-permute-start = (bf16[512,128]{1,0:T(8,128)(2,1)S(1)}, bf16[512,128]{1,0:T(8,128)(2,1)S(1)}, u32[]{:S(2)}, u32[]{:S(2)}) collective-permute-start(bf16[512,128]{1,0:T(8,128)(2,1)S(1)} %get-tuple-element.19), channel_id=1, source_target_pairs={{0,64},{1,2},{2,1},{3,4},{4,3},{5,6},{6,5},{7,8},{8,7},{9,10},{10,... | collective-permute-start | bytes 393224 | tf_op jit(solution)/shard_map/ppermute | solution.py:528
  6.4 1.8 %collective-permute-start.4 = (f32[24,128]{1,0:T(8,128)S(1)}, f32[24,128]{1,0:T(8,128)S(1)}, u32[]{:S(2)}, u32[]{:S(2)}) collective-permute-start(f32[24,128]{1,0:T(8,128)S(1)} %get-tuple-element.23.side_ref), channel_id=1, source_target_pairs={{0,1},{1,0},{2,3},{3,2},{4,5},{5,4},{6,7},{7,6},{8,9},{9,8},{10,11... | collective-permute-start | bytes 36872 | tf_op jit(solution)/shard_map/ppermute | solution.py:528
  7.3 3.4 %collective-permute-start.5 = (bf16[48,128]{1,0:T(8,128)(2,1)S(1)}, bf16[48,128]{1,0:T(8,128)(2,1)S(1)}, u32[]{:S(2)}, u32[]{:S(2)}) collective-permute-start(bf16[48,128]{1,0:T(8,128)(2,1)S(1)} %get-tuple-element.28), channel_id=1, source_target_pairs={{0,64},{1,2},{2,1},{3,4},{4,3},{5,6},{6,5},{7,8},{8,7},{9,10},{10,... | collective-permute-start | bytes 36872 | tf_op jit(solution)/shard_map/ppermute | solution.py:528
  10.9 2.8 %collective-permute-start.6 = (f32[8,128]{1,0:T(8,128)S(1)}, f32[8,128]{1,0:T(8,128)S(1)}, u32[]{:S(2)}, u32[]{:S(2)}) collective-permute-start(f32[8,128]{1,0:T(8,128)S(1)} %get-tuple-element.29), channel_id=1, source_target_pairs={{0,1},{1,0},{2,3},{3,2},{4,5},{5,4},{6,7},{7,6},{8,9},{9,8},{10,11... | collective-permute-start | bytes 12296 | tf_op jit(solution)/shard_map/ppermute | solution.py:612
  13.7 5.6 %collective-permute-start.9 = (f32[8,128]{1,0:T(8,128)S(1)}, f32[8,128]{1,0:T(8,128)S(1)}, u32[]{:S(2)}, u32[]{:S(2)}) collective-permute-start(f32[8,128]{1,0:T(8,128)S(1)} %add.12), channel_id=1, source_target_pairs={{0,5},{1,4},{2,7},{3,6},{4,1},{5,0},{6,3},{7,2},{8,13},{9,12},{10,... | collective-permute-start | bytes 12296 | tf_op jit(solution)/shard_map/ppermute | solution.py:614
  15.6 4.2 %collective-permute-start.8 = (f32[8,128]{1,0:T(8,128)S(1)}, f32[8,128]{1,0:T(8,128)S(1)}, u32[]{:S(2)}, u32[]{:S(2)}) collective-permute-start(f32[8,128]{1,0:T(8,128)S(1)} %add.12), channel_id=1, source_target_pairs={{0,7},{1,6},{2,5},{3,4},{4,3},{5,2},{6,1},{7,0},{8,15},{9,14},{10,... | collective-permute-start | bytes 12296 | tf_op jit(solution)/shard_map/ppermute | solution.py:614
  18.5 3.0 %collective-permute-start.7 = (f32[8,128]{1,0:T(8,128)S(1)}, f32[8,128]{1,0:T(8,128)S(1)}, u32[]{:S(2)}, u32[]{:S(2)}) collective-permute-start(f32[8,128]{1,0:T(8,128)S(1)} %add.12), channel_id=1, source_target_pairs={{0,3},{1,2},{2,1},{3,0},{4,7},{5,6},{6,5},{7,4},{8,11},{9,10},{10,... | collective-permute-start | bytes 12296 | tf_op jit(solution)/shard_map/ppermute | solution.py:614
  21.5 3.0 %collective-permute-start.10 = (f32[8,128]{1,0:T(8,128)S(1)}, f32[8,128]{1,0:T(8,128)S(1)}, u32[]{:S(2)}, u32[]{:S(2)}) collective-permute-start(f32[8,128]{1,0:T(8,128)S(1)} %add_add_fusion), channel_id=1, source_target_pairs={{0,9},{1,8},{2,0},{3,1},{4,2},{5,3},{6,4},{7,5},{8,17},{9,16},{10,... | collective-permute-start | bytes 12296 | tf_op jit(solution)/shard_map/ppermute | solution.py:528
  24.6 3.6 %collective-permute-start.12 = (f32[16,128]{1,0:T(8,128)S(1)}, f32[16,128]{1,0:T(8,128)S(1)}, u32[]{:S(2)}, u32[]{:S(2)}) collective-permute-start(f32[16,128]{1,0:T(8,128)S(1)} %pad_maximum_fusion.own_ref), channel_id=1, source_target_pairs={{0,65},{1,64},{2,67},{3,66},{4,69},{5,68},{6,71},{7,70},{8,73},{9,... | collective-permute-start | bytes 24584 | tf_op jit(solution)/shard_map/ppermute | solution.py:528
  26.9 1.3 %collective-permute-start.11 = (f32[16,128]{1,0:T(8,128)S(1)}, f32[16,128]{1,0:T(8,128)S(1)}, u32[]{:S(2)}, u32[]{:S(2)}) collective-permute-start(f32[16,128]{1,0:T(8,128)S(1)} %pad_maximum_fusion.own_ref), channel_id=1, source_target_pairs={{0,1},{1,0},{2,3},{3,2},{4,5},{5,4},{6,7},{7,6},{8,9},{9,8},{10,11... | collective-permute-start | bytes 24584 | tf_op jit(solution)/shard_map/ppermute | solution.py:528

commit v6 on v5

--- a/solution.py
+++ b/solution.py
@@ -45,6 +45,7 @@
         self.o_st = self.rows * NK
         self.msg = self.o_st + 2 * self.st16
         self.edge = NK + 8
+        self.halves = -(-levels // PER)
         self.far = NK + 2 * 16
 
     def place(self):
@@ -351,10 +352,61 @@
     out_ref[...] = total
 
 
-def product_kernel(
-    z, own_ref, x1_ref, x0_ref, oa_ref, stat_ref, block_ref, d_ref, out_ref, dep_ref, v3, tall
-):
-    gx, swath, t = z.place()
+def weigh(v):
+    return v * lane_roll(v, LANES // 2)
+
+
+def outer_rows(z, swath):
+    sub = iota((8, LANES), 0)
+    return ((sub < 2) & (swath == 0)) | ((sub >= 4) & (swath == z.nsw - 1))
+
+
+def find(z, outer, dep, owner, index):
+    table = jnp.zeros((8, LANES), F32)
+    for o in range(z.nsw):
+        row = jnp.where(outer, dep[8 + o : 9 + o, :], dep[o : o + 1, :])
+        table = jnp.where(owner == float(o), row, table)
+    return jnp.take_along_axis(table, index, axis=1)
+
+
+PLACE = [(s, y) for s in range(3) for y in range(2)]
+
+
+def twice_back(miscs, back, stats):
+    W = back.shape[1]
+    m_of = iota((8, W), 0) % NM
+    k_of = iota((NK, W), 0) // NM
+    mech = [miscs[s][y : y + 1] for s, y in PLACE]
+    cx = [0.5 * stats[s][y : y + 1] for s, y in PLACE]
+    cy = [0.5 * stats[s][2 + y : 3 + y] for s, y in PLACE]
+    kern = [stats[s][4 + y : 5 + y] for s, y in PLACE]
+
+    def unadvect(v, i, at):
+        return (
+            (1.0 - 4.0 * KD) * v[at]
+            + pltpu.roll((KD - cx[i]) * v[at], 1, 1)
+            + pltpu.roll((KD + cx[i]) * v[at], W - 1, 1)
+            + (KD - cy[i - 1]) * v[at - 1]
+            + (KD + cy[i + 1]) * v[at + 1]
+        )
+
+    w = [
+        kern[i] * jnp.where(mech[i] == (m_of + 1).astype(F32), back[i : i + 1, :], 0.0)
+        for i in range(6)
+    ]
+    u = []
+    for i in range(1, 5):
+        mid = unadvect(w, i, i)
+        both = jnp.concatenate([mid, mid], axis=0)
+        u.append(jnp.where(mech[i] == (k_of + 1).astype(F32), both, 0.0))
+    return [unadvect(u, 2 + y, 1 + y) for y in range(2)]
+
+
+PER = 5
+
+
+def tiles_of(z, oa_ref, stat_ref, block_ref):
+    _, _, t = z.place()
     odd = t % 2 == 1
 
     def tiles(l):
@@ -362,90 +414,126 @@
         b = jnp.concatenate([stat_ref[l], block_ref[l]], axis=1)
         return jnp.where(odd, a, b), oa_ref[0, l], jnp.where(odd, b, a)
 
+    return tiles
+
+
+def stack(miscs, f):
+    out = jnp.zeros((8, 2 * LANES), F32)
+    for s, y in PLACE:
+        row = miscs[s][2 * f + y : 2 * f + y + 1]
+        out = jnp.where(iota(out.shape, 0) == 2 * s + y, row, out)
+    return out
+
+
+def coefs_kernel(z, oa_ref, stat_ref, block_ref, coef_ref, far_ref):
+    tiles = tiles_of(z, oa_ref, stat_ref, block_ref)
     miscs = tiles(z.levels)
-    W = 2 * LANES
-    pixels = LANES // 2
+    for n, f in enumerate((3, 1, 2)):
+        far_ref[8 * n : 8 * n + 8, :] = stack(miscs, f)[:, LANES:]
+    sub = iota((8, LANES), 0)
+    lane = iota((8, LANES), 1)
+
+    def pack(block, g, old):
+        b = 16 * g
+        rel = lane - b
+        own, side = block[:, 0:LANES], block[:, LANES:]
+        out = old
+        for lo, v, shift in ((0, own, 4), (4, side, 4), (8, side, 12), (12, own, 12)):
+            out = jnp.where((rel >= lo) & (rel < lo + 4), lane_roll(v, b + shift), out)
+        return out
+
+    misc_seams = []
+    for s in range(3):
+        all_levels = jnp.zeros((8, LANES), F32)
+        for g in range(PER):
+            all_levels = pack(miscs[s], g, all_levels)
+        misc_seams.append(all_levels)
+    rel = lane % 16
+    nearer = (rel == 4) | (rel == 11)
+    farther = (rel == 5) | (rel == 10)
+    for h in range(z.halves):
+        packed = [jnp.zeros((8, LANES), F32)] * 3
+        for g in range(min(PER, z.levels - PER * h)):
+            blocks = tiles(PER * h + g)
+            packed = [pack(blocks[s], g, packed[s]) for s in range(3)]
+
+        def respond(columns, i, packed=packed):
+            one = jnp.where(columns & (sub == i), 1.0, 0.0)
+            return twice_back(misc_seams, one, packed)
+
+        beside = {i: respond(nearer, i) for i in range(1, 5)}
+        beyond = {i: respond(farther, i) for i in (2, 3)}
+        for y in range(2):
+            for c, v in enumerate(
+                (beside[2 + y][y], beyond[2 + y][y], beside[1 + y][y], beside[3 + y][y])
+            ):
+                coef_ref[h, y, c] = v
+
+
+def prepare_kernel(z, own_ref, oa_ref, stat_ref, block_ref, v_ref, dep_ref):
+    _, swath, _ = z.place()
+    tiles = tiles_of(z, oa_ref, stat_ref, block_ref)
+    miscs = tiles(z.levels)
+    dep = weigh(own_ref[...])
+    sub = iota((8, LANES), 0)
+    dep_ref[...] = jnp.sum(jnp.where(sub == swath, dep[0:8], 0.0), axis=0, keepdims=True)[
+        :, 0 : LANES // 2
+    ]
+    owner, index, weight = (stack(miscs, f)[:, 0:LANES] for f in (3, 1, 2))
+    near = find(z, outer_rows(z, swath), dep, owner, index.astype(jnp.int32))
+    back = jnp.concatenate([weight * near, jnp.zeros((8, LANES), F32)], axis=1)
+
+    def level(l, carry):
+        out = twice_back(miscs, back, tiles(l))
+        for y in range(2):
+            at = pl.ds(pl.multiple_of((2 * l + y) * LANES, LANES), LANES)
+            v_ref[:, at] = out[y][:, 0:LANES]
+        return carry
+
+    lax.fori_loop(0, z.levels, level, 0, unroll=UNROLL)
+
+
+def join_kernel(part_ref, next_ref, far_ref, out_ref):
+    out_ref[0:8, :] = part_ref[...]
+    out_ref[8:16, :] = next_ref[...]
+
+
+def product_kernel(
+    z, x1_ref, x0_ref, v_ref, coef_ref, far_ref, d_ref, out_ref, v3, tall
+):
+    gx, swath, _ = z.place()
     left, right = sides_of(z, gx, x0_ref[...], x1_ref[...])
-
-    def weigh(v):
-        return v * lane_roll(v, pixels)
-
-    deps = [weigh(v) for v in (own_ref[...], left, right)]
-    sub = iota((8, LANES), 0)
-    dep_ref[...] = jnp.sum(jnp.where(sub == swath, deps[0][0:8], 0.0), axis=0, keepdims=True)[
-        :, 0:pixels
-    ]
-    outer = ((sub < 2) & (swath == 0)) | ((sub >= 4) & (swath == z.nsw - 1))
-
-    def stack(f):
-        out = jnp.zeros((8, W), F32)
-        for s in range(3):
+    outer = outer_rows(z, swath)
+    owner, index = far_ref[0:8, :], far_ref[8:16, :].astype(jnp.int32)
+    lane = iota((8, LANES), 1)
+    beside = far_ref[16:24, :] * jnp.where(
+        lane < 2,
+        find(z, outer, weigh(right), owner[:, 0:1], index),
+        find(z, outer, weigh(left), owner[:, LANES - 1 :], index),
+    )
+    on_left = lane % 16 >= 8
+    near = jnp.where(on_left, beside[:, LANES - 1 :], beside[:, 0:1])
+    away = jnp.where(on_left, beside[:, LANES - 2 : LANES - 1], beside[:, 1:2])
+    wide = iota((NK, LANES), 1)
+    for h in range(z.halves):
+        seams = []
+        for y in range(2):
+            a, b, c, e = (coef_ref[h, y, i] for i in range(4))
+            seams.append(
+                (a * near[2 + y : 3 + y] + b * away[2 + y : 3 + y])
+                + (c * near[1 + y : 2 + y] + e * near[3 + y : 4 + y])
+            )
+        for g in range(min(PER, z.levels - PER * h)):
             for y in range(2):
-                row = miscs[s][2 * f + y : 2 * f + y + 1]
-                out = jnp.where(iota((8, W), 0) == 2 * s + y, row, out)
-        return out
-
-    owner = stack(3)
-    index = stack(1).astype(jnp.int32)
-    weight = stack(2)
-
-    def find(dep, owner, index):
-        found = jnp.zeros((8, LANES), F32)
-        for o in range(z.nsw):
-            row = jnp.where(outer, dep[8 + o : 9 + o, :], dep[o : o + 1, :])
-            value = jnp.take_along_axis(row, index, axis=1)
-            found = jnp.where(owner == float(o), value, found)
-        return found
-
-    lane = iota((8, LANES), 1)
-    far = (owner[:, LANES:], index[:, LANES:])
-    beside = jnp.where(
-        lane < 2, find(deps[2], *far), jnp.where(lane >= LANES - 2, find(deps[1], *far), 0.0)
-    )
-    near = find(deps[0], owner[:, 0:LANES], index[:, 0:LANES])
-    back = weight * jnp.concatenate([near, beside], axis=1)
-    place = [(s, y) for s in range(3) for y in range(2)]
-    k_of = iota((NK, W), 0) // NM
-    m_of = iota((8, W), 0) % NM
-    drive = []
-    for i, (s, y) in enumerate(place):
-        mech = miscs[s][y : y + 1]
-        drive.append(jnp.where(mech == (m_of + 1).astype(F32), back[i : i + 1, :], 0.0))
-    masks = [
-        miscs[s][y : y + 1] == (k_of + 1).astype(F32) for s, y in place[1:5]
-    ]
-
-    def unadvect(mid, cx, up, cy_up, down, cy_down):
-        return (
-            (1.0 - 4.0 * KD) * mid
-            + pltpu.roll((KD - cx) * mid, 1, 1)
-            + pltpu.roll((KD + cx) * mid, W - 1, 1)
-            + (KD - cy_up) * up
-            + (KD + cy_down) * down
-        )
-
-    def level(l, carry):
-        stats = tiles(l)
-        cx = [0.5 * stats[s][y : y + 1] for s, y in place]
-        cy = [0.5 * stats[s][2 + y : 3 + y] for s, y in place]
-        kern = [stats[s][4 + y : 5 + y] for s, y in place]
-        w = [kern[i] * drive[i] for i in range(6)]
-        u = []
-        for i in range(1, 5):
-            mid = unadvect(w[i], cx[i], w[i - 1], cy[i - 1], w[i + 1], cy[i + 1])
-            twice = jnp.concatenate([mid, mid], axis=0)
-            u.append(jnp.where(masks[i - 1], twice, 0.0))
-        for y in range(2):
-            i = 2 + y
-            v = unadvect(u[i - 1], cx[i], u[i - 2], cy[i - 1], u[i], cy[i + 1])[:, 0:LANES]
-            high, low = split(v)
-            at = pl.ds(pl.multiple_of((2 * l + y) * LANES, LANES), LANES)
-            v3[0:NK, at] = high
-            v3[NK : 2 * NK, at] = low
-            v3[2 * NK :, at] = high
-        return carry
-
-    lax.fori_loop(0, z.levels, level, 0, unroll=UNROLL)
+                r = 2 * (PER * h + g) + y
+                first = lane_roll(seams[y], LANES - 16 * g - 12)
+                last = lane_roll(seams[y], 124 - 16 * g)
+                more = jnp.where(wide < 2, first, jnp.where(wide >= LANES - 2, last, 0.0))
+                at = slice(r * LANES, (r + 1) * LANES)
+                high, low = split(v_ref[:, at] + more)
+                v3[0:NK, at] = high
+                v3[NK : 2 * NK, at] = low
+                v3[2 * NK :, at] = high
     d = d_ref[...]
     for r in range(0, z.rows, 2):
         both = lax.dot_general(
@@ -616,21 +704,47 @@
     ]
     for turn in turns:
         part = part + turn
-    both = jnp.concatenate([part, move(part, along_z)], axis=0)
+    coef, far = pl.pallas_call(
+        functools.partial(coefs_kernel, z),
+        out_shape=(shape(z.halves, 2, 4, NK, LANES), shape(24, LANES)),
+        in_specs=[VMEM] * 3,
+        out_specs=(VMEM, VMEM),
+        compiler_params=LIMIT,
+        name="coefs",
+    )(ext, stat, block)
+    both = pl.pallas_call(
+        join_kernel,
+        out_shape=shape(16, LANES),
+        in_specs=[VMEM] * 3,
+        out_specs=VMEM,
+        compiler_params=LIMIT,
+        name="join",
+    )(part, move(part, along_z), far)
     b0 = move(both, along_x(0, 1))
     b1 = move(both, along_x(1, 1))
-    product, dep = pl.pallas_call(
+    v, dep = pl.pallas_call(
+        functools.partial(prepare_kernel, z),
+        out_shape=(
+            shape(NK, z.rows * LANES),
+            shape(1, pixels),
+        ),
+        in_specs=[VMEM] * 4,
+        out_specs=(VMEM, VMEM),
+        compiler_params=LIMIT,
+        name="prepare",
+    )(both, ext, stat, block)
+    product = pl.pallas_call(
         functools.partial(product_kernel, z),
-        out_shape=(shape(*cells, dtype=BF), shape(1, pixels)),
-        in_specs=[VMEM] * 7,
-        out_specs=(VMEM, VMEM),
+        out_shape=shape(*cells, dtype=BF),
+        in_specs=[VMEM] * 6,
+        out_specs=VMEM,
         scratch_shapes=[
             pltpu.VMEM((3 * NK, z.rows * LANES), BF),
             pltpu.VMEM(cells, F32),
         ],
         compiler_params=LIMIT,
         name="product",
-    )(both, b1, b0, ext, stat, block, d)
+    )(b1, b0, v, coef, far, d)
     return product.reshape(direction.shape), dep.reshape(-1)
 
 

time: 30.5 us -> 30.3 us (level)
  waiting for transfers between devices: 6.66 us -> 4.66 us
  Pallas kernels: 5.74 us -> 7.53 us
    ppermute x9, waiting for transfers between devices: 3.61 us -> 1.61 us  [move(): return lax.ppermute(v, ALL, perm)]
    pallas_call x1 -> x4, Pallas kernels: 1.74 us -> 3.53 us  [the longest x1 1.53 us: per_device(): pl.pallas_call(functools.partial(product_kernel, z), out_shape=shape(*cel...]
  transfers between devices with their start and end apart: 13 -> 13, of which waited for: 6 -> 6; matrix products, arithmetic and copies ran while one was open for 0% -> 0% of each run, Pallas kernels for 7% -> 14%
where the time goes in v6:
time: 30.3 us; the launch traced here: 29.7 us
  starting transfers between devices  16.8 us (55%)
  Pallas kernels  7.53 us (25%)
  waiting for transfers between devices  4.66 us (15%)
  between operations  0.69 us (2%)
    ppermute x9, starting transfers between devices, move(): return lax.ppermute(v, ALL, perm)  9.24 us
    ppermute x3, starting transfers between devices, per_device(): lax.ppermute(part, 'swath', [(i, i ^ 2 * k ^ 1) for i in range(nsw)])  5.63 us
    ppermute x3, waiting for transfers between devices, per_device(): lax.ppermute(part, 'swath', [(i, i ^ 2 * k ^ 1) for i in range(nsw)])  2.23 us
    ppermute x1, starting transfers between devices, per_device(): part = part + lax.ppermute(part, 'swath', [(i, i ^ 1) for i in range(nsw)])  1.97 us
    pallas_call x1, Pallas kernels, per_device(): pl.pallas_call(functools.partial(columns_kernel, z), out_shape=(shape(16,...  1.79 us
    pallas_call x1, Pallas kernels, per_device(): pl.pallas_call(functools.partial(project_kernel, z), out_shape=(shape(z.o...  1.76 us
    ppermute x9, waiting for transfers between devices, move(): return lax.ppermute(v, ALL, perm)  1.61 us
    pallas_call x1, Pallas kernels, per_device(): pl.pallas_call(functools.partial(product_kernel, z), out_shape=shape(*cel...  1.53 us
  transfers between devices with their start and end apart: 13, of which 6 were waited for; matrix products, arithmetic and copies ran while one was open for 0% of the time, Pallas kernels for 14%

profile of v6, /device:TPU:97, one launch (start us, length us, event | category | flops | bytes accessed | tf_op | source)
XLA Modules:
  0.0 29.7 jit_solution(10685845819278484140)
XLA Ops:
  0.6 1.8 %project.1 = (f32[320,128]{1,0:T(8,128)S(1)}, bf16[512,128]{1,0:T(8,128)(2,1)S(1)}, f32[24,128]{1,0:T(8,128)S(1)}, f32[96,128]{1,0:T(8,128)S(1)}, bf16[48,120]{1,0:T(8,128)(2,1)S(1)}) custom-call(bf16[2400,128]{1,0:T(8,128)(2,1)} %bitcast.5, bf16[4,120,120]{2,1,0:T(8,128)(2,1)} %prop_hbm.1, f32[10,2,128]{2,1,0:T(2,128)} %cx_hbm.1, f32[10,2,128]{2,1,0:T(2,128)} %cy_hbm.1, ...), custom_call_target="tpu_custom_call" | custom-call | tf_op jit(solution)/shard_map/project/pallas_call | solution.py:620
  2.4 1.4 %collective-permute-start.3 = (f32[24,128]{1,0:T(8,128)S(1)}, f32[24,128]{1,0:T(8,128)S(1)}, u32[]{:S(2)}, u32[]{:S(2)}) collective-permute-start(f32[24,128]{1,0:T(8,128)S(1)} %get-tuple-element.24), channel_id=1, source_target_pairs={{0,64},{1,65},{2,66},{3,67},{4,68},{5,69},{6,70},{7,71},{8,72},{9,... | collective-permute-start | bytes 36872 | tf_op jit(solution)/shard_map/ppermute | solution.py:616
  3.8 1.0 %collective-permute-start.2 = (f32[24,128]{1,0:T(8,128)S(1)}, f32[24,128]{1,0:T(8,128)S(1)}, u32[]{:S(2)}, u32[]{:S(2)}) collective-permute-start(f32[24,128]{1,0:T(8,128)S(1)} %get-tuple-element.24), channel_id=1, source_target_pairs={{0,1},{1,0},{2,3},{3,2},{4,5},{5,4},{6,7},{7,6},{8,9},{9,8},{10,11... | collective-permute-start | bytes 36872 | tf_op jit(solution)/shard_map/ppermute | solution.py:616
  4.7 0.0 collective-permute-start.1
  4.7 1.6 %collective-permute-start = (bf16[512,128]{1,0:T(8,128)(2,1)S(1)}, bf16[512,128]{1,0:T(8,128)(2,1)S(1)}, u32[]{:S(2)}, u32[]{:S(2)}) collective-permute-start(bf16[512,128]{1,0:T(8,128)(2,1)S(1)} %get-tuple-element.21), channel_id=1, source_target_pairs={{0,64},{1,2},{2,1},{3,4},{4,3},{5,6},{6,5},{7,8},{8,7},{9,10},{10,... | collective-permute-start | bytes 393224 | tf_op jit(solution)/shard_map/ppermute | solution.py:616
  6.3 0.0 collective-permute-done.3.x0_ref
  6.4 0.0 collective-permute-done.2.x1_ref
  6.4 0.9 %collective-permute-start.4 = (f32[24,128]{1,0:T(8,128)S(1)}, f32[24,128]{1,0:T(8,128)S(1)}, u32[]{:S(2)}, u32[]{:S(2)}) collective-permute-start(f32[24,128]{1,0:T(8,128)S(1)} %get-tuple-element.25.side_ref), channel_id=1, source_target_pairs={{0,1},{1,0},{2,3},{3,2},{4,5},{5,4},{6,7},{7,6},{8,9},{9,8},{10,11... | collective-permute-start | bytes 36872 | tf_op jit(solution)/shard_map/ppermute | solution.py:616
  7.3 0.9 %collective-permute-start.5 = (bf16[48,128]{1,0:T(8,128)(2,1)S(1)}, bf16[48,128]{1,0:T(8,128)(2,1)S(1)}, u32[]{:S(2)}, u32[]{:S(2)}) collective-permute-start(bf16[48,128]{1,0:T(8,128)(2,1)S(1)} %get-tuple-element.30), channel_id=1, source_target_pairs={{0,64},{1,2},{2,1},{3,4},{4,3},{5,6},{6,5},{7,8},{8,7},{9,10},{10,... | collective-permute-start | bytes 36872 | tf_op jit(solution)/shard_map/ppermute | solution.py:616
  8.2 0.0 collective-permute-done.4.far_ref
  8.2 0.0 collective-permute-done.1.a_ref
  8.2 1.8 %columns.1 = (f32[16,128]{1,0:T(8,128)S(1)}, f32[2,11,8,256]{3,2,1,0:T(8,128)S(1)}, f32[16,128]{1,0:T(8,128)S(1)}) custom-call(bf16[512,128]{1,0:T(8,128)(2,1)S(1)} %collective-permute-done.1.a_ref, f32[320,128]{1,0:T(8,128)S(1)} %get-tuple-element.22.g_ref, f32[96,128]{1,0:T(8,128)S(1)} %get-tuple-element.23.st_ref, ...), custom_call_target="tpu_custom_call" | custom-call | tf_op jit(solution)/shard_map/columns/pallas_call | solution.py:673
  10.0 0.0 collective-permute-done.b_ref
  10.0 0.3 beyond.1
  10.2 0.5 %collective-permute-done.5.far_ref = bf16[48,128]{1,0:T(8,128)(2,1)S(1)} collective-permute-done((bf16[48,128]{1,0:T(8,128)(2,1)S(1)}, bf16[48,128]{1,0:T(8,128)(2,1)S(1)}, u32[]{:S(2)}, u32[]{:S(2)}) %collective-permute-start.5) | collective-permute-done | bytes 12320 | tf_op jit(solution)/shard_map/ppermute | solution.py:616
  10.7 0.2 corner.1
  10.9 2.0 %collective-permute-start.6 = (f32[8,128]{1,0:T(8,128)S(1)}, f32[8,128]{1,0:T(8,128)S(1)}, u32[]{:S(2)}, u32[]{:S(2)}) collective-permute-start(f32[8,128]{1,0:T(8,128)S(1)} %get-tuple-element.31), channel_id=1, source_target_pairs={{0,1},{1,0},{2,3},{3,2},{4,5},{5,4},{6,7},{7,6},{8,9},{9,8},{10,11... | collective-permute-start | bytes 12296 | tf_op jit(solution)/shard_map/ppermute | solution.py:700
  12.8 0.8 %collective-permute-done.6 = f32[8,128]{1,0:T(8,128)S(1)} collective-permute-done((f32[8,128]{1,0:T(8,128)S(1)}, f32[8,128]{1,0:T(8,128)S(1)}, u32[]{:S(2)}, u32[]{:S(2)}) %collective-permute-start.6) | collective-permute-done | bytes 4128 | tf_op jit(solution)/shard_map/ppermute | solution.py:700
  13.7 2.0 %collective-permute-start.9 = (f32[8,128]{1,0:T(8,128)S(1)}, f32[8,128]{1,0:T(8,128)S(1)}, u32[]{:S(2)}, u32[]{:S(2)}) collective-permute-start(f32[8,128]{1,0:T(8,128)S(1)} %add.12), channel_id=1, source_target_pairs={{0,5},{1,4},{2,7},{3,6},{4,1},{5,0},{6,3},{7,2},{8,13},{9,12},{10,... | collective-permute-start | bytes 12296 | tf_op jit(solution)/shard_map/ppermute | solution.py:702
  15.6 2.9 %collective-permute-start.8 = (f32[8,128]{1,0:T(8,128)S(1)}, f32[8,128]{1,0:T(8,128)S(1)}, u32[]{:S(2)}, u32[]{:S(2)}) collective-permute-start(f32[8,128]{1,0:T(8,128)S(1)} %add.12), channel_id=1, source_target_pairs={{0,7},{1,6},{2,5},{3,4},{4,3},{5,2},{6,1},{7,0},{8,15},{9,14},{10,... | collective-permute-start | bytes 12296 | tf_op jit(solution)/shard_map/ppermute | solution.py:702
  18.5 0.8 %collective-permute-start.7 = (f32[8,128]{1,0:T(8,128)S(1)}, f32[8,128]{1,0:T(8,128)S(1)}, u32[]{:S(2)}, u32[]{:S(2)}) collective-permute-start(f32[8,128]{1,0:T(8,128)S(1)} %add.12), channel_id=1, source_target_pairs={{0,3},{1,2},{2,1},{3,0},{4,7},{5,6},{6,5},{7,4},{8,11},{9,10},{10,... | collective-permute-start | bytes 12296 | tf_op jit(solution)/shard_map/ppermute | solution.py:702
  19.3 0.0 collective-permute-done.9
  19.3 0.6 %collective-permute-done.8 = f32[8,128]{1,0:T(8,128)S(1)} collective-permute-done((f32[8,128]{1,0:T(8,128)S(1)}, f32[8,128]{1,0:T(8,128)S(1)}, u32[]{:S(2)}, u32[]{:S(2)}) %collective-permute-start.8) | collective-permute-done | bytes 4128 | tf_op jit(solution)/shard_map/ppermute | solution.py:702
  19.9 1.6 %collective-permute-done.7 = f32[8,128]{1,0:T(8,128)S(1)} collective-permute-done((f32[8,128]{1,0:T(8,128)S(1)}, f32[8,128]{1,0:T(8,128)S(1)}, u32[]{:S(2)}, u32[]{:S(2)}) %collective-permute-start.7) | collective-permute-done | bytes 4128 | tf_op jit(solution)/shard_map/ppermute | solution.py:702
  21.5 1.1 %collective-permute-start.10 = (f32[8,128]{1,0:T(8,128)S(1)}, f32[8,128]{1,0:T(8,128)S(1)}, u32[]{:S(2)}, u32[]{:S(2)}) collective-permute-start(f32[8,128]{1,0:T(8,128)S(1)} %add_add_fusion.part_ref), channel_id=1, source_target_pairs={{0,9},{1,8},{2,0},{3,1},{4,2},{5,3},{6,4},{7,5},{8,17},{9,16},{10,... | collective-permute-start | bytes 12296 | tf_op jit(solution)/shard_map/ppermute | solution.py:616
  22.6 0.9 %coefs.1 = (f32[2,2,4,16,128]{4,3,2,1,0:T(8,128)S(1)}, f32[24,128]{1,0:T(8,128)S(1)}) custom-call(f32[2,11,8,256]{3,2,1,0:T(8,128)S(1)} %get-tuple-element.32.oa_ref, f32[11,8,128]{2,1,0:T(8,128)S(1)} %get-tuple-element.33.stat_ref, f32[11,8,128]{2,1,0:T(8,128)S(1)} %get-tuple-element.34.block_ref), custom_call_target="tpu_custom_call" | custom-call | tf_op jit(solution)/shard_map/coefs/pallas_call | solution.py:707
  23.5 1.1 %collective-permute-done.10.next_ref = f32[8,128]{1,0:T(8,128)S(1)} collective-permute-done((f32[8,128]{1,0:T(8,128)S(1)}, f32[8,128]{1,0:T(8,128)S(1)}, u32[]{:S(2)}, u32[]{:S(2)}) %collective-permute-start.10) | collective-permute-done | bytes 4128 | tf_op jit(solution)/shard_map/ppermute | solution.py:616
  24.6 2.3 %collective-permute-start.12 = (f32[16,128]{1,0:T(8,128)S(1)}, f32[16,128]{1,0:T(8,128)S(1)}, u32[]{:S(2)}, u32[]{:S(2)}) collective-permute-start(f32[16,128]{1,0:T(8,128)S(1)} %join.1.own_ref), channel_id=1, source_target_pairs={{0,65},{1,64},{2,67},{3,66},{4,69},{5,68},{6,71},{7,70},{8,73},{9,... | collective-permute-start | bytes 24584 | tf_op jit(solution)/shard_map/ppermute | solution.py:616
  26.9 0.2 collective-permute-start.11
  27.0 1.1 %prepare.1 = (f32[16,2560]{1,0:T(8,128)S(1)}, f32[1,64]{1,0:T(1,128)}) custom-call(f32[16,128]{1,0:T(8,128)S(1)} %join.1.own_ref, f32[2,11,8,256]{3,2,1,0:T(8,128)S(1)} %get-tuple-element.32.oa_ref, f32[11,8,128]{2,1,0:T(8,128)S(1)} %get-tuple-element.33.stat_ref, f32[11,8,128]{2,1,0:T(8,128)S(1)} %get-tuple-element.34.block_ref), custom_call_target="tpu_custom_call" | custom-call | tf_op jit(solution)/shard_map/prepare/pallas_call | solution.py:725
  28.1 0.1 collective-permute-done.12.x0_ref
  28.2 0.0 collective-permute-done.11.x1_ref
  28.2 1.5 %product.1 = bf16[2400,128]{1,0:T(8,128)(2,1)} custom-call(f32[16,128]{1,0:T(8,128)S(1)} %collective-permute-done.11.x1_ref, f32[16,128]{1,0:T(8,128)S(1)} %collective-permute-done.12.x0_ref, f32[16,2560]{1,0:T(8,128)S(1)} %get-tuple-element.36.v_ref, f32[2,2,4,16,128]{4,3,2,1,0:T(8,128)S(1)} %get-tuple-element.37.coef_ref, ...), custom_call_target="tpu_custom_call" | custom-call | tf_op jit(solution)/shard_map/product/pallas_call | solution.py:736
  (4 shorter events, 0.0 us)
Async XLA Ops:
  2.4 3.9 %collective-permute-start.3 = (f32[24,128]{1,0:T(8,128)S(1)}, f32[24,128]{1,0:T(8,128)S(1)}, u32[]{:S(2)}, u32[]{:S(2)}) collective-permute-start(f32[24,128]{1,0:T(8,128)S(1)} %get-tuple-element.24), channel_id=1, source_target_pairs={{0,64},{1,65},{2,66},{3,67},{4,68},{5,69},{6,70},{7,71},{8,72},{9,... | collective-permute-start | bytes 36872 | tf_op jit(solution)/shard_map/ppermute | solution.py:616
  3.8 2.6 %collective-permute-start.2 = (f32[24,128]{1,0:T(8,128)S(1)}, f32[24,128]{1,0:T(8,128)S(1)}, u32[]{:S(2)}, u32[]{:S(2)}) collective-permute-start(f32[24,128]{1,0:T(8,128)S(1)} %get-tuple-element.24), channel_id=1, source_target_pairs={{0,1},{1,0},{2,3},{3,2},{4,5},{5,4},{6,7},{7,6},{8,9},{9,8},{10,11... | collective-permute-start | bytes 36872 | tf_op jit(solution)/shard_map/ppermute | solution.py:616
  4.7 3.4 %collective-permute-start.1 = (bf16[512,128]{1,0:T(8,128)(2,1)S(1)}, bf16[512,128]{1,0:T(8,128)(2,1)S(1)}, u32[]{:S(2)}, u32[]{:S(2)}) collective-permute-start(bf16[512,128]{1,0:T(8,128)(2,1)S(1)} %get-tuple-element.21), channel_id=1, source_target_pairs={{0,1},{1,0},{2,3},{3,2},{4,5},{5,4},{6,7},{7,6},{8,9},{9,8},{10,11... | collective-permute-start | bytes 393224 | tf_op jit(solution)/shard_map/ppermute | solution.py:616
  4.7 5.2 %collective-permute-start = (bf16[512,128]{1,0:T(8,128)(2,1)S(1)}, bf16[512,128]{1,0:T(8,128)(2,1)S(1)}, u32[]{:S(2)}, u32[]{:S(2)}) collective-permute-start(bf16[512,128]{1,0:T(8,128)(2,1)S(1)} %get-tuple-element.21), channel_id=1, source_target_pairs={{0,64},{1,2},{2,1},{3,4},{4,3},{5,6},{6,5},{7,8},{8,7},{9,10},{10,... | collective-permute-start | bytes 393224 | tf_op jit(solution)/shard_map/ppermute | solution.py:616
  6.4 1.8 %collective-permute-start.4 = (f32[24,128]{1,0:T(8,128)S(1)}, f32[24,128]{1,0:T(8,128)S(1)}, u32[]{:S(2)}, u32[]{:S(2)}) collective-permute-start(f32[24,128]{1,0:T(8,128)S(1)} %get-tuple-element.25.side_ref), channel_id=1, source_target_pairs={{0,1},{1,0},{2,3},{3,2},{4,5},{5,4},{6,7},{7,6},{8,9},{9,8},{10,11... | collective-permute-start | bytes 36872 | tf_op jit(solution)/shard_map/ppermute | solution.py:616
  7.3 3.4 %collective-permute-start.5 = (bf16[48,128]{1,0:T(8,128)(2,1)S(1)}, bf16[48,128]{1,0:T(8,128)(2,1)S(1)}, u32[]{:S(2)}, u32[]{:S(2)}) collective-permute-start(bf16[48,128]{1,0:T(8,128)(2,1)S(1)} %get-tuple-element.30), channel_id=1, source_target_pairs={{0,64},{1,2},{2,1},{3,4},{4,3},{5,6},{6,5},{7,8},{8,7},{9,10},{10,... | collective-permute-start | bytes 36872 | tf_op jit(solution)/shard_map/ppermute | solution.py:616
  10.9 2.8 %collective-permute-start.6 = (f32[8,128]{1,0:T(8,128)S(1)}, f32[8,128]{1,0:T(8,128)S(1)}, u32[]{:S(2)}, u32[]{:S(2)}) collective-permute-start(f32[8,128]{1,0:T(8,128)S(1)} %get-tuple-element.31), channel_id=1, source_target_pairs={{0,1},{1,0},{2,3},{3,2},{4,5},{5,4},{6,7},{7,6},{8,9},{9,8},{10,11... | collective-permute-start | bytes 12296 | tf_op jit(solution)/shard_map/ppermute | solution.py:700
  13.7 5.6 %collective-permute-start.9 = (f32[8,128]{1,0:T(8,128)S(1)}, f32[8,128]{1,0:T(8,128)S(1)}, u32[]{:S(2)}, u32[]{:S(2)}) collective-permute-start(f32[8,128]{1,0:T(8,128)S(1)} %add.12), channel_id=1, source_target_pairs={{0,5},{1,4},{2,7},{3,6},{4,1},{5,0},{6,3},{7,2},{8,13},{9,12},{10,... | collective-permute-start | bytes 12296 | tf_op jit(solution)/shard_map/ppermute | solution.py:702
  15.6 4.2 %collective-permute-start.8 = (f32[8,128]{1,0:T(8,128)S(1)}, f32[8,128]{1,0:T(8,128)S(1)}, u32[]{:S(2)}, u32[]{:S(2)}) collective-permute-start(f32[8,128]{1,0:T(8,128)S(1)} %add.12), channel_id=1, source_target_pairs={{0,7},{1,6},{2,5},{3,4},{4,3},{5,2},{6,1},{7,0},{8,15},{9,14},{10,... | collective-permute-start | bytes 12296 | tf_op jit(solution)/shard_map/ppermute | solution.py:702
  18.5 3.0 %collective-permute-start.7 = (f32[8,128]{1,0:T(8,128)S(1)}, f32[8,128]{1,0:T(8,128)S(1)}, u32[]{:S(2)}, u32[]{:S(2)}) collective-permute-start(f32[8,128]{1,0:T(8,128)S(1)} %add.12), channel_id=1, source_target_pairs={{0,3},{1,2},{2,1},{3,0},{4,7},{5,6},{6,5},{7,4},{8,11},{9,10},{10,... | collective-permute-start | bytes 12296 | tf_op jit(solution)/shard_map/ppermute | solution.py:702
  21.5 3.0 %collective-permute-start.10 = (f32[8,128]{1,0:T(8,128)S(1)}, f32[8,128]{1,0:T(8,128)S(1)}, u32[]{:S(2)}, u32[]{:S(2)}) collective-permute-start(f32[8,128]{1,0:T(8,128)S(1)} %add_add_fusion.part_ref), channel_id=1, source_target_pairs={{0,9},{1,8},{2,0},{3,1},{4,2},{5,3},{6,4},{7,5},{8,17},{9,16},{10,... | collective-permute-start | bytes 12296 | tf_op jit(solution)/shard_map/ppermute | solution.py:616
  24.6 3.6 %collective-permute-start.12 = (f32[16,128]{1,0:T(8,128)S(1)}, f32[16,128]{1,0:T(8,128)S(1)}, u32[]{:S(2)}, u32[]{:S(2)}) collective-permute-start(f32[16,128]{1,0:T(8,128)S(1)} %join.1.own_ref), channel_id=1, source_target_pairs={{0,65},{1,64},{2,67},{3,66},{4,69},{5,68},{6,71},{7,70},{8,73},{9,... | collective-permute-start | bytes 24584 | tf_op jit(solution)/shard_map/ppermute | solution.py:616
  26.9 1.3 %collective-permute-start.11 = (f32[16,128]{1,0:T(8,128)S(1)}, f32[16,128]{1,0:T(8,128)S(1)}, u32[]{:S(2)}, u32[]{:S(2)}) collective-permute-start(f32[16,128]{1,0:T(8,128)S(1)} %join.1.own_ref), channel_id=1, source_target_pairs={{0,1},{1,0},{2,3},{3,2},{4,5},{5,4},{6,7},{7,6},{8,9},{9,8},{10,11... | collective-permute-start | bytes 24584 | tf_op jit(solution)/shard_map/ppermute | solution.py:616

commit v7 on v6

--- a/solution.py
+++ b/solution.py
@@ -361,12 +361,19 @@
     return ((sub < 2) & (swath == 0)) | ((sub >= 4) & (swath == z.nsw - 1))
 
 
-def find(z, outer, dep, owner, index):
-    table = jnp.zeros((8, LANES), F32)
-    for o in range(z.nsw):
-        row = jnp.where(outer, dep[8 + o : 9 + o, :], dep[o : o + 1, :])
-        table = jnp.where(owner == float(o), row, table)
-    return jnp.take_along_axis(table, index, axis=1)
+def table_of(outer, sums, owner):
+    row = owner.astype(jnp.int32)
+    return jnp.where(
+        outer,
+        jnp.take_along_axis(sums[8:16], row, axis=0),
+        jnp.take_along_axis(sums[0:8], row, axis=0),
+    )
+
+
+def find(table, index):
+    at = index.astype(jnp.int32)
+    half = LANES // 2
+    return jnp.take_along_axis(table, at, axis=1) * jnp.take_along_axis(table, at + half, axis=1)
 
 
 PLACE = [(s, y) for s in range(3) for y in range(2)]
@@ -428,10 +435,17 @@
 def coefs_kernel(z, oa_ref, stat_ref, block_ref, coef_ref, far_ref):
     tiles = tiles_of(z, oa_ref, stat_ref, block_ref)
     miscs = tiles(z.levels)
-    for n, f in enumerate((3, 1, 2)):
-        far_ref[8 * n : 8 * n + 8, :] = stack(miscs, f)[:, LANES:]
     sub = iota((8, LANES), 0)
     lane = iota((8, LANES), 1)
+    on_left = lane % 16 >= 8
+    owner, index, weight = (stack(miscs, f)[:, LANES:] for f in (3, 1, 2))
+    far_ref[0:8, :] = jnp.broadcast_to(owner[:, 0:1], (8, LANES))
+    far_ref[8:16, :] = jnp.broadcast_to(owner[:, LANES - 1 :], (8, LANES))
+    for n, v in ((2, index), (4, weight)):
+        nearer = jnp.where(on_left, v[:, LANES - 1 :], v[:, 0:1])
+        farther = jnp.where(on_left, v[:, LANES - 2 : LANES - 1], v[:, 1:2])
+        far_ref[8 * n : 8 * n + 8, :] = nearer
+        far_ref[8 * n + 8 : 8 * n + 16, :] = farther
 
     def pack(block, g, old):
         b = 16 * g
@@ -480,7 +494,7 @@
         :, 0 : LANES // 2
     ]
     owner, index, weight = (stack(miscs, f)[:, 0:LANES] for f in (3, 1, 2))
-    near = find(z, outer_rows(z, swath), dep, owner, index.astype(jnp.int32))
+    near = find(table_of(outer_rows(z, swath), own_ref[...], owner), index)
     back = jnp.concatenate([weight * near, jnp.zeros((8, LANES), F32)], axis=1)
 
     def level(l, carry):
@@ -504,16 +518,16 @@
     gx, swath, _ = z.place()
     left, right = sides_of(z, gx, x0_ref[...], x1_ref[...])
     outer = outer_rows(z, swath)
-    owner, index = far_ref[0:8, :], far_ref[8:16, :].astype(jnp.int32)
-    lane = iota((8, LANES), 1)
-    beside = far_ref[16:24, :] * jnp.where(
-        lane < 2,
-        find(z, outer, weigh(right), owner[:, 0:1], index),
-        find(z, outer, weigh(left), owner[:, LANES - 1 :], index),
-    )
-    on_left = lane % 16 >= 8
-    near = jnp.where(on_left, beside[:, LANES - 1 :], beside[:, 0:1])
-    away = jnp.where(on_left, beside[:, LANES - 2 : LANES - 1], beside[:, 1:2])
+    right = table_of(outer, right, far_ref[0:8, :])
+    left = table_of(outer, left, far_ref[8:16, :])
+    on_left = iota((8, LANES), 1) % 16 >= 8
+
+    def back(n):
+        index = far_ref[16 + 8 * n : 24 + 8 * n, :]
+        weight = far_ref[32 + 8 * n : 40 + 8 * n, :]
+        return weight * jnp.where(on_left, find(left, index), find(right, index))
+
+    near, away = back(0), back(1)
     wide = iota((NK, LANES), 1)
     for h in range(z.halves):
         seams = []
@@ -706,7 +720,7 @@
         part = part + turn
     coef, far = pl.pallas_call(
         functools.partial(coefs_kernel, z),
-        out_shape=(shape(z.halves, 2, 4, NK, LANES), shape(24, LANES)),
+        out_shape=(shape(z.halves, 2, 4, NK, LANES), shape(48, LANES)),
         in_specs=[VMEM] * 3,
         out_specs=(VMEM, VMEM),
         compiler_params=LIMIT,

time: 30.3 us -> 30.2 us (level)
  transfers between devices with their start and end apart: 13 -> 13, of which waited for: 6 -> 5; matrix products, arithmetic and copies ran while one was open for 0% -> 0% of each run, Pallas kernels for 14% -> 14%
where the time goes in v7:
time: 30.2 us; the launch traced here: 29.6 us
  starting transfers between devices  16.8 us (56%)
  Pallas kernels  7.5 us (25%)
  waiting for transfers between devices  4.57 us (15%)
  between operations  0.69 us (2%)
    ppermute x9, starting transfers between devices, move(): return lax.ppermute(v, ALL, perm)  9.24 us
    ppermute x3, starting transfers between devices, per_device(): lax.ppermute(part, 'swath', [(i, i ^ 2 * k ^ 1) for i in range(nsw)])  5.63 us
    ppermute x3, waiting for transfers between devices, per_device(): lax.ppermute(part, 'swath', [(i, i ^ 2 * k ^ 1) for i in range(nsw)])  2.23 us
    ppermute x1, starting transfers between devices, per_device(): part = part + lax.ppermute(part, 'swath', [(i, i ^ 1) for i in range(nsw)])  1.97 us
    pallas_call x1, Pallas kernels, per_device(): pl.pallas_call(functools.partial(columns_kernel, z), out_shape=(shape(16,...  1.79 us
    pallas_call x1, Pallas kernels, per_device(): pl.pallas_call(functools.partial(project_kernel, z), out_shape=(shape(z.o...  1.76 us
    ppermute x9, waiting for transfers between devices, move(): return lax.ppermute(v, ALL, perm)  1.52 us
    pallas_call x1, Pallas kernels, per_device(): pl.pallas_call(functools.partial(product_kernel, z), out_shape=shape(*cel...  1.39 us
  transfers between devices with their start and end apart: 13, of which 5 were waited for; matrix products, arithmetic and copies ran while one was open for 0% of the time, Pallas kernels for 14%

profile of v7, /device:TPU:97, one launch (start us, length us, event | category | flops | bytes accessed | tf_op | source)
XLA Modules:
  0.0 29.6 jit_solution(7276756382841568821)
XLA Ops:
  0.6 1.8 %project.1 = (f32[320,128]{1,0:T(8,128)S(1)}, bf16[512,128]{1,0:T(8,128)(2,1)S(1)}, f32[24,128]{1,0:T(8,128)S(1)}, f32[96,128]{1,0:T(8,128)S(1)}, bf16[48,120]{1,0:T(8,128)(2,1)S(1)}) custom-call(bf16[2400,128]{1,0:T(8,128)(2,1)} %bitcast.5, bf16[4,120,120]{2,1,0:T(8,128)(2,1)} %prop_hbm.1, f32[10,2,128]{2,1,0:T(2,128)} %cx_hbm.1, f32[10,2,128]{2,1,0:T(2,128)} %cy_hbm.1, ...), custom_call_target="tpu_custom_call" | custom-call | tf_op jit(solution)/shard_map/project/pallas_call | solution.py:634
  2.4 1.4 %collective-permute-start.3 = (f32[24,128]{1,0:T(8,128)S(1)}, f32[24,128]{1,0:T(8,128)S(1)}, u32[]{:S(2)}, u32[]{:S(2)}) collective-permute-start(f32[24,128]{1,0:T(8,128)S(1)} %get-tuple-element.24), channel_id=1, source_target_pairs={{0,64},{1,65},{2,66},{3,67},{4,68},{5,69},{6,70},{7,71},{8,72},{9,... | collective-permute-start | bytes 36872 | tf_op jit(solution)/shard_map/ppermute | solution.py:630
  3.8 1.0 %collective-permute-start.2 = (f32[24,128]{1,0:T(8,128)S(1)}, f32[24,128]{1,0:T(8,128)S(1)}, u32[]{:S(2)}, u32[]{:S(2)}) collective-permute-start(f32[24,128]{1,0:T(8,128)S(1)} %get-tuple-element.24), channel_id=1, source_target_pairs={{0,1},{1,0},{2,3},{3,2},{4,5},{5,4},{6,7},{7,6},{8,9},{9,8},{10,11... | collective-permute-start | bytes 36872 | tf_op jit(solution)/shard_map/ppermute | solution.py:630
  4.7 0.0 collective-permute-start.1
  4.7 1.6 %collective-permute-start = (bf16[512,128]{1,0:T(8,128)(2,1)S(1)}, bf16[512,128]{1,0:T(8,128)(2,1)S(1)}, u32[]{:S(2)}, u32[]{:S(2)}) collective-permute-start(bf16[512,128]{1,0:T(8,128)(2,1)S(1)} %get-tuple-element.21), channel_id=1, source_target_pairs={{0,64},{1,2},{2,1},{3,4},{4,3},{5,6},{6,5},{7,8},{8,7},{9,10},{10,... | collective-permute-start | bytes 393224 | tf_op jit(solution)/shard_map/ppermute | solution.py:630
  6.3 0.0 collective-permute-done.3.x0_ref
  6.4 0.0 collective-permute-done.2.x1_ref
  6.4 0.9 %collective-permute-start.4 = (f32[24,128]{1,0:T(8,128)S(1)}, f32[24,128]{1,0:T(8,128)S(1)}, u32[]{:S(2)}, u32[]{:S(2)}) collective-permute-start(f32[24,128]{1,0:T(8,128)S(1)} %get-tuple-element.25.side_ref), channel_id=1, source_target_pairs={{0,1},{1,0},{2,3},{3,2},{4,5},{5,4},{6,7},{7,6},{8,9},{9,8},{10,11... | collective-permute-start | bytes 36872 | tf_op jit(solution)/shard_map/ppermute | solution.py:630
  7.3 0.9 %collective-permute-start.5 = (bf16[48,128]{1,0:T(8,128)(2,1)S(1)}, bf16[48,128]{1,0:T(8,128)(2,1)S(1)}, u32[]{:S(2)}, u32[]{:S(2)}) collective-permute-start(bf16[48,128]{1,0:T(8,128)(2,1)S(1)} %get-tuple-element.30), channel_id=1, source_target_pairs={{0,64},{1,2},{2,1},{3,4},{4,3},{5,6},{6,5},{7,8},{8,7},{9,10},{10,... | collective-permute-start | bytes 36872 | tf_op jit(solution)/shard_map/ppermute | solution.py:630
  8.2 0.0 collective-permute-done.4.far_ref
  8.2 0.0 collective-permute-done.1.a_ref
  8.2 1.8 %columns.1 = (f32[16,128]{1,0:T(8,128)S(1)}, f32[2,11,8,256]{3,2,1,0:T(8,128)S(1)}, f32[16,128]{1,0:T(8,128)S(1)}) custom-call(bf16[512,128]{1,0:T(8,128)(2,1)S(1)} %collective-permute-done.1.a_ref, f32[320,128]{1,0:T(8,128)S(1)} %get-tuple-element.22.g_ref, f32[96,128]{1,0:T(8,128)S(1)} %get-tuple-element.23.st_ref, ...), custom_call_target="tpu_custom_call" | custom-call | tf_op jit(solution)/shard_map/columns/pallas_call | solution.py:687
  10.0 0.0 collective-permute-done.b_ref
  10.0 0.3 beyond.1
  10.2 0.5 %collective-permute-done.5.far_ref = bf16[48,128]{1,0:T(8,128)(2,1)S(1)} collective-permute-done((bf16[48,128]{1,0:T(8,128)(2,1)S(1)}, bf16[48,128]{1,0:T(8,128)(2,1)S(1)}, u32[]{:S(2)}, u32[]{:S(2)}) %collective-permute-start.5) | collective-permute-done | bytes 12320 | tf_op jit(solution)/shard_map/ppermute | solution.py:630
  10.7 0.2 corner.1
  10.9 2.0 %collective-permute-start.6 = (f32[8,128]{1,0:T(8,128)S(1)}, f32[8,128]{1,0:T(8,128)S(1)}, u32[]{:S(2)}, u32[]{:S(2)}) collective-permute-start(f32[8,128]{1,0:T(8,128)S(1)} %get-tuple-element.31), channel_id=1, source_target_pairs={{0,1},{1,0},{2,3},{3,2},{4,5},{5,4},{6,7},{7,6},{8,9},{9,8},{10,11... | collective-permute-start | bytes 12296 | tf_op jit(solution)/shard_map/ppermute | solution.py:714
  12.8 0.8 %collective-permute-done.6 = f32[8,128]{1,0:T(8,128)S(1)} collective-permute-done((f32[8,128]{1,0:T(8,128)S(1)}, f32[8,128]{1,0:T(8,128)S(1)}, u32[]{:S(2)}, u32[]{:S(2)}) %collective-permute-start.6) | collective-permute-done | bytes 4128 | tf_op jit(solution)/shard_map/ppermute | solution.py:714
  13.7 2.0 %collective-permute-start.9 = (f32[8,128]{1,0:T(8,128)S(1)}, f32[8,128]{1,0:T(8,128)S(1)}, u32[]{:S(2)}, u32[]{:S(2)}) collective-permute-start(f32[8,128]{1,0:T(8,128)S(1)} %add.12), channel_id=1, source_target_pairs={{0,5},{1,4},{2,7},{3,6},{4,1},{5,0},{6,3},{7,2},{8,13},{9,12},{10,... | collective-permute-start | bytes 12296 | tf_op jit(solution)/shard_map/ppermute | solution.py:716
  15.6 2.9 %collective-permute-start.8 = (f32[8,128]{1,0:T(8,128)S(1)}, f32[8,128]{1,0:T(8,128)S(1)}, u32[]{:S(2)}, u32[]{:S(2)}) collective-permute-start(f32[8,128]{1,0:T(8,128)S(1)} %add.12), channel_id=1, source_target_pairs={{0,7},{1,6},{2,5},{3,4},{4,3},{5,2},{6,1},{7,0},{8,15},{9,14},{10,... | collective-permute-start | bytes 12296 | tf_op jit(solution)/shard_map/ppermute | solution.py:716
  18.5 0.8 %collective-permute-start.7 = (f32[8,128]{1,0:T(8,128)S(1)}, f32[8,128]{1,0:T(8,128)S(1)}, u32[]{:S(2)}, u32[]{:S(2)}) collective-permute-start(f32[8,128]{1,0:T(8,128)S(1)} %add.12), channel_id=1, source_target_pairs={{0,3},{1,2},{2,1},{3,0},{4,7},{5,6},{6,5},{7,4},{8,11},{9,10},{10,... | collective-permute-start | bytes 12296 | tf_op jit(solution)/shard_map/ppermute | solution.py:716
  19.3 0.0 collective-permute-done.9
  19.3 0.6 %collective-permute-done.8 = f32[8,128]{1,0:T(8,128)S(1)} collective-permute-done((f32[8,128]{1,0:T(8,128)S(1)}, f32[8,128]{1,0:T(8,128)S(1)}, u32[]{:S(2)}, u32[]{:S(2)}) %collective-permute-start.8) | collective-permute-done | bytes 4128 | tf_op jit(solution)/shard_map/ppermute | solution.py:716
  19.9 1.6 %collective-permute-done.7 = f32[8,128]{1,0:T(8,128)S(1)} collective-permute-done((f32[8,128]{1,0:T(8,128)S(1)}, f32[8,128]{1,0:T(8,128)S(1)}, u32[]{:S(2)}, u32[]{:S(2)}) %collective-permute-start.7) | collective-permute-done | bytes 4128 | tf_op jit(solution)/shard_map/ppermute | solution.py:716
  21.5 1.1 %collective-permute-start.10 = (f32[8,128]{1,0:T(8,128)S(1)}, f32[8,128]{1,0:T(8,128)S(1)}, u32[]{:S(2)}, u32[]{:S(2)}) collective-permute-start(f32[8,128]{1,0:T(8,128)S(1)} %add_add_fusion.part_ref), channel_id=1, source_target_pairs={{0,9},{1,8},{2,0},{3,1},{4,2},{5,3},{6,4},{7,5},{8,17},{9,16},{10,... | collective-permute-start | bytes 12296 | tf_op jit(solution)/shard_map/ppermute | solution.py:630
  22.6 0.9 %coefs.1 = (f32[2,2,4,16,128]{4,3,2,1,0:T(8,128)S(1)}, f32[48,128]{1,0:T(8,128)S(1)}) custom-call(f32[2,11,8,256]{3,2,1,0:T(8,128)S(1)} %get-tuple-element.32.oa_ref, f32[11,8,128]{2,1,0:T(8,128)S(1)} %get-tuple-element.33.stat_ref, f32[11,8,128]{2,1,0:T(8,128)S(1)} %get-tuple-element.34.block_ref), custom_call_target="tpu_custom_call" | custom-call | tf_op jit(solution)/shard_map/coefs/pallas_call | solution.py:721
  23.5 1.0 %collective-permute-done.10.next_ref = f32[8,128]{1,0:T(8,128)S(1)} collective-permute-done((f32[8,128]{1,0:T(8,128)S(1)}, f32[8,128]{1,0:T(8,128)S(1)}, u32[]{:S(2)}, u32[]{:S(2)}) %collective-permute-start.10) | collective-permute-done | bytes 4128 | tf_op jit(solution)/shard_map/ppermute | solution.py:630
  24.6 2.3 %collective-permute-start.12 = (f32[16,128]{1,0:T(8,128)S(1)}, f32[16,128]{1,0:T(8,128)S(1)}, u32[]{:S(2)}, u32[]{:S(2)}) collective-permute-start(f32[16,128]{1,0:T(8,128)S(1)} %join.1.own_ref), channel_id=1, source_target_pairs={{0,65},{1,64},{2,67},{3,66},{4,69},{5,68},{6,71},{7,70},{8,73},{9,... | collective-permute-start | bytes 24584 | tf_op jit(solution)/shard_map/ppermute | solution.py:630
  26.9 0.2 collective-permute-start.11
  27.0 1.2 %prepare.1 = (f32[16,2560]{1,0:T(8,128)S(1)}, f32[1,64]{1,0:T(1,128)}) custom-call(f32[16,128]{1,0:T(8,128)S(1)} %join.1.own_ref, f32[2,11,8,256]{3,2,1,0:T(8,128)S(1)} %get-tuple-element.32.oa_ref, f32[11,8,128]{2,1,0:T(8,128)S(1)} %get-tuple-element.33.stat_ref, f32[11,8,128]{2,1,0:T(8,128)S(1)} %get-tuple-element.34.block_ref), custom_call_target="tpu_custom_call" | custom-call | tf_op jit(solution)/shard_map/prepare/pallas_call | solution.py:739
  28.2 0.0 collective-permute-done.12.x0_ref
  28.2 0.0 collective-permute-done.11.x1_ref
  28.2 1.4 %product.1 = bf16[2400,128]{1,0:T(8,128)(2,1)} custom-call(f32[16,128]{1,0:T(8,128)S(1)} %collective-permute-done.11.x1_ref, f32[16,128]{1,0:T(8,128)S(1)} %collective-permute-done.12.x0_ref, f32[16,2560]{1,0:T(8,128)S(1)} %get-tuple-element.36.v_ref, f32[2,2,4,16,128]{4,3,2,1,0:T(8,128)S(1)} %get-tuple-element.37.coef_ref, ...), custom_call_target="tpu_custom_call" | custom-call | tf_op jit(solution)/shard_map/product/pallas_call | solution.py:750
  (4 shorter events, 0.0 us)
Async XLA Ops:
  2.4 3.9 %collective-permute-start.3 = (f32[24,128]{1,0:T(8,128)S(1)}, f32[24,128]{1,0:T(8,128)S(1)}, u32[]{:S(2)}, u32[]{:S(2)}) collective-permute-start(f32[24,128]{1,0:T(8,128)S(1)} %get-tuple-element.24), channel_id=1, source_target_pairs={{0,64},{1,65},{2,66},{3,67},{4,68},{5,69},{6,70},{7,71},{8,72},{9,... | collective-permute-start | bytes 36872 | tf_op jit(solution)/shard_map/ppermute | solution.py:630
  3.8 2.6 %collective-permute-start.2 = (f32[24,128]{1,0:T(8,128)S(1)}, f32[24,128]{1,0:T(8,128)S(1)}, u32[]{:S(2)}, u32[]{:S(2)}) collective-permute-start(f32[24,128]{1,0:T(8,128)S(1)} %get-tuple-element.24), channel_id=1, source_target_pairs={{0,1},{1,0},{2,3},{3,2},{4,5},{5,4},{6,7},{7,6},{8,9},{9,8},{10,11... | collective-permute-start | bytes 36872 | tf_op jit(solution)/shard_map/ppermute | solution.py:630
  4.7 3.4 %collective-permute-start.1 = (bf16[512,128]{1,0:T(8,128)(2,1)S(1)}, bf16[512,128]{1,0:T(8,128)(2,1)S(1)}, u32[]{:S(2)}, u32[]{:S(2)}) collective-permute-start(bf16[512,128]{1,0:T(8,128)(2,1)S(1)} %get-tuple-element.21), channel_id=1, source_target_pairs={{0,1},{1,0},{2,3},{3,2},{4,5},{5,4},{6,7},{7,6},{8,9},{9,8},{10,11... | collective-permute-start | bytes 393224 | tf_op jit(solution)/shard_map/ppermute | solution.py:630
  4.7 5.2 %collective-permute-start = (bf16[512,128]{1,0:T(8,128)(2,1)S(1)}, bf16[512,128]{1,0:T(8,128)(2,1)S(1)}, u32[]{:S(2)}, u32[]{:S(2)}) collective-permute-start(bf16[512,128]{1,0:T(8,128)(2,1)S(1)} %get-tuple-element.21), channel_id=1, source_target_pairs={{0,64},{1,2},{2,1},{3,4},{4,3},{5,6},{6,5},{7,8},{8,7},{9,10},{10,... | collective-permute-start | bytes 393224 | tf_op jit(solution)/shard_map/ppermute | solution.py:630
  6.4 1.8 %collective-permute-start.4 = (f32[24,128]{1,0:T(8,128)S(1)}, f32[24,128]{1,0:T(8,128)S(1)}, u32[]{:S(2)}, u32[]{:S(2)}) collective-permute-start(f32[24,128]{1,0:T(8,128)S(1)} %get-tuple-element.25.side_ref), channel_id=1, source_target_pairs={{0,1},{1,0},{2,3},{3,2},{4,5},{5,4},{6,7},{7,6},{8,9},{9,8},{10,11... | collective-permute-start | bytes 36872 | tf_op jit(solution)/shard_map/ppermute | solution.py:630
  7.3 3.4 %collective-permute-start.5 = (bf16[48,128]{1,0:T(8,128)(2,1)S(1)}, bf16[48,128]{1,0:T(8,128)(2,1)S(1)}, u32[]{:S(2)}, u32[]{:S(2)}) collective-permute-start(bf16[48,128]{1,0:T(8,128)(2,1)S(1)} %get-tuple-element.30), channel_id=1, source_target_pairs={{0,64},{1,2},{2,1},{3,4},{4,3},{5,6},{6,5},{7,8},{8,7},{9,10},{10,... | collective-permute-start | bytes 36872 | tf_op jit(solution)/shard_map/ppermute | solution.py:630
  10.9 2.8 %collective-permute-start.6 = (f32[8,128]{1,0:T(8,128)S(1)}, f32[8,128]{1,0:T(8,128)S(1)}, u32[]{:S(2)}, u32[]{:S(2)}) collective-permute-start(f32[8,128]{1,0:T(8,128)S(1)} %get-tuple-element.31), channel_id=1, source_target_pairs={{0,1},{1,0},{2,3},{3,2},{4,5},{5,4},{6,7},{7,6},{8,9},{9,8},{10,11... | collective-permute-start | bytes 12296 | tf_op jit(solution)/shard_map/ppermute | solution.py:714
  13.7 5.6 %collective-permute-start.9 = (f32[8,128]{1,0:T(8,128)S(1)}, f32[8,128]{1,0:T(8,128)S(1)}, u32[]{:S(2)}, u32[]{:S(2)}) collective-permute-start(f32[8,128]{1,0:T(8,128)S(1)} %add.12), channel_id=1, source_target_pairs={{0,5},{1,4},{2,7},{3,6},{4,1},{5,0},{6,3},{7,2},{8,13},{9,12},{10,... | collective-permute-start | bytes 12296 | tf_op jit(solution)/shard_map/ppermute | solution.py:716
  15.6 4.2 %collective-permute-start.8 = (f32[8,128]{1,0:T(8,128)S(1)}, f32[8,128]{1,0:T(8,128)S(1)}, u32[]{:S(2)}, u32[]{:S(2)}) collective-permute-start(f32[8,128]{1,0:T(8,128)S(1)} %add.12), channel_id=1, source_target_pairs={{0,7},{1,6},{2,5},{3,4},{4,3},{5,2},{6,1},{7,0},{8,15},{9,14},{10,... | collective-permute-start | bytes 12296 | tf_op jit(solution)/shard_map/ppermute | solution.py:716
  18.5 3.0 %collective-permute-start.7 = (f32[8,128]{1,0:T(8,128)S(1)}, f32[8,128]{1,0:T(8,128)S(1)}, u32[]{:S(2)}, u32[]{:S(2)}) collective-permute-start(f32[8,128]{1,0:T(8,128)S(1)} %add.12), channel_id=1, source_target_pairs={{0,3},{1,2},{2,1},{3,0},{4,7},{5,6},{6,5},{7,4},{8,11},{9,10},{10,... | collective-permute-start | bytes 12296 | tf_op jit(solution)/shard_map/ppermute | solution.py:716
  21.5 3.0 %collective-permute-start.10 = (f32[8,128]{1,0:T(8,128)S(1)}, f32[8,128]{1,0:T(8,128)S(1)}, u32[]{:S(2)}, u32[]{:S(2)}) collective-permute-start(f32[8,128]{1,0:T(8,128)S(1)} %add_add_fusion.part_ref), channel_id=1, source_target_pairs={{0,9},{1,8},{2,0},{3,1},{4,2},{5,3},{6,4},{7,5},{8,17},{9,16},{10,... | collective-permute-start | bytes 12296 | tf_op jit(solution)/shard_map/ppermute | solution.py:630
  24.6 3.6 %collective-permute-start.12 = (f32[16,128]{1,0:T(8,128)S(1)}, f32[16,128]{1,0:T(8,128)S(1)}, u32[]{:S(2)}, u32[]{:S(2)}) collective-permute-start(f32[16,128]{1,0:T(8,128)S(1)} %join.1.own_ref), channel_id=1, source_target_pairs={{0,65},{1,64},{2,67},{3,66},{4,69},{5,68},{6,71},{7,70},{8,73},{9,... | collective-permute-start | bytes 24584 | tf_op jit(solution)/shard_map/ppermute | solution.py:630
  26.9 1.3 %collective-permute-start.11 = (f32[16,128]{1,0:T(8,128)S(1)}, f32[16,128]{1,0:T(8,128)S(1)}, u32[]{:S(2)}, u32[]{:S(2)}) collective-permute-start(f32[16,128]{1,0:T(8,128)S(1)} %join.1.own_ref), channel_id=1, source_target_pairs={{0,1},{1,0},{2,3},{3,2},{4,5},{5,4},{6,7},{7,6},{8,9},{9,8},{10,11... | collective-permute-start | bytes 24584 | tf_op jit(solution)/shard_map/ppermute | solution.py:630

commit v8 on v7

--- a/solution.py
+++ b/solution.py
@@ -437,7 +437,7 @@
     miscs = tiles(z.levels)
     sub = iota((8, LANES), 0)
     lane = iota((8, LANES), 1)
-    on_left = lane % 16 >= 8
+    on_left = lane % 16 >= 4
     owner, index, weight = (stack(miscs, f)[:, LANES:] for f in (3, 1, 2))
     far_ref[0:8, :] = jnp.broadcast_to(owner[:, 0:1], (8, LANES))
     far_ref[8:16, :] = jnp.broadcast_to(owner[:, LANES - 1 :], (8, LANES))
@@ -481,7 +481,9 @@
             for c, v in enumerate(
                 (beside[2 + y][y], beyond[2 + y][y], beside[1 + y][y], beside[3 + y][y])
             ):
-                coef_ref[h, y, c] = v
+                coef_ref[h, y, c] = jnp.where(
+                    iota((NK, LANES), 1) % 16 < 4, v, lane_roll(v, LANES - 8)
+                )
 
 
 def prepare_kernel(z, own_ref, oa_ref, stat_ref, block_ref, v_ref, dep_ref):
@@ -520,7 +522,7 @@
     outer = outer_rows(z, swath)
     right = table_of(outer, right, far_ref[0:8, :])
     left = table_of(outer, left, far_ref[8:16, :])
-    on_left = iota((8, LANES), 1) % 16 >= 8
+    on_left = iota((8, LANES), 1) % 16 >= 4
 
     def back(n):
         index = far_ref[16 + 8 * n : 24 + 8 * n, :]
@@ -540,9 +542,8 @@
         for g in range(min(PER, z.levels - PER * h)):
             for y in range(2):
                 r = 2 * (PER * h + g) + y
-                first = lane_roll(seams[y], LANES - 16 * g - 12)
-                last = lane_roll(seams[y], 124 - 16 * g)
-                more = jnp.where(wide < 2, first, jnp.where(wide >= LANES - 2, last, 0.0))
+                more = lane_roll(seams[y], LANES - 16 * g - 4)
+                more = jnp.where((wide < 2) | (wide >= LANES - 2), more, 0.0)
                 at = slice(r * LANES, (r + 1) * LANES)
                 high, low = split(v_ref[:, at] + more)
                 v3[0:NK, at] = high

time: 30.2 us -> 30.2 us (level)
  no operation moved by 1% of the time
where the time goes in v8:
time: 30.2 us; the launch traced here: 29.6 us
  starting transfers between devices  16.8 us (56%)
  Pallas kernels  7.57 us (25%)
  waiting for transfers between devices  4.48 us (15%)
  between operations  0.69 us (2%)
    ppermute x9, starting transfers between devices, move(): return lax.ppermute(v, ALL, perm)  9.24 us
    ppermute x3, starting transfers between devices, per_device(): lax.ppermute(part, 'swath', [(i, i ^ 2 * k ^ 1) for i in range(nsw)])  5.63 us
    ppermute x3, waiting for transfers between devices, per_device(): lax.ppermute(part, 'swath', [(i, i ^ 2 * k ^ 1) for i in range(nsw)])  2.23 us
    ppermute x1, starting transfers between devices, per_device(): part = part + lax.ppermute(part, 'swath', [(i, i ^ 1) for i in range(nsw)])  1.97 us
    pallas_call x1, Pallas kernels, per_device(): pl.pallas_call(functools.partial(columns_kernel, z), out_shape=(shape(16,...  1.79 us
    pallas_call x1, Pallas kernels, per_device(): pl.pallas_call(functools.partial(project_kernel, z), out_shape=(shape(z.o...  1.76 us
    ppermute x9, waiting for transfers between devices, move(): return lax.ppermute(v, ALL, perm)  1.43 us
    pallas_call x1, Pallas kernels, per_device(): pl.pallas_call(functools.partial(product_kernel, z), out_shape=shape(*cel...  1.37 us
  transfers between devices with their start and end apart: 13, of which 5 were waited for; matrix products, arithmetic and copies ran while one was open for 0% of the time, Pallas kernels for 14%

profile of v8, /device:TPU:97, one launch (start us, length us, event | category | flops | bytes accessed | tf_op | source)
XLA Modules:
  0.0 29.6 jit_solution(16218868735878781020)
XLA Ops:
  0.6 1.8 %project.1 = (f32[320,128]{1,0:T(8,128)S(1)}, bf16[512,128]{1,0:T(8,128)(2,1)S(1)}, f32[24,128]{1,0:T(8,128)S(1)}, f32[96,128]{1,0:T(8,128)S(1)}, bf16[48,120]{1,0:T(8,128)(2,1)S(1)}) custom-call(bf16[2400,128]{1,0:T(8,128)(2,1)} %bitcast.5, bf16[4,120,120]{2,1,0:T(8,128)(2,1)} %prop_hbm.1, f32[10,2,128]{2,1,0:T(2,128)} %cx_hbm.1, f32[10,2,128]{2,1,0:T(2,128)} %cy_hbm.1, ...), custom_call_target="tpu_custom_call" | custom-call | tf_op jit(solution)/shard_map/project/pallas_call | solution.py:635
  2.4 1.4 %collective-permute-start.3 = (f32[24,128]{1,0:T(8,128)S(1)}, f32[24,128]{1,0:T(8,128)S(1)}, u32[]{:S(2)}, u32[]{:S(2)}) collective-permute-start(f32[24,128]{1,0:T(8,128)S(1)} %get-tuple-element.24), channel_id=1, source_target_pairs={{0,64},{1,65},{2,66},{3,67},{4,68},{5,69},{6,70},{7,71},{8,72},{9,... | collective-permute-start | bytes 36872 | tf_op jit(solution)/shard_map/ppermute | solution.py:631
  3.8 1.0 %collective-permute-start.2 = (f32[24,128]{1,0:T(8,128)S(1)}, f32[24,128]{1,0:T(8,128)S(1)}, u32[]{:S(2)}, u32[]{:S(2)}) collective-permute-start(f32[24,128]{1,0:T(8,128)S(1)} %get-tuple-element.24), channel_id=1, source_target_pairs={{0,1},{1,0},{2,3},{3,2},{4,5},{5,4},{6,7},{7,6},{8,9},{9,8},{10,11... | collective-permute-start | bytes 36872 | tf_op jit(solution)/shard_map/ppermute | solution.py:631
  4.7 0.0 collective-permute-start.1
  4.7 1.6 %collective-permute-start = (bf16[512,128]{1,0:T(8,128)(2,1)S(1)}, bf16[512,128]{1,0:T(8,128)(2,1)S(1)}, u32[]{:S(2)}, u32[]{:S(2)}) collective-permute-start(bf16[512,128]{1,0:T(8,128)(2,1)S(1)} %get-tuple-element.21), channel_id=1, source_target_pairs={{0,64},{1,2},{2,1},{3,4},{4,3},{5,6},{6,5},{7,8},{8,7},{9,10},{10,... | collective-permute-start | bytes 393224 | tf_op jit(solution)/shard_map/ppermute | solution.py:631
  6.3 0.0 collective-permute-done.3.x0_ref
  6.4 0.0 collective-permute-done.2.x1_ref
  6.4 0.9 %collective-permute-start.4 = (f32[24,128]{1,0:T(8,128)S(1)}, f32[24,128]{1,0:T(8,128)S(1)}, u32[]{:S(2)}, u32[]{:S(2)}) collective-permute-start(f32[24,128]{1,0:T(8,128)S(1)} %get-tuple-element.25.side_ref), channel_id=1, source_target_pairs={{0,1},{1,0},{2,3},{3,2},{4,5},{5,4},{6,7},{7,6},{8,9},{9,8},{10,11... | collective-permute-start | bytes 36872 | tf_op jit(solution)/shard_map/ppermute | solution.py:631
  7.3 0.9 %collective-permute-start.5 = (bf16[48,128]{1,0:T(8,128)(2,1)S(1)}, bf16[48,128]{1,0:T(8,128)(2,1)S(1)}, u32[]{:S(2)}, u32[]{:S(2)}) collective-permute-start(bf16[48,128]{1,0:T(8,128)(2,1)S(1)} %get-tuple-element.30), channel_id=1, source_target_pairs={{0,64},{1,2},{2,1},{3,4},{4,3},{5,6},{6,5},{7,8},{8,7},{9,10},{10,... | collective-permute-start | bytes 36872 | tf_op jit(solution)/shard_map/ppermute | solution.py:631
  8.2 0.0 collective-permute-done.4.far_ref
  8.2 0.0 collective-permute-done.1.a_ref
  8.2 1.8 %columns.1 = (f32[16,128]{1,0:T(8,128)S(1)}, f32[2,11,8,256]{3,2,1,0:T(8,128)S(1)}, f32[16,128]{1,0:T(8,128)S(1)}) custom-call(bf16[512,128]{1,0:T(8,128)(2,1)S(1)} %collective-permute-done.1.a_ref, f32[320,128]{1,0:T(8,128)S(1)} %get-tuple-element.22.g_ref, f32[96,128]{1,0:T(8,128)S(1)} %get-tuple-element.23.st_ref, ...), custom_call_target="tpu_custom_call" | custom-call | tf_op jit(solution)/shard_map/columns/pallas_call | solution.py:688
  10.0 0.0 collective-permute-done.b_ref
  10.0 0.3 beyond.1
  10.2 0.5 %collective-permute-done.5.far_ref = bf16[48,128]{1,0:T(8,128)(2,1)S(1)} collective-permute-done((bf16[48,128]{1,0:T(8,128)(2,1)S(1)}, bf16[48,128]{1,0:T(8,128)(2,1)S(1)}, u32[]{:S(2)}, u32[]{:S(2)}) %collective-permute-start.5) | collective-permute-done | bytes 12320 | tf_op jit(solution)/shard_map/ppermute | solution.py:631
  10.7 0.2 corner.1
  10.9 2.0 %collective-permute-start.6 = (f32[8,128]{1,0:T(8,128)S(1)}, f32[8,128]{1,0:T(8,128)S(1)}, u32[]{:S(2)}, u32[]{:S(2)}) collective-permute-start(f32[8,128]{1,0:T(8,128)S(1)} %get-tuple-element.31), channel_id=1, source_target_pairs={{0,1},{1,0},{2,3},{3,2},{4,5},{5,4},{6,7},{7,6},{8,9},{9,8},{10,11... | collective-permute-start | bytes 12296 | tf_op jit(solution)/shard_map/ppermute | solution.py:715
  12.8 0.8 %collective-permute-done.6 = f32[8,128]{1,0:T(8,128)S(1)} collective-permute-done((f32[8,128]{1,0:T(8,128)S(1)}, f32[8,128]{1,0:T(8,128)S(1)}, u32[]{:S(2)}, u32[]{:S(2)}) %collective-permute-start.6) | collective-permute-done | bytes 4128 | tf_op jit(solution)/shard_map/ppermute | solution.py:715
  13.7 2.0 %collective-permute-start.9 = (f32[8,128]{1,0:T(8,128)S(1)}, f32[8,128]{1,0:T(8,128)S(1)}, u32[]{:S(2)}, u32[]{:S(2)}) collective-permute-start(f32[8,128]{1,0:T(8,128)S(1)} %add.12), channel_id=1, source_target_pairs={{0,5},{1,4},{2,7},{3,6},{4,1},{5,0},{6,3},{7,2},{8,13},{9,12},{10,... | collective-permute-start | bytes 12296 | tf_op jit(solution)/shard_map/ppermute | solution.py:717
  15.6 2.9 %collective-permute-start.8 = (f32[8,128]{1,0:T(8,128)S(1)}, f32[8,128]{1,0:T(8,128)S(1)}, u32[]{:S(2)}, u32[]{:S(2)}) collective-permute-start(f32[8,128]{1,0:T(8,128)S(1)} %add.12), channel_id=1, source_target_pairs={{0,7},{1,6},{2,5},{3,4},{4,3},{5,2},{6,1},{7,0},{8,15},{9,14},{10,... | collective-permute-start | bytes 12296 | tf_op jit(solution)/shard_map/ppermute | solution.py:717
  18.5 0.8 %collective-permute-start.7 = (f32[8,128]{1,0:T(8,128)S(1)}, f32[8,128]{1,0:T(8,128)S(1)}, u32[]{:S(2)}, u32[]{:S(2)}) collective-permute-start(f32[8,128]{1,0:T(8,128)S(1)} %add.12), channel_id=1, source_target_pairs={{0,3},{1,2},{2,1},{3,0},{4,7},{5,6},{6,5},{7,4},{8,11},{9,10},{10,... | collective-permute-start | bytes 12296 | tf_op jit(solution)/shard_map/ppermute | solution.py:717
  19.3 0.0 collective-permute-done.9
  19.3 0.6 %collective-permute-done.8 = f32[8,128]{1,0:T(8,128)S(1)} collective-permute-done((f32[8,128]{1,0:T(8,128)S(1)}, f32[8,128]{1,0:T(8,128)S(1)}, u32[]{:S(2)}, u32[]{:S(2)}) %collective-permute-start.8) | collective-permute-done | bytes 4128 | tf_op jit(solution)/shard_map/ppermute | solution.py:717
  19.9 1.6 %collective-permute-done.7 = f32[8,128]{1,0:T(8,128)S(1)} collective-permute-done((f32[8,128]{1,0:T(8,128)S(1)}, f32[8,128]{1,0:T(8,128)S(1)}, u32[]{:S(2)}, u32[]{:S(2)}) %collective-permute-start.7) | collective-permute-done | bytes 4128 | tf_op jit(solution)/shard_map/ppermute | solution.py:717
  21.5 1.1 %collective-permute-start.10 = (f32[8,128]{1,0:T(8,128)S(1)}, f32[8,128]{1,0:T(8,128)S(1)}, u32[]{:S(2)}, u32[]{:S(2)}) collective-permute-start(f32[8,128]{1,0:T(8,128)S(1)} %add_add_fusion.part_ref), channel_id=1, source_target_pairs={{0,9},{1,8},{2,0},{3,1},{4,2},{5,3},{6,4},{7,5},{8,17},{9,16},{10,... | collective-permute-start | bytes 12296 | tf_op jit(solution)/shard_map/ppermute | solution.py:631
  22.6 1.0 %coefs.1 = (f32[2,2,4,16,128]{4,3,2,1,0:T(8,128)S(1)}, f32[48,128]{1,0:T(8,128)S(1)}) custom-call(f32[2,11,8,256]{3,2,1,0:T(8,128)S(1)} %get-tuple-element.32.oa_ref, f32[11,8,128]{2,1,0:T(8,128)S(1)} %get-tuple-element.33.stat_ref, f32[11,8,128]{2,1,0:T(8,128)S(1)} %get-tuple-element.34.block_ref), custom_call_target="tpu_custom_call" | custom-call | tf_op jit(solution)/shard_map/coefs/pallas_call | solution.py:722
  23.6 1.0 %collective-permute-done.10.next_ref = f32[8,128]{1,0:T(8,128)S(1)} collective-permute-done((f32[8,128]{1,0:T(8,128)S(1)}, f32[8,128]{1,0:T(8,128)S(1)}, u32[]{:S(2)}, u32[]{:S(2)}) %collective-permute-start.10) | collective-permute-done | bytes 4128 | tf_op jit(solution)/shard_map/ppermute | solution.py:631
  24.6 2.3 %collective-permute-start.12 = (f32[16,128]{1,0:T(8,128)S(1)}, f32[16,128]{1,0:T(8,128)S(1)}, u32[]{:S(2)}, u32[]{:S(2)}) collective-permute-start(f32[16,128]{1,0:T(8,128)S(1)} %join.1.own_ref), channel_id=1, source_target_pairs={{0,65},{1,64},{2,67},{3,66},{4,69},{5,68},{6,71},{7,70},{8,73},{9,... | collective-permute-start | bytes 24584 | tf_op jit(solution)/shard_map/ppermute | solution.py:631
  26.9 0.2 collective-permute-start.11
  27.0 1.2 %prepare.1 = (f32[16,2560]{1,0:T(8,128)S(1)}, f32[1,64]{1,0:T(1,128)}) custom-call(f32[16,128]{1,0:T(8,128)S(1)} %join.1.own_ref, f32[2,11,8,256]{3,2,1,0:T(8,128)S(1)} %get-tuple-element.32.oa_ref, f32[11,8,128]{2,1,0:T(8,128)S(1)} %get-tuple-element.33.stat_ref, f32[11,8,128]{2,1,0:T(8,128)S(1)} %get-tuple-element.34.block_ref), custom_call_target="tpu_custom_call" | custom-call | tf_op jit(solution)/shard_map/prepare/pallas_call | solution.py:740
  28.2 0.0 collective-permute-done.12.x0_ref
  28.2 0.0 collective-permute-done.11.x1_ref
  28.2 1.4 %product.1 = bf16[2400,128]{1,0:T(8,128)(2,1)} custom-call(f32[16,128]{1,0:T(8,128)S(1)} %collective-permute-done.11.x1_ref, f32[16,128]{1,0:T(8,128)S(1)} %collective-permute-done.12.x0_ref, f32[16,2560]{1,0:T(8,128)S(1)} %get-tuple-element.36.v_ref, f32[2,2,4,16,128]{4,3,2,1,0:T(8,128)S(1)} %get-tuple-element.37.coef_ref, ...), custom_call_target="tpu_custom_call" | custom-call | tf_op jit(solution)/shard_map/product/pallas_call | solution.py:751
  (4 shorter events, 0.0 us)
Async XLA Ops:
  2.4 3.9 %collective-permute-start.3 = (f32[24,128]{1,0:T(8,128)S(1)}, f32[24,128]{1,0:T(8,128)S(1)}, u32[]{:S(2)}, u32[]{:S(2)}) collective-permute-start(f32[24,128]{1,0:T(8,128)S(1)} %get-tuple-element.24), channel_id=1, source_target_pairs={{0,64},{1,65},{2,66},{3,67},{4,68},{5,69},{6,70},{7,71},{8,72},{9,... | collective-permute-start | bytes 36872 | tf_op jit(solution)/shard_map/ppermute | solution.py:631
  3.8 2.6 %collective-permute-start.2 = (f32[24,128]{1,0:T(8,128)S(1)}, f32[24,128]{1,0:T(8,128)S(1)}, u32[]{:S(2)}, u32[]{:S(2)}) collective-permute-start(f32[24,128]{1,0:T(8,128)S(1)} %get-tuple-element.24), channel_id=1, source_target_pairs={{0,1},{1,0},{2,3},{3,2},{4,5},{5,4},{6,7},{7,6},{8,9},{9,8},{10,11... | collective-permute-start | bytes 36872 | tf_op jit(solution)/shard_map/ppermute | solution.py:631
  4.7 3.4 %collective-permute-start.1 = (bf16[512,128]{1,0:T(8,128)(2,1)S(1)}, bf16[512,128]{1,0:T(8,128)(2,1)S(1)}, u32[]{:S(2)}, u32[]{:S(2)}) collective-permute-start(bf16[512,128]{1,0:T(8,128)(2,1)S(1)} %get-tuple-element.21), channel_id=1, source_target_pairs={{0,1},{1,0},{2,3},{3,2},{4,5},{5,4},{6,7},{7,6},{8,9},{9,8},{10,11... | collective-permute-start | bytes 393224 | tf_op jit(solution)/shard_map/ppermute | solution.py:631
  4.7 5.2 %collective-permute-start = (bf16[512,128]{1,0:T(8,128)(2,1)S(1)}, bf16[512,128]{1,0:T(8,128)(2,1)S(1)}, u32[]{:S(2)}, u32[]{:S(2)}) collective-permute-start(bf16[512,128]{1,0:T(8,128)(2,1)S(1)} %get-tuple-element.21), channel_id=1, source_target_pairs={{0,64},{1,2},{2,1},{3,4},{4,3},{5,6},{6,5},{7,8},{8,7},{9,10},{10,... | collective-permute-start | bytes 393224 | tf_op jit(solution)/shard_map/ppermute | solution.py:631
  6.4 1.8 %collective-permute-start.4 = (f32[24,128]{1,0:T(8,128)S(1)}, f32[24,128]{1,0:T(8,128)S(1)}, u32[]{:S(2)}, u32[]{:S(2)}) collective-permute-start(f32[24,128]{1,0:T(8,128)S(1)} %get-tuple-element.25.side_ref), channel_id=1, source_target_pairs={{0,1},{1,0},{2,3},{3,2},{4,5},{5,4},{6,7},{7,6},{8,9},{9,8},{10,11... | collective-permute-start | bytes 36872 | tf_op jit(solution)/shard_map/ppermute | solution.py:631
  7.3 3.4 %collective-permute-start.5 = (bf16[48,128]{1,0:T(8,128)(2,1)S(1)}, bf16[48,128]{1,0:T(8,128)(2,1)S(1)}, u32[]{:S(2)}, u32[]{:S(2)}) collective-permute-start(bf16[48,128]{1,0:T(8,128)(2,1)S(1)} %get-tuple-element.30), channel_id=1, source_target_pairs={{0,64},{1,2},{2,1},{3,4},{4,3},{5,6},{6,5},{7,8},{8,7},{9,10},{10,... | collective-permute-start | bytes 36872 | tf_op jit(solution)/shard_map/ppermute | solution.py:631
  10.9 2.8 %collective-permute-start.6 = (f32[8,128]{1,0:T(8,128)S(1)}, f32[8,128]{1,0:T(8,128)S(1)}, u32[]{:S(2)}, u32[]{:S(2)}) collective-permute-start(f32[8,128]{1,0:T(8,128)S(1)} %get-tuple-element.31), channel_id=1, source_target_pairs={{0,1},{1,0},{2,3},{3,2},{4,5},{5,4},{6,7},{7,6},{8,9},{9,8},{10,11... | collective-permute-start | bytes 12296 | tf_op jit(solution)/shard_map/ppermute | solution.py:715
  13.7 5.6 %collective-permute-start.9 = (f32[8,128]{1,0:T(8,128)S(1)}, f32[8,128]{1,0:T(8,128)S(1)}, u32[]{:S(2)}, u32[]{:S(2)}) collective-permute-start(f32[8,128]{1,0:T(8,128)S(1)} %add.12), channel_id=1, source_target_pairs={{0,5},{1,4},{2,7},{3,6},{4,1},{5,0},{6,3},{7,2},{8,13},{9,12},{10,... | collective-permute-start | bytes 12296 | tf_op jit(solution)/shard_map/ppermute | solution.py:717
  15.6 4.2 %collective-permute-start.8 = (f32[8,128]{1,0:T(8,128)S(1)}, f32[8,128]{1,0:T(8,128)S(1)}, u32[]{:S(2)}, u32[]{:S(2)}) collective-permute-start(f32[8,128]{1,0:T(8,128)S(1)} %add.12), channel_id=1, source_target_pairs={{0,7},{1,6},{2,5},{3,4},{4,3},{5,2},{6,1},{7,0},{8,15},{9,14},{10,... | collective-permute-start | bytes 12296 | tf_op jit(solution)/shard_map/ppermute | solution.py:717
  18.5 3.0 %collective-permute-start.7 = (f32[8,128]{1,0:T(8,128)S(1)}, f32[8,128]{1,0:T(8,128)S(1)}, u32[]{:S(2)}, u32[]{:S(2)}) collective-permute-start(f32[8,128]{1,0:T(8,128)S(1)} %add.12), channel_id=1, source_target_pairs={{0,3},{1,2},{2,1},{3,0},{4,7},{5,6},{6,5},{7,4},{8,11},{9,10},{10,... | collective-permute-start | bytes 12296 | tf_op jit(solution)/shard_map/ppermute | solution.py:717
  21.5 3.0 %collective-permute-start.10 = (f32[8,128]{1,0:T(8,128)S(1)}, f32[8,128]{1,0:T(8,128)S(1)}, u32[]{:S(2)}, u32[]{:S(2)}) collective-permute-start(f32[8,128]{1,0:T(8,128)S(1)} %add_add_fusion.part_ref), channel_id=1, source_target_pairs={{0,9},{1,8},{2,0},{3,1},{4,2},{5,3},{6,4},{7,5},{8,17},{9,16},{10,... | collective-permute-start | bytes 12296 | tf_op jit(solution)/shard_map/ppermute | solution.py:631
  24.6 3.6 %collective-permute-start.12 = (f32[16,128]{1,0:T(8,128)S(1)}, f32[16,128]{1,0:T(8,128)S(1)}, u32[]{:S(2)}, u32[]{:S(2)}) collective-permute-start(f32[16,128]{1,0:T(8,128)S(1)} %join.1.own_ref), channel_id=1, source_target_pairs={{0,65},{1,64},{2,67},{3,66},{4,69},{5,68},{6,71},{7,70},{8,73},{9,... | collective-permute-start | bytes 24584 | tf_op jit(solution)/shard_map/ppermute | solution.py:631
  26.9 1.3 %collective-permute-start.11 = (f32[16,128]{1,0:T(8,128)S(1)}, f32[16,128]{1,0:T(8,128)S(1)}, u32[]{:S(2)}, u32[]{:S(2)}) collective-permute-start(f32[16,128]{1,0:T(8,128)S(1)} %join.1.own_ref), channel_id=1, source_target_pairs={{0,1},{1,0},{2,3},{3,2},{4,5},{5,4},{6,7},{7,6},{8,9},{9,8},{10,11... | collective-permute-start | bytes 24584 | tf_op jit(solution)/shard_map/ppermute | solution.py:631
